TPU v7x, 32 devices: a whole 2x2x4 slice. The times are simulated.
32 devices in a mesh: dp: 4 (over x, core), seq: 8 (over z, y).
Axes of the slice: x: 2, y: 2, z: 4, core: 2. Of those that a mesh axis runs over, the one named last changes fastest.
Arguments:
- inputs: bfloat16 [8, 4096, 512], P('dp', 'seq'), may hold values from -6 to 6
- segment_ids: int32 [8, 4096], P('dp', 'seq'), may hold values from 0 to 4095, as said below
- real_block: int32 [8, 128], P('dp', 'seq'), may hold values from 0 to 1, as said below
- gain_attn: bfloat16 [512], replicated, may hold values from 0.25 to 1.75
- w_query: bfloat16 [512, 512], replicated, may hold values from -0.25 to 0.25
- w_key: bfloat16 [512, 512], replicated, may hold values from -0.25 to 0.25
- w_value: bfloat16 [512, 512], replicated, may hold values from -0.25 to 0.25
- w_output: bfloat16 [512, 512], replicated, may hold values from -2 to 2
- w_sort: bfloat16 [512, 512], replicated, may hold values from -0.25 to 0.25
- gain_ffn: bfloat16 [512], replicated, may hold values from 0.25 to 1.75
- w_in: bfloat16 [512, 2048], replicated, may hold values from -0.25 to 0.25
- w_out: bfloat16 [2048, 512], replicated, may hold values from -0.125 to 0.125
- cotangent: bfloat16 [8, 4096, 512], P('dp', 'seq'), may hold values from -6 to 6
Outputs:
- output: bfloat16 [8, 4096, 512], P('dp', 'seq')
- input_grad: bfloat16 [8, 4096, 512], P('dp', 'seq')
- penalty: float32 [], replicated
- grad_gain_attn: float32 [512], replicated
- grad_query: float32 [512, 512], replicated
- grad_key: float32 [512, 512], replicated
- grad_value: float32 [512, 512], replicated
- grad_output: float32 [512, 512], replicated
- grad_sort: float32 [512, 512], replicated
- slope_feedforward_scaler: float32 [512], replicated
- grad_in: float32 [512, 2048], replicated
- grad_out: float32 [2048, 512], replicated
Inputs may be any that keep to these rules, and one draw needn't show every extreme that they name: `segment_ids`: Non-decreasing along each sequence; the ids of the pack that begins at position p * 256 lie in p * 256 to p * 256 + 255, so ids of different packs differ; the last position of every sequence holds the top id of its pack. `real_block`: the last block of every sequence is 1.
All inputs are finite; a program needn't handle non-finite values.
Results may differ from a plain program's by a relative error of at most 0.035.
Values may be sent and summed in bfloat16 or wider, within the bound.
No kernel may reach another device: no remote copies, remote signals or barrier semaphores. Data moves between devices by JAX's collectives and lax.ppermute only.
A program may use at most 384 MiB of HBM per device.

v0:
```python
import math

import jax
import jax.numpy as jnp
from jax import lax
from jax.experimental import pallas as pl
from jax.experimental.pallas import tpu as pltpu
from jax.sharding import PartitionSpec as P

HEADS = 8
BLOCK = 32
ITERS = 8
GROUP = 128

EPS = 1e-06
NEG = -1000000000.0
SORT_GAIN = 2.5
F32 = jnp.float32
BF16 = jnp.bfloat16
VMEM_BYTES = 56 * 2**20
COST = 3.0


def bits(size):
    return [1 << k for k in range(size.bit_length() - 1)]


def swap(array, axis, bit):
    return lax.ppermute(array, axis, [(i, i ^ bit) for i in range(lax.axis_size(axis))])


def send(array, dp_bits, seq_bits):
    seq = lax.axis_size("seq")
    mask = dp_bits * seq + seq_bits
    count = lax.axis_size("dp") * seq
    return lax.ppermute(array, ("dp", "seq"), [(i, i ^ mask) for i in range(count)])


CORE = (1, 0)
PLANE = ((0, 1), (2, 0), (2, 1))
LINE = ((0, 4), (0, 2), (0, 6))


def add_kernel(count, *refs):
    outs = refs[count:]
    each = outs[0].shape[0]
    for n, out_ref in enumerate(outs):
        part = pl.ds(n * each, each)
        total = refs[0][part].astype(F32)
        for ref in refs[1:count]:
            total = total + ref[part].astype(F32)
        out_ref[...] = total.astype(BF16)


def add_split(arrays, pieces, after=()):
    shape = arrays[0].shape
    out = like((shape[0] // pieces,) + shape[1:], BF16)
    kernel = lambda *refs: add_kernel(len(arrays), *refs)
    return list(call(kernel, [out] * pieces, arrays, after=after))


def sum_stages(keep, give):
    got = send(give, *CORE)
    own = add_split([keep, got], 4)
    yield own
    got = [send(g, *to) for g, to in zip(own[1:], PLANE)]
    own = add_split([own[0]] + got, 4)
    yield own
    got = [send(g, *to) for g, to in zip(own[1:], LINE)]
    own = add_split([own[0]] + got, 1)
    for bit in bits(lax.axis_size("seq"))[3:]:
        own = add_split([own[0], send(own[0], 0, bit)], 1)
    yield own
    got = [send(own[0], *to) for to in LINE]
    quarter = jnp.concatenate(own + got, axis=0)
    yield [quarter]
    got = [send(quarter, *to) for to in PLANE]
    quarters = [quarter] + got
    yield quarters
    yield quarters + [send(q, *CORE) for q in quarters]


def exchange(chunks):
    return lax.all_to_all(chunks, "seq", 0, 0, tiled=True)


def add(left, right):
    return (left.astype(F32) + right.astype(F32)).astype(BF16)


def sum_seq(part):
    for bit in bits(lax.axis_size("seq")):
        part = add(part, swap(part, "seq", bit))
    return part


def dot(left, right, left_dim=1, right_dim=0):
    return lax.dot_general(
        left, right, (((left_dim,), (right_dim,)), ((), ())), preferred_element_type=F32
    )


def whole(array):
    return pl.BlockSpec(array.shape, lambda *_: (0,) * array.ndim)


def nth(array, index):
    return pl.BlockSpec((1,) + array.shape[1:], lambda *_: (index,) + (0,) * (array.ndim - 1))


def call(
    kernel, outs, args, specs=None, scratch=(), flops=0, out_specs=None, grid=(1,), after=(), **more
):
    specs = specs or [whole(a) for a in args]
    moved = sum(math.prod(o.shape) * o.dtype.itemsize for o in outs)
    moved += sum(math.prod(a.shape) * a.dtype.itemsize for a in args)
    count, skip = len(args), len(after)
    return pl.pallas_call(
        lambda *refs: kernel(*refs[:count], *refs[count + skip :]),
        out_shape=outs,
        grid=grid,
        in_specs=list(specs) + [pl.BlockSpec(memory_space=pl.ANY)] * skip,
        out_specs=out_specs or [whole(o) for o in outs],
        scratch_shapes=list(scratch),
        compiler_params=pltpu.CompilerParams(vmem_limit_bytes=VMEM_BYTES),
        cost_estimate=pl.CostEstimate(
            flops=int(flops * COST), bytes_accessed=int(moved * COST), transcendentals=0
        ),
        **more,
    )(*args, *after)


SCALAR = pl.BlockSpec(memory_space=pltpu.SMEM)


def like(shape, dtype):
    return jax.ShapeDtypeStruct(shape, dtype)


def lay(buffer, value):
    for c in range(buffer.shape[0]):
        buffer[c] = value[:, c * 128 : (c + 1) * 128]


def lift(buffer):
    return jnp.concatenate([buffer[c] for c in range(buffer.shape[0])], axis=1)


def pick(buffer, t, count):
    return jnp.concatenate(
        [buffer[c, pl.ds(t, count, stride=BLOCK), :] for c in range(buffer.shape[0])], axis=1
    )


def strew(buffer, t, rows):
    for c in range(buffer.shape[0]):
        buffer[c, pl.ds(t, rows.shape[0], stride=BLOCK), :] = rows[:, c * 128 : (c + 1) * 128]


def chunk_shape(parts, blocks, width):
    row_parts = min(parts, BLOCK)
    return (parts, BLOCK // row_parts, blocks, width * row_parts // parts)


def chunk_places(shape, t):
    per = BLOCK // shape[1]
    cols = shape[0] // per
    return [(t // shape[1]) * cols + f for f in range(cols)], t % shape[1]


def store_row(ref, t, rows, shape=None):
    parts, place = chunk_places(shape or ref.shape, t)
    for f, part in enumerate(parts):
        ref[part, place] = rows[:, f * ref.shape[3] : (f + 1) * ref.shape[3]]


def load_row(ref, t):
    parts, place = chunk_places(ref.shape, t)
    return jnp.concatenate([ref[part, place] for part in parts], axis=1)


def row_buffer(span, width):
    return pltpu.VMEM((width // 128, span, 128), F32)


def enter_kernel(x_ref, gain_ref, flag_ref, hidden_ref, *refs):
    rows_refs, buffer = refs[:-1], refs[-1]
    seqs = len(rows_refs)
    parts, _, blocks, cols = rows_refs[0].shape
    width = hidden_ref.shape[2]
    each = width // cols
    shape = chunk_shape(parts, blocks, width)
    for s in range(seqs):
        x = x_ref[s].astype(F32)
        scale = lax.rsqrt(jnp.mean(x * x, axis=-1, keepdims=True) + EPS)
        hidden = (x * scale * gain_ref[...]).astype(BF16)
        hidden_ref[s] = hidden
        lay(buffer, hidden.astype(F32))
        total = None
        for t in range(BLOCK):
            rows = pick(buffer, t, blocks)
            store_row(rows_refs[s], t, rows.astype(BF16), shape)
            total = rows if total is None else total + rows
        low = (total * (1.0 / BLOCK)).astype(BF16)
        for part in range(parts):
            for f in range(each):
                rows_refs[0][part, shape[1] + s * each + f] = low[:, f * cols : (f + 1) * cols]
    for part in range(parts):
        rows_refs[0][part, shape[1] + seqs * each] = flag_ref[...]


def enter(inputs, gain, real, parts):
    seqs, span, width = inputs.shape
    blocks = span // BLOCK
    p, r, n, w = chunk_shape(parts, blocks, width)
    flags = jnp.repeat(real.astype(BF16).T, w // seqs, axis=1)
    more = seqs * (width // w) + 1
    return call(
        enter_kernel,
        [like(inputs.shape, BF16)]
        + [like((p, r + (more if s == 0 else 0), n, w), BF16) for s in range(seqs)],
        [inputs, gain, flags],
        scratch=[row_buffer(span, width)],
    )


def told_of(first, seqs, width):
    parts, _, blocks, cols = first.shape
    shape = chunk_shape(parts, blocks, width)
    each = width // cols
    told = first[:, shape[1] :]
    told = told.transpose(1, 0, 2, 3).reshape(told.shape[1], parts * blocks, cols)
    flags = told[-1][:, :: cols // seqs].T
    told = told[:-1].reshape(seqs, each, parts * blocks, cols).transpose(0, 2, 1, 3)
    return told.reshape(seqs, parts * blocks, width), flags


def told_summary(first_ref, s):
    parts, rows, blocks, width = first_ref.shape
    row = chunk_shape(parts, blocks, width)[1] + s
    return first_ref[:, row].reshape(parts * blocks, width)


def told_flags(first_ref, seqs, s):
    parts, rows, blocks, width = first_ref.shape
    flags = first_ref[:, rows - 1, :, s * (width // seqs) : s * (width // seqs) + 128]
    return flags.reshape(parts * blocks, 128).astype(F32)


def plan_kernel(sort_scale, told_ref, w_ref, proj_ref, steps_ref, plan_ref, low_ref, entropy_ref, count_ref):
    seqs = plan_ref.shape[0]
    plans, reals = [], []
    entropy = jnp.zeros((), F32)
    for s in range(seqs):
        summary = told_summary(told_ref, s)
        flags = told_flags(told_ref, seqs, s)
        real = flags.T > 0.5
        proj = dot(summary, w_ref[...]).astype(BF16)
        proj_ref[s] = proj
        plans.append(jnp.where(real, sort_scale * dot(proj, summary, 1, 1), NEG))
        reals.append(real)
    for step in range(2 * ITERS):
        axis = 1 - step % 2
        for s in range(seqs):
            peak = jnp.max(plans[s], axis=axis, keepdims=True)
            share = jnp.exp(plans[s] - peak)
            total = jnp.sum(share, axis=axis, keepdims=True)
            fall = peak + jnp.log(total)
            share = share * (1.0 / total)
            if axis == 0:
                fall = jnp.where(reals[s][:1], fall, 0.0)
                share = jnp.where(reals[s], share, 0.0)
            plans[s] = plans[s] - fall
            steps_ref[step, s] = share
    for s in range(seqs):
        flags = told_flags(told_ref, seqs, s)[:, :1]
        prob = jnp.exp(plans[s])
        plan_ref[s] = plans[s]
        low_ref[s] = prob.astype(BF16)
        entropy = entropy + jnp.sum(jnp.where(flags > 0.5, prob * plans[s], 0.0))
    entropy_ref[...] = jnp.full(entropy_ref.shape, entropy, F32)
    blocks = [jnp.sum(told_flags(told_ref, seqs, s), axis=0, keepdims=True) for s in range(seqs)]
    count_ref[...] = jnp.broadcast_to(sum(blocks), count_ref.shape)


def plan_back_kernel(
    sort_scale,
    count_ref,
    place_ref,
    heard_ref,
    told_ref,
    w_ref,
    proj_ref,
    steps_ref,
    plan_ref,
    d_summary_ref,
    grad_ref,
    buffer,
):
    place = place_ref[0, 0]
    seqs = plan_ref.shape[0]
    blocks = told_ref.shape[2]
    part = 1.0 / count_ref[:1]
    grads = []
    for s in range(seqs):
        flags = told_flags(told_ref, seqs, s)[:, :1]
        plan = plan_ref[s]
        prob = jnp.exp(plan)
        d_prob = heard_ref[s].astype(F32)
        grads.append(prob * d_prob - jnp.where(flags > 0.5, prob * plan + prob, 0.0) * part)
    for step in reversed(range(2 * ITERS)):
        for s in range(seqs):
            total = jnp.sum(grads[s], axis=1 - step % 2, keepdims=True)
            grads[s] = grads[s] - steps_ref[step, s] * total
    grad_sort = None
    for s in range(seqs):
        summary = told_summary(told_ref, s)
        flags = told_flags(told_ref, seqs, s)
        real = flags.T > 0.5
        d_logits = jnp.where(real, grads[s], 0.0)
        low = d_logits.astype(BF16)
        d_proj = (sort_scale * dot(low, summary)).astype(BF16)
        turned = low.astype(F32).T.astype(BF16)
        buffer[...] = sort_scale * dot(turned, proj_ref[s]) + dot(d_proj, w_ref[...], 1, 1)
        first = pl.multiple_of(place * blocks, blocks)
        d_summary_ref[s] = buffer[pl.ds(first, blocks), :]
        here = dot(summary, d_proj, 0, 0)
        grad_sort = here if grad_sort is None else grad_sort + here
    grad_ref[...] = grad_sort.astype(grad_ref.dtype)


def spread_row(ref, t):
    parts, rows, blocks, width = ref.shape
    return ref[:, t].reshape(parts * blocks, width)


def mix_kernel(low_ref, spread_ref, mixed_ref):
    parts, rows, blocks, width = mixed_ref.shape
    for t in range(rows):
        mixed = dot(low_ref[0], spread_row(spread_ref, t)).astype(BF16)
        mixed_ref[:, t] = mixed.reshape(parts, blocks, width)


def mix(low, spread, index, width):
    shape = chunk_shape(spread.shape[0], spread.shape[2], width)
    return call(mix_kernel, [like(shape, BF16)], [low, spread], [nth(low, index), whole(spread)])[0]


def unmix_kernel(low_ref, *refs):
    seqs = low_ref.shape[0]
    spread_refs, d_mixed_refs = refs[:seqs], refs[seqs : 2 * seqs]
    d_spread_ref, d_prob_ref = refs[2 * seqs :]
    parts, rows, blocks, width = d_mixed_refs[0].shape
    for s in range(seqs):
        turned = low_ref[s].astype(F32).T.astype(BF16)
        d_prob = None
        for t in range(rows):
            grad = spread_row(d_mixed_refs[s], t)
            here = dot(grad, spread_row(spread_refs[s], t), 1, 1)
            d_prob = here if d_prob is None else d_prob + here
            back = dot(turned, grad).astype(BF16)
            d_spread_ref[:, s * rows + t] = back.reshape(parts, blocks, width)
        d_prob_ref[s] = d_prob.astype(BF16)


def unmix(low, spread, d_mixed, after=()):
    p, r, n, w = d_mixed[0].shape
    seqs = low.shape[0]
    return call(
        unmix_kernel,
        [like((p, seqs * r, n, w), BF16), like(low.shape, BF16)],
        [low, *spread, *d_mixed],
        after=after,
    )


def block_masks():
    lane = lax.broadcasted_iota(jnp.int32, (BLOCK, 2 * GROUP), 1)
    owner = (lane % GROUP) // BLOCK
    return [owner == b for b in range(GROUP // BLOCK)]


def narrow(full, masks, start):
    out = full[start : start + BLOCK]
    for b in range(1, len(masks)):
        out = jnp.where(masks[b], full[start + b * BLOCK : start + (b + 1) * BLOCK], out)
    return out


def widen(first, second, masks):
    zero = jnp.zeros_like(first)
    return jnp.concatenate(
        [jnp.where(m, first, zero) for m in masks] + [jnp.where(m, second, zero) for m in masks],
        axis=0,
    ).astype(BF16)


def two_heads_lanes(rows):
    lane = lax.broadcasted_iota(jnp.int32, rows.shape, 1)
    low = lane < rows.shape[1] // 2
    zero = jnp.zeros_like(rows)
    return jnp.concatenate([jnp.where(low, rows, zero), jnp.where(low, zero, rows)], axis=0)


def two_heads_rows(columns):
    row = lax.broadcasted_iota(jnp.int32, columns.shape, 0)
    low = row < columns.shape[0] // 2
    zero = jnp.zeros_like(columns)
    return jnp.concatenate([jnp.where(low, columns, zero), jnp.where(low, zero, columns)], axis=1)


def own_heads(full):
    half = full.shape[1] // 2
    row = lax.broadcasted_iota(jnp.int32, (full.shape[0], half), 0)
    return jnp.where(row < full.shape[0] // 2, full[:, :half], full[:, half:])


def turn(array):
    return array.astype(F32).T.astype(BF16)


def project_kernel(hidden_ref, wq_ref, wk_ref, wv_ref, q_ref, k_ref, v_ref, qt_ref, kt_ref, vt_ref):
    hidden = hidden_ref[0]
    for w_ref, flat_ref, turned_ref in (
        (wq_ref, q_ref, qt_ref),
        (wk_ref, k_ref, kt_ref),
        (wv_ref, v_ref, vt_ref),
    ):
        full = dot(hidden, w_ref[...])
        flat_ref[0] = full.astype(BF16)
        turned_ref[0] = full.T.astype(BF16)


def project(hidden, wq, wk, wv):
    seqs, span, width = hidden.shape
    flat = pl.BlockSpec((1, span, width), lambda s: (s, 0, 0))
    turned = pl.BlockSpec((1, width, span), lambda s: (s, 0, 0))
    return call(
        project_kernel,
        [like((seqs, span, width), BF16)] * 3 + [like((seqs, width, span), BF16)] * 3,
        [hidden, wq, wk, wv],
        [flat] + [whole(wq)] * 3,
        flops=6 * seqs * span * width * width,
        grid=(seqs,),
        out_specs=[flat] * 3 + [turned] * 3,
    )


def attend_kernel(
    att_scale,
    rows_ref,
    allowed_ref,
    wk_ref,
    wv_ref,
    k_ref,
    qt_ref,
    vt_ref,
    att_ref,
    mixed_ref,
    vs_ref,
    kst_ref,
    weights_ref,
    buffer,
    ks,
    vst,
):
    span, width = mixed_ref.shape
    for t in range(BLOCK):
        strew(buffer, t, load_row(rows_ref, t).astype(F32))
    mixed_ref[...] = lift(buffer).astype(BF16)
    mixed = mixed_ref[...]
    full = dot(mixed, wk_ref[...])
    ks[...] = full.astype(BF16)
    kst_ref[...] = full.T.astype(BF16)
    full = dot(mixed, wv_ref[...])
    vs_ref[...] = full.astype(BF16)
    vst[...] = full.T.astype(BF16)
    masks = block_masks()
    pairs = HEADS // 2

    def group(g, carry):
        rows = pl.ds(pl.multiple_of(g * GROUP, GROUP), GROUP)
        allowed = allowed_ref[0, :, rows]
        allowed = jnp.concatenate([allowed, allowed], axis=1) > 0.5
        for p in range(pairs):
            lanes = pl.ds(p * GROUP, GROUP)
            keys = jnp.concatenate([k_ref[0, rows, lanes], ks[rows, lanes]], axis=0)
            scores = dot(keys, two_heads_rows(qt_ref[0, lanes, rows]))
            near = jnp.where(allowed, narrow(scores, masks, 0) * att_scale, NEG)
            far = narrow(scores, masks, GROUP) * att_scale
            peak = jnp.maximum(
                jnp.max(near, axis=0, keepdims=True), jnp.max(far, axis=0, keepdims=True)
            )
            near = jnp.exp(near - peak)
            far = jnp.exp(far - peak)
            total = jnp.sum(near, axis=0, keepdims=True) + jnp.sum(far, axis=0, keepdims=True)
            part = 1.0 / total
            near = near * part
            far = far * part
            weights_ref[g * pairs + p, :BLOCK] = near
            weights_ref[g * pairs + p, BLOCK:] = far
            values = jnp.concatenate([vt_ref[0, lanes, rows], vst[lanes, rows]], axis=1)
            out = own_heads(dot(values, widen(near, far, masks)))
            att_ref[rows, lanes] = out.T.astype(BF16)
        return carry

    lax.fori_loop(0, span // GROUP, group, 0)


def attend(rows, allowed, wk, wv, k, qt, vt, index):
    seqs, span, width = k.shape
    units = span // GROUP * (HEADS // 2)
    flat = like((span, width), BF16)
    args = [rows, allowed, wk, wv, k, qt, vt]
    return call(
        lambda *refs: attend_kernel(1.0 / math.sqrt(width // HEADS), *refs),
        [flat] * 3 + [like((width, span), BF16), like((units, 2 * BLOCK, 2 * GROUP), F32)],
        args,
        [whole(rows), nth(allowed, index), whole(wk), whole(wv)]
        + [nth(a, index) for a in (k, qt, vt)],
        [row_buffer(span, width), pltpu.VMEM((span, width), BF16), pltpu.VMEM((width, span), BF16)],
        flops=8 * span * width * width,
    )


def attend_back_kernel(
    att_scale,
    d_att_ref,
    q_ref,
    v_ref,
    kt_ref,
    vs_ref,
    kst_ref,
    weights_ref,
    wk_ref,
    wv_ref,
    d_rows_ref,
    dq,
    dk,
    dv,
    dks,
    dvs,
    buffer,
    datt_t,
):
    span, width = vs_ref.shape
    datt_t[...] = turn(d_att_ref[0])
    masks = block_masks()
    pairs = HEADS // 2

    def group(g, carry):
        rows = pl.ds(pl.multiple_of(g * GROUP, GROUP), GROUP)
        for p in range(pairs):
            lanes = pl.ds(p * GROUP, GROUP)
            values = jnp.concatenate([v_ref[0, rows, lanes], vs_ref[rows, lanes]], axis=0)
            d_weights = dot(values, two_heads_rows(datt_t[lanes, rows]))
            near = weights_ref[g * pairs + p, :BLOCK]
            far = weights_ref[g * pairs + p, BLOCK:]
            d_near = near * narrow(d_weights, masks, 0)
            d_far = far * narrow(d_weights, masks, GROUP)
            total = jnp.sum(d_near, axis=0, keepdims=True) + jnp.sum(d_far, axis=0, keepdims=True)
            d_near = d_near - near * total
            d_far = d_far - far * total
            d_scores = widen(d_near, d_far, masks)
            keys = jnp.concatenate([kt_ref[0, lanes, rows], kst_ref[lanes, rows]], axis=1)
            dq[rows, lanes] = (own_heads(dot(keys, d_scores)).T * att_scale).astype(BF16)
            d_keys = (dot(d_scores, two_heads_lanes(q_ref[0, rows, lanes])) * att_scale).astype(BF16)
            dk[rows, lanes] = d_keys[:GROUP]
            dks[rows, lanes] = d_keys[GROUP:]
            d_values = dot(
                widen(near, far, masks), two_heads_lanes(d_att_ref[0, rows, lanes])
            ).astype(BF16)
            dv[rows, lanes] = d_values[:GROUP]
            dvs[rows, lanes] = d_values[GROUP:]
        return carry

    lax.fori_loop(0, span // GROUP, group, 0)
    lay(buffer, dot(dks[...], wk_ref[...], 1, 1) + dot(dvs[...], wv_ref[...], 1, 1))
    for t in range(BLOCK):
        store_row(d_rows_ref, t, pick(buffer, t, d_rows_ref.shape[2]).astype(BF16))


def attend_back(d_att, q, v, kt, kept, wk, wv, shape, index, after=()):
    seqs, span, width = q.shape
    args = [d_att, q, v, kt, *kept, wk, wv]
    flat = like((span, width), BF16)
    return call(
        lambda *refs: attend_back_kernel(1.0 / math.sqrt(width // HEADS), *refs),
        [like(shape, BF16)] + [flat] * 5,
        args,
        [nth(a, index) for a in args[:4]]
        + [whole(a) for a in args[4:]],
        [row_buffer(span, width), pltpu.VMEM((width, span), BF16)],
        flops=12 * span * width * width,
        after=after,
    )


def late_kernel(split_ref, hidden_ref, gwo_ref, *refs):
    keep_ref, give_ref, buffer = refs[-3:]
    seqs, span, width = hidden_ref.shape
    core, place = split_ref[0], split_ref[1]
    per = len(refs[:-3]) // seqs
    totals = [None, None, None]
    for s in range(seqs):
        mixed_ref, dq, dk, dv, dks, dvs = refs[s * per : (s + 1) * per]
        hidden_t = turn(hidden_ref[s])
        mixed_t = turn(mixed_ref[...])
        here = (
            dot(hidden_t, dq[...]),
            dot(hidden_t, dk[...]) + dot(mixed_t, dks[...]),
            dot(hidden_t, dv[...]) + dot(mixed_t, dvs[...]),
        )
        totals = [h if t is None else t + h for t, h in zip(totals, here)]
    for n in range(3):
        buffer[n] = totals[n]
    buffer[3] = gwo_ref[...].astype(F32)
    blocks, rows = keep_ref.shape[0], keep_ref.shape[1] // 4
    for side, ref in ((core, keep_ref), (1 - core, give_ref)):
        for j in range(blocks):
            part = pl.ds(pl.multiple_of((side * blocks + j) * rows, rows), rows)
            at = j ^ (place % blocks)
            for n in range(4):
                ref[at, n * rows : (n + 1) * rows] = buffer[n, part].astype(BF16)


def late(split, hidden, gwo, parts, after=()):
    seqs, span, width = hidden.shape
    args = [split, hidden, gwo, *[a for part in parts for a in part]]
    shape = like((16, 4 * width // 32, width), BF16)
    return call(
        late_kernel,
        [shape, shape],
        args,
        [SCALAR] + [whole(a) for a in args[1:]],
        [pltpu.VMEM((4, width, width), F32)],
        flops=10 * seqs * span * width * width,
        after=after,
    )


def end_blocks(split_ref, refs):
    each = refs[0].shape[0]
    for n, ref in enumerate(refs):
        for r in range(each):
            yield ref[r], (n * each + r) ^ split_ref[1]


def late_end_kernel(split_ref, *refs):
    outs = refs[-4:]
    rows = refs[0].shape[1] // 4
    for block, index in end_blocks(split_ref, refs[:-4]):
        part = pl.ds(pl.multiple_of(index * rows, rows), rows)
        for n, out_ref in enumerate(outs):
            out_ref[part] = block[n * rows : (n + 1) * rows].astype(F32)


def late_end(split, parts):
    width = parts[0].shape[2]
    return call(
        late_end_kernel,
        [like((width, width), F32)] * 4,
        [split, *parts],
        [SCALAR] + [whole(p) for p in parts],
    )


def d_hidden_kernel(wq_ref, wk_ref, wv_ref, *refs):
    out_ref = refs[-1]
    for s in range(out_ref.shape[0]):
        dq, dk, dv = refs[3 * s : 3 * s + 3]
        out_ref[s] = (
            dot(dq[...], wq_ref[...], 1, 1)
            + dot(dk[...], wk_ref[...], 1, 1)
            + dot(dv[...], wv_ref[...], 1, 1)
        )


def d_hidden_of(wq, wk, wv, parts, after=()):
    args = [wq, wk, wv] + [a for part in parts for a in part]
    shape = (len(parts),) + parts[0][0].shape
    flops = 6 * shape[0] * shape[1] * shape[2] ** 2
    return call(d_hidden_kernel, [like(shape, F32)], args, flops=flops, after=after)[0]


def feed_kernel(
    seqs,
    split_ref,
    x_ref,
    cot_ref,
    gain_ref,
    wo_ref,
    win_ref,
    wout_ref,
    *refs,
):
    att_refs = refs[:seqs]
    (
        out_ref,
        keep_ref,
        give_ref,
        gwo_ref,
        d_resid_ref,
        d_att_ref,
        slope_ref,
        y1,
        unit,
        h2,
        h2t,
        d_h2,
        f_all,
        du_all,
        scales,
    ) = refs[seqs:]
    step = pl.program_id(0)
    span = x_ref.shape[0]
    tile = 512
    tiles = [pl.ds(r, tile) for r in range(0, span, tile)]

    def att_tile(rows):
        each = att_refs[0].shape[0]
        return att_refs[rows.start // each][pl.ds(rows.start % each, tile)]

    @pl.when(step == 0)
    def _():
        for rows in tiles:
            y = x_ref[rows].astype(F32) + dot(att_tile(rows), wo_ref[...])
            y1[rows] = y
            scale = lax.rsqrt(jnp.mean(y * y, axis=-1, keepdims=True) + EPS)
            n = y * scale
            unit[rows] = n
            scales[rows] = jnp.broadcast_to(scale, (tile, scales.shape[1]))
            low = (n * gain_ref[...]).astype(BF16)
            h2[rows] = low
            h2t[:, rows] = turn(low)
            d_h2[rows] = jnp.zeros((tile, d_h2.shape[1]), F32)

    root = math.sqrt(2.0 / math.pi)
    for rows in tiles:
        u = dot(h2[rows], win_ref[...])
        square = u * u
        bend = jnp.tanh(root * u * (1.0 + 0.044715 * square))
        half = 0.5 + 0.5 * bend
        f = (u * half).astype(BF16)
        slope = half + (0.5 * root) * u * (1.0 - bend * bend) * (1.0 + 0.134145 * square)
        du = (dot(cot_ref[rows], wout_ref[...], 1, 1) * slope).astype(BF16)
        y1[rows] = y1[rows] + dot(f, wout_ref[...])
        d_h2[rows] = d_h2[rows] + dot(du, win_ref[...], 1, 1)
        f_all[:, rows] = turn(f)
        du_all[rows] = du
    grads = (
        dot(f_all[...], cot_ref[...]).astype(BF16),
        dot(h2t[...], du_all[...]).astype(BF16),
    )
    blocks, block = keep_ref.shape[0], keep_ref.shape[1] // 2
    count = grads[0].shape[0] // block
    for first, ref in ((0, give_ref), (2, keep_ref)):

        @pl.when(step // 2 * 2 == first)
        def _():
            for j in range(count):
                at = ((step % 2) * count + j) ^ (split_ref[1] % blocks)
                for n in range(2):
                    ref[at, n * block : (n + 1) * block] = grads[n][j * block : (j + 1) * block]


    @pl.when(step == pl.num_programs(0) - 1)
    def _():
        total = None
        grad = None
        for rows in tiles:
            out_ref[rows] = y1[rows].astype(BF16)
            up, n = d_h2[rows], unit[rows]
            here = jnp.sum(up * n, axis=0, keepdims=True)
            total = here if total is None else total + here
            d_n = up * gain_ref[...]
            d_y = scales[rows][:, :1] * (d_n - n * jnp.mean(d_n * n, axis=-1, keepdims=True))
            d_y = d_y + cot_ref[rows].astype(F32)
            low = d_y.astype(BF16)
            d_resid_ref[rows] = low
            d_att_ref[rows] = dot(low, wo_ref[...], 1, 1).astype(BF16)
            du_all[rows] = low
            f_all[:, rows] = turn(att_tile(rows))
        gwo_ref[...] = dot(f_all[...], du_all[...]).astype(BF16)
        slope_ref[...] = jnp.broadcast_to(total, slope_ref.shape)


def feed(split, x, att, cot, gain, wo, win, wout):
    span, width = x.shape
    hidden = win.shape[1]
    steps = hidden // width
    flat = lambda dtype: like((span, width), dtype)
    parts = like((16, 2 * hidden // 32, width), BF16)
    outs = [
        flat(BF16),
        parts,
        parts,
        like((width, width), BF16),
        flat(BF16),
        flat(BF16),
        like((8, width), F32),
    ]

    def chunk(c, split_ref):
        return ((1 - c // 2) ^ split_ref[0]) * 2 + c % 2

    return pl.pallas_call(
        lambda *refs: feed_kernel(len(att), *refs),
        grid_spec=pltpu.PrefetchScalarGridSpec(
            num_scalar_prefetch=1,
            grid=(steps,),
            in_specs=[whole(a) for a in (x, cot, gain, wo)]
            + [
                pl.BlockSpec((width, width), lambda c, r: (0, chunk(c, r))),
                pl.BlockSpec((width, width), lambda c, r: (chunk(c, r), 0)),
            ]
            + [whole(a) for a in att],
            out_specs=[whole(o) for o in outs],
            scratch_shapes=[
                pltpu.VMEM((span, width), F32),
                pltpu.VMEM((span, width), F32),
                pltpu.VMEM((span, width), BF16),
                pltpu.VMEM((width, span), BF16),
                pltpu.VMEM((span, width), F32),
                pltpu.VMEM((width, span), BF16),
                pltpu.VMEM((span, width), BF16),
                pltpu.VMEM((span, 128), F32),
            ],
        ),
        out_shape=outs,
        compiler_params=pltpu.CompilerParams(vmem_limit_bytes=VMEM_BYTES),
        cost_estimate=pl.CostEstimate(
            flops=int(COST * 12 * span * width * hidden),
            bytes_accessed=int(COST * (24 << 20)),
            transcendentals=0,
        ),
    )(split, x, cot, gain, wo, win, wout, *att)


def feed_end_kernel(split_ref, *refs):
    gout_ref, gin_ref = refs[-2:]
    width = gout_ref.shape[1]
    rows = refs[0].shape[1] // 2
    per = width // rows
    for block, index in end_blocks(split_ref, refs[:-2]):
        gout_ref[pl.ds(pl.multiple_of(index * rows, rows), rows)] = block[:rows].astype(F32)
        part = pl.ds(pl.multiple_of(index % per * rows, rows), rows)
        lanes = pl.ds(pl.multiple_of(index // per * width, width), width)
        gin_ref[part, lanes] = block[rows:].astype(F32)


def feed_end(split, parts):
    width = parts[0].shape[2]
    hidden = 16 * parts[0].shape[1]
    return call(
        feed_end_kernel,
        [like((hidden, width), F32), like((width, hidden), F32)],
        [split, *parts],
        [SCALAR] + [whole(p) for p in parts],
    )


def leave_kernel(
    x_ref, gain_ref, d_hidden_ref, rows_ref, d_summary_ref, d_resid_ref, out_ref, total_ref, buffer
):
    d_summary = d_summary_ref[0] * (1.0 / BLOCK)
    for t in range(BLOCK):
        strew(buffer, t, load_row(rows_ref, t).astype(F32) + d_summary)
    x = x_ref[0].astype(F32)
    scale = lax.rsqrt(jnp.mean(x * x, axis=-1, keepdims=True) + EPS)
    n = x * scale
    up = d_hidden_ref[0] + lift(buffer)
    total_ref[0] = jnp.broadcast_to(jnp.sum(up * n, axis=0, keepdims=True), total_ref.shape[1:])
    d_n = up * gain_ref[...]
    d_x = scale * (d_n - n * jnp.mean(d_n * n, axis=-1, keepdims=True))
    out_ref[0] = (d_x + d_resid_ref[0].astype(F32)).astype(BF16)


def leave(inputs, gain, d_hidden, rows, d_summary, d_resid, after=()):
    seqs, span, width = inputs.shape
    p, r, n, w = rows.shape
    args = [inputs, gain, d_hidden, rows, d_summary, d_resid]
    each = lambda a: pl.BlockSpec((1,) + a.shape[1:], lambda s: (s, 0, 0))
    outs = [like(inputs.shape, BF16), like((seqs, 8, width), F32)]
    return call(
        leave_kernel,
        outs,
        args,
        [
            each(inputs),
            whole(gain),
            each(d_hidden),
            pl.BlockSpec((p, r // seqs, n, w), lambda s: (0, s, 0, 0)),
            each(d_summary),
            each(d_resid),
        ],
        [row_buffer(span, width)],
        grid=(seqs,),
        out_specs=[each(o) for o in outs],
        after=after,
    )


def plan_plain(sort_scale, summary_all, real, w_sort):
    def plan_of(logits):
        plan = jnp.where(real, logits, NEG)
        for _ in range(ITERS):
            plan = plan - jax.nn.logsumexp(plan, axis=2, keepdims=True)
            fall = jax.nn.logsumexp(plan, axis=1, keepdims=True)
            plan = plan - jnp.where(real, fall, 0.0)
        return plan

    proj = lax.dot_general(
        summary_all, w_sort, (((2,), (0,)), ((), ())), preferred_element_type=F32
    ).astype(BF16)
    logits = sort_scale * jnp.einsum("sid,sjd->sij", proj, summary_all, preferred_element_type=F32)
    plan, back = jax.vjp(plan_of, logits)
    return proj, plan, back


def places():
    dp, seq = lax.axis_index("dp"), lax.axis_index("seq")
    core, x, y = dp % 2, (dp // 2) % 2, seq % 2
    line = (seq // 2) % 2 * 2 + (seq // 4) % 2
    return jnp.stack([core, core * 16 + x * 8 + y * 4 + line]).astype(jnp.int32)


def body(
    inputs,
    segment_ids,
    real_block,
    gain_attn,
    w_query,
    w_key,
    w_value,
    w_output,
    w_sort,
    gain_ffn,
    w_in,
    w_out,
    cotangent,
):
    seqs, span, width = inputs.shape
    blocks = span // BLOCK
    seq_size, dp_size = lax.axis_size("seq"), lax.axis_size("dp")
    count = blocks * seq_size
    small_plan = count == 128
    sort_scale = SORT_GAIN * BLOCK / math.sqrt(width)
    gain_one = gain_attn.astype(F32).reshape(1, width)
    gain_two = gain_ffn.astype(F32).reshape(1, width)
    place = lax.axis_index("seq")
    first_block = place * blocks
    place = place.astype(jnp.int32).reshape(1, 1)
    split = places()

    hidden, *rows = enter(inputs, gain_one, real_block, seq_size)
    spread = [exchange(r) for r in rows]
    q, k, v, qt, kt, vt = project(hidden, w_query, w_key, w_value)

    if small_plan:
        proj, steps, plan, low, entropy, total_blocks = call(
            lambda *refs: plan_kernel(sort_scale, *refs),
            [
                like((seqs, count, width), BF16),
                like((2 * ITERS, seqs, count, count), F32),
                like((seqs, count, count), F32),
                like((seqs, count, count), BF16),
                like((8, 128), F32),
                like((8, 128), F32),
            ],
            [spread[0], w_sort],
            after=(q,),
        )
        entropy = entropy[0, 0]
    else:
        summary_all, reals = told_of(spread[0], seqs, width)
        real = reals[:, None, :] == 1
        proj, plan, plan_back = plan_plain(sort_scale, summary_all, real, w_sort)
        prob = jnp.exp(plan)
        low = prob.astype(BF16)
        entropy = jnp.sum(jnp.where(reals[:, :, None] == 1, prob * plan, 0.0))
        total_blocks = jnp.full((8, 128), jnp.sum(reals.astype(F32)))
    for bit in bits(dp_size):
        total_blocks = total_blocks + swap(total_blocks, "dp", bit)

    segments = segment_ids.reshape(seqs, blocks, BLOCK)
    allowed = (segments.transpose(0, 2, 1)[:, :, :, None] == segments[:, None]).astype(F32)
    allowed = allowed.reshape(seqs, BLOCK, span)

    att, kept = [], []
    for s in range(seqs):
        part = mix(low, spread[s], s, width)
        here, *rest = attend(exchange(part), allowed, w_key, w_value, k, qt, vt, s)
        att.append(here)
        kept.append(rest)

    flat = (seqs * span, width)
    output, keep, give, grad_output, d_resid, d_att, slope = feed(
        split,
        inputs.reshape(flat),
        att,
        cotangent.reshape(flat),
        gain_two,
        w_output,
        w_in,
        w_out,
    )
    d_resid = d_resid.reshape(inputs.shape)
    d_att = d_att.reshape(inputs.shape)
    stages = sum_stages(keep, give)
    next(stages)
    grads, d_mixed = [], []
    chunks = chunk_shape(seq_size, blocks, width)
    for s in range(seqs):
        sent, *here = attend_back(d_att, q, v, kt, kept[s][1:], w_key, w_value, chunks, s)
        grads.append(here)
        if s == 0:
            next(stages)
        d_mixed.append(exchange(sent))
    parts = late(
        split, hidden, grad_output, [[kept[s][0], *grads[s]] for s in range(seqs)]
    )
    next(stages)
    d_hidden = d_hidden_of(w_query, w_key, w_value, [g[:3] for g in grads])
    late_stages = sum_stages(*parts)
    d_rows, d_prob = unmix(low, spread, d_mixed)
    heard = sum_seq(d_prob)
    d_rows = exchange(d_rows)
    *_, last = stages
    grad_out, grad_in = feed_end(split, last)
    *_, last = late_stages
    grad_query, grad_key, grad_value, grad_output = late_end(split, last)

    if small_plan:
        args = [
            total_blocks,
            place,
            heard,
            spread[0],
            w_sort,
            proj,
            steps,
            plan,
        ]
        outs = [like((seqs, blocks, width), F32), like((width, width), BF16)]
        d_summary, grad_sort = pl.pallas_call(
            lambda *refs: plan_back_kernel(sort_scale, *refs),
            out_shape=outs,
            grid=(1,),
            in_specs=[whole(total_blocks), SCALAR] + [whole(a) for a in args[2:]],
            out_specs=[whole(o) for o in outs],
            scratch_shapes=[pltpu.VMEM((count, width), F32)],
            compiler_params=pltpu.CompilerParams(vmem_limit_bytes=VMEM_BYTES),
        )(*args)
    else:
        d_prob = heard.astype(F32)
        d_plan = prob * d_prob - (
            jnp.where(reals[:, :, None] == 1, prob * plan + prob, 0.0) / total_blocks[0, 0]
        )
        (d_logits,) = plan_back(d_plan)
        d_logits = d_logits.astype(BF16)
        d_proj = sort_scale * jnp.einsum(
            "sij,sjd->sid", d_logits, summary_all, preferred_element_type=F32
        )
        d_proj = d_proj.astype(BF16)
        grad_sort = jnp.einsum("sid,sie->de", summary_all, d_proj, preferred_element_type=F32)
        d_summary = sort_scale * jnp.einsum(
            "sij,sid->sjd", d_logits, proj, preferred_element_type=F32
        ) + jnp.einsum("sie,de->sid", d_proj, w_sort, preferred_element_type=F32)
        d_summary = lax.dynamic_slice_in_dim(d_summary, first_block, blocks, 1)

    grad_sort = grad_sort.astype(BF16)
    grad_sort = add(grad_sort, send(grad_sort, *CORE))
    input_grad, gains = leave(
        inputs, gain_one, d_hidden, d_rows, d_summary, d_resid, (grad_sort,)
    )
    grad_sort = grad_sort.astype(F32) + send(grad_sort, 2, 0).astype(F32)
    small = jnp.concatenate(
        [
            jnp.sum(gains[:, :1], axis=0),
            slope[:1],
            jnp.full((1, width), entropy / seq_size),
            jnp.zeros((5, width), F32),
        ]
    )
    small = lax.all_to_all(
        jnp.broadcast_to(small[None], (dp_size * seq_size,) + small.shape),
        ("dp", "seq"),
        0,
        0,
        tiled=True,
    )
    small = jnp.sum(small, axis=0)
    penalty = -small[2, 0] / total_blocks[0, 0]
    return (
        output.reshape(inputs.shape),
        input_grad,
        penalty,
        small[0],
        grad_query,
        grad_key,
        grad_value,
        grad_output,
        grad_sort,
        small[1],
        grad_in,
        grad_out,
    )


def solution(mesh):
    placed = (
        P("dp", "seq", None),
        P("dp", "seq"),
        P("dp", "seq"),
        P(),
        P(),
        P(),
        P(),
        P(),
        P(),
        P(),
        P(),
        P(),
        P("dp", "seq", None),
    )
    return jax.shard_map(
        body,
        mesh=mesh,
        in_specs=placed,
        out_specs=(
            P("dp", "seq", None),
            P("dp", "seq", None),
            P(),
            P(),
            P(),
            P(),
            P(),
            P(),
            P(),
            P(),
            P(),
            P(),
        ),
        check_vma=False,
    )
```

profile of v0, /device:TPU:0, one launch (start us, length us, event | category | flops | bytes accessed | tf_op | source)
XLA Modules:
  0.0 344.1 jit_solution(106926280210491328)
XLA Ops:
  3.4 4.7 %shard_map.220 = (bf16[2,512,512]{2,1,0:T(8,128)(2,1)}, bf16[8,7,16,512]{3,2,1,0:T(8,128)(2,1)}, bf16[8,4,16,512]{3,2,1,0:T(8,128)(2,1)}) custom-call(bf16[2,512,512]{2,1,0:T(8,128)(2,1)} %refs_0_.5, f32[1,512]{1,0:T(1,128)} %bitcast.29, bf16[16,512]{1,0:T(8,128)(2,1)} %bitcast.26), custom_call_target="tpu_custom_call" | custom-call | bytes 10672128 | tf_op jit(solution)/shard_map/pallas_call | solution.py:118
  8.1 30.7 %all_to_all.40.refs_0_.refs_1_.refs_3_ = bf16[8,7,16,512]{3,2,1,0:T(8,128)(2,1)} all-to-all(bf16[8,7,16,512]{3,2,1,0:T(8,128)(2,1)} %get-tuple-element.86), channel_id=1, replica_groups=mesh['dp'=4,'seq'=8] {'seq'}, dimensions={0} | all-to-all | bytes 1835008 | tf_op jit(solution)/shard_map/all_to_all | solution.py:84
  38.8 3.5 %all-to-all-start.2 = ((bf16[8,4,16,512]{3,2,1,0:T(8,128)(2,1)}), bf16[8,4,16,512]{3,2,1,0:T(8,128)(2,1)S(1)}, u32[]{:S(2)}, u32[]{:S(2)}) async-start(bf16[8,4,16,512]{3,2,1,0:T(8,128)(2,1)} %get-tuple-element.94), calls=%async_computation.2 | async-start | bytes 1048576 | tf_op jit(solution)/shard_map/all_to_all | solution.py:84
  42.3 4.9 %shard_map.221 = (bf16[2,512,512]{2,1,0:T(8,128)(2,1)}, bf16[2,512,512]{2,1,0:T(8,128)(2,1)}, bf16[2,512,512]{2,1,0:T(8,128)(2,1)}, bf16[2,512,512]{2,1,0:T(8,12...) custom-call(bf16[2,512,512]{2,1,0:T(8,128)(2,1)} %get-tuple-element.87.refs_0_.refs_1_, ...), custom_call_target="tpu_custom_call" | custom-call | flops 4831838208 | bytes 26738688 | tf_op jit(solution)/shard_map/pallas_call | solution.py:118
  47.3 5.3 %shard_map.222 = (bf16[2,128,512]{2,1,0:T(8,128)(2,1)}, f32[16,2,128,128]{3,2,1,0:T(8,128)}, f32[2,128,128]{2,1,0:T(8,128)}, bf16[2,128,128]{2,1,0:T(8,128)(2,1)}, f32[8,128]{1,0:T(8,128)}, /*index=5*/f32[8,128]{1,0:T(8,128)}) custom-call(bf16[8,7,16,512]{3,2,1,0:T(8,128)(2,1)} %all_to_all.40.refs_0_.refs_1_.refs_3_, bf16[512,512]{1,0:T(8,128)(2,1)} %refs_4_.3, ...), custom_call_target="tpu_custom_call" | custom-call | bytes 12017664 | tf_op jit(solution)/shard_map/pallas_call | solution.py:118
  52.6 2.3 shard_map.223
  56.4 4.4 %all-to-all-start.1 = ((bf16[8,4,16,512]{3,2,1,0:T(8,128)(2,1)}), bf16[8,4,16,512]{3,2,1,0:T(8,128)(2,1)S(1)}, u32[]{:S(2)}, u32[]{:S(2)}) async-start(bf16[8,4,16,512]{3,2,1,0:T(8,128)(2,1)} %shard_map.223), calls=%async_computation.1 | async-start | bytes 1048576 | tf_op jit(solution)/shard_map/all_to_all | solution.py:84
  60.9 2.2 shard_map.225
  63.1 11.5 %all-to-all-done.1.refs_0_ = bf16[8,4,16,512]{3,2,1,0:T(8,128)(2,1)S(1)} async-done(((bf16[8,4,16,512]{3,2,1,0:T(8,128)(2,1)}), bf16[8,4,16,512]{3,2,1,0:T(8,128)(2,1)S(1)}, u32[]{:S(2)}, u32[]{:S(2)}) %all-to-all-start.1) | async-done | bytes 524320 | tf_op jit(solution)/shard_map/all_to_all | solution.py:84
  74.5 3.7 %all-to-all-start.3 = ((bf16[8,4,16,512]{3,2,1,0:T(8,128)(2,1)}), bf16[8,4,16,512]{3,2,1,0:T(8,128)(2,1)S(1)}, u32[]{:S(2)}, u32[]{:S(2)}) async-start(bf16[8,4,16,512]{3,2,1,0:T(8,128)(2,1)} %shard_map.225), calls=%async_computation.3 | async-start | bytes 1048576 | tf_op jit(solution)/shard_map/all_to_all | solution.py:84
  80.8 9.8 %shard_map.224 = (bf16[512,512]{1,0:T(8,128)(2,1)}, bf16[512,512]{1,0:T(8,128)(2,1)}, bf16[512,512]{1,0:T(8,128)(2,1)}, bf16[512,512]{1,0:T(8,128)(2,1)}, f32[16,64,256]{2,1,0:T(8,128)}) custom-call(bf16[8,4,16,512]{3,2,1,0:T(8,128)(2,1)} %copy-done.13, f32[2,32,512]{2,1,0:T(8,128)} %compare_convert_fusion.refs_1_, bf16[512,512]{1,0:T(8,128)(2,1)} %refs_1_.5, ...), custom_call_target="tpu_custom_call" | custom-call | flops 3221225472 | bytes 23986176 | tf_op jit(solution)/shard_map/pallas_call | solution.py:118
  92.7 9.8 %shard_map.226 = (bf16[512,512]{1,0:T(8,128)(2,1)}, bf16[512,512]{1,0:T(8,128)(2,1)}, bf16[512,512]{1,0:T(8,128)(2,1)}, bf16[512,512]{1,0:T(8,128)(2,1)}, f32[16,64,256]{2,1,0:T(8,128)}) custom-call(bf16[8,4,16,512]{3,2,1,0:T(8,128)(2,1)} %copy-done.12, f32[2,32,512]{2,1,0:T(8,128)} %compare_convert_fusion.refs_1_, bf16[512,512]{1,0:T(8,128)(2,1)} %refs_1_.5, ...), custom_call_target="tpu_custom_call" | custom-call | flops 3221225472 | bytes 23986176 | tf_op jit(solution)/shard_map/pallas_call | solution.py:118
  102.5 25.8 %shard_map.227 = (bf16[1024,512]{1,0:T(8,128)(2,1)}, bf16[16,128,512]{2,1,0:T(8,128)(2,1)}, bf16[16,128,512]{2,1,0:T(8,128)(2,1)}, bf16[512,512]{1,0:T(8,128)(2,...) custom-call(s32[2]{0:T(128)} %pad_add_fusion.refs_0_, bf16[1024,512]{1,0:T(8,128)(2,1)} %bitcast.24, ...), custom_call_target="tpu_custom_call" | custom-call | flops 38654705664 | bytes 75497472 | tf_op jit(solution)/shard_map/pallas_call | solution.py:807
  128.3 11.1 %shard_map.229 = (bf16[8,4,16,512]{3,2,1,0:T(8,128)(2,1)}, bf16[512,512]{1,0:T(8,128)(2,1)}, bf16[512,512]{1,0:T(8,128)(2,1)}, bf16[512,512]{1,0:T(8,128)(2,1)},...) custom-call(bf16[2,512,512]{2,1,0:T(8,128)(2,1)} %bitcast.37, ...), custom_call_target="tpu_custom_call" | custom-call | flops 4831838208 | bytes 31457280 | tf_op jit(solution)/shard_map/pallas_call | solution.py:118
  139.4 4.5 %all-to-all-start.5 = ((bf16[8,4,16,512]{3,2,1,0:T(8,128)(2,1)}), bf16[8,4,16,512]{3,2,1,0:T(8,128)(2,1)S(1)}, u32[]{:S(2)}, u32[]{:S(2)}) async-start(bf16[8,4,16,512]{3,2,1,0:T(8,128)(2,1)} %get-tuple-element.113), calls=%async_computation.5 | async-start | bytes 1048576 | tf_op jit(solution)/shard_map/all_to_all | solution.py:84
  143.9 10.9 %shard_map.228 = (bf16[8,4,16,512]{3,2,1,0:T(8,128)(2,1)}, bf16[512,512]{1,0:T(8,128)(2,1)}, bf16[512,512]{1,0:T(8,128)(2,1)}, bf16[512,512]{1,0:T(8,128)(2,1)},...) custom-call(bf16[2,512,512]{2,1,0:T(8,128)(2,1)} %bitcast.38, ...), custom_call_target="tpu_custom_call" | custom-call | flops 4831838208 | bytes 31457280 | tf_op jit(solution)/shard_map/pallas_call | solution.py:118
  154.8 2.3 all-to-all-done.5.refs_4_
  157.1 3.7 %all-to-all-start.4 = ((bf16[8,4,16,512]{3,2,1,0:T(8,128)(2,1)}), bf16[8,4,16,512]{3,2,1,0:T(8,128)(2,1)S(1)}, u32[]{:S(2)}, u32[]{:S(2)}) async-start(bf16[8,4,16,512]{3,2,1,0:T(8,128)(2,1)} %get-tuple-element.112), calls=%async_computation.4 | async-start | bytes 1048576 | tf_op jit(solution)/shard_map/all_to_all | solution.py:84
  160.8 7.6 %shard_map.234 = (bf16[16,64,512]{2,1,0:T(8,128)(2,1)}, bf16[16,64,512]{2,1,0:T(8,128)(2,1)}) custom-call(s32[2]{0:T(128)} %pad_add_fusion.refs_0_, bf16[2,512,512]{2,1,0:T(8,128)(2,1)} %get-tuple-element.87.refs_0_.refs_1_, bf16[512,512]{1,0:T(8,128)(2,1)} %get-tuple-element.127.refs_2_, bf16[512,512]{1,0:T(8,128)(2,1)} %get-tuple-element.128.refs_3_, ...), custom_call_target="tpu_custom_call" | custom-call | flops 8053063680 | bytes 29884440 | tf_op jit(solution)/shard_map/pallas_call | solution.py:118
  168.7 7.3 %all-to-all-done.4.refs_3_ = bf16[8,4,16,512]{3,2,1,0:T(8,128)(2,1)S(1)} async-done(((bf16[8,4,16,512]{3,2,1,0:T(8,128)(2,1)}), bf16[8,4,16,512]{3,2,1,0:T(8,128)(2,1)S(1)}, u32[]{:S(2)}, u32[]{:S(2)}) %all-to-all-start.4) | async-done | bytes 524320 | tf_op jit(solution)/shard_map/all_to_all | solution.py:84
  176.8 3.4 shard_map.231
  180.2 4.0 %all-to-all-start.6 = ((bf16[8,8,16,512]{3,2,1,0:T(8,128)(2,1)}), bf16[8,8,16,512]{3,2,1,0:T(8,128)(2,1)S(1)}, u32[]{:S(2)}, u32[]{:S(2)}) async-start(bf16[8,8,16,512]{3,2,1,0:T(8,128)(2,1)} %get-tuple-element.114), calls=%async_computation.6 | async-start | bytes 2097152 | tf_op jit(solution)/shard_map/all_to_all | solution.py:84
  184.2 1.9 collective-permute-start.2
  186.0 2.6 shard_map.235
  190.3 1.8 collective-permute-start.9
  192.1 13.9 %collective-permute-done.2 = bf16[2,128,128]{2,1,0:T(8,128)(2,1)S(1)} collective-permute-done((bf16[2,128,128]{2,1,0:T(8,128)(2,1)S(1)}, bf16[2,128,128]{2,1,0:T(8,128)(2,1)S(1)}, u32[]{:S(2)}, u32[]{:S(2)}) %collective-permute-start.2) | collective-permute-done | bytes 65568 | tf_op jit(solution)/shard_map/ppermute | solution.py:29
  206.1 4.3 %collective-permute-done.7.refs_1_ = bf16[4,64,512]{2,1,0:T(8,128)(2,1)S(1)} collective-permute-done((bf16[4,64,512]{2,1,0:T(8,128)(2,1)}, bf16[4,64,512]{2,1,0:T(8,128)(2,1)S(1)}, u32[]{:S(2)}, u32[]{:S(2)}) %collective-permute-start.7) | collective-permute-done | bytes 262176 | tf_op jit(solution)/shard_map/ppermute | solution.py:36
  211.2 1.9 shard_map.236
  213.2 2.4 collective-permute-start.10
  221.0 3.7 %shard_map.239 = (bf16[4,128,512]{2,1,0:T(8,128)(2,1)}, bf16[4,128,512]{2,1,0:T(8,128)(2,1)}, bf16[4,128,512]{2,1,0:T(8,128)(2,1)}, bf16[4,128,512]{2,1,0:T(8,128)(2,1)}) custom-call(bf16[16,128,512]{2,1,0:T(8,128)(2,1)} %get-tuple-element.148.refs_0_, bf16[16,128,512]{2,1,0:T(8,128)(2,1)} %copy-done.6), custom_call_target="tpu_custom_call" | custom-call | bytes 18874368 | tf_op jit(solution)/shard_map/pallas_call | solution.py:118
  225.6 2.7 collective-permute-start.27
  239.1 5.0 %shard_map.232 = (f32[2,16,512]{2,1,0:T(8,128)}, bf16[512,512]{1,0:T(8,128)(2,1)}) custom-call(f32[8,128]{1,0:T(8,128)} %add.62.refs_0_, s32[1,1]{1,0:T(1,128)} %bitcast.10.refs_1_, bf16[2,128,128]{2,1,0:T(8,128)(2,1)} %add_convert_fusion.1.refs_2_, bf16[8,7,16,512]{3,2,1,0:T(8,128)(2,1)} %all_to_all.40.refs_0_.refs_1_.refs_3_, bf16[512,512]{1,0:T(8,128)(2,1)} %refs_4_.3, ...), custom_call_target="tpu_custom_call" | custom-call | tf_op jit(solution)/shard_map/pallas_call | solution.py:1046
  244.2 2.6 collective-permute-start.13
  246.8 3.9 %collective-permute-done.27.refs_3_ = bf16[4,128,512]{2,1,0:T(8,128)(2,1)S(1)} collective-permute-done((bf16[4,128,512]{2,1,0:T(8,128)(2,1)}, bf16[4,128,512]{2,1,0:T(8,128)(2,1)S(1)}, u32[]{:S(2)}, u32[]{:S(2)}) %collective-permute-start.27) | collective-permute-done | bytes 524320 | tf_op jit(solution)/shard_map/ppermute | solution.py:36
  251.6 2.4 shard_map.240
  255.1 3.3 collective-permute-start.30
  258.4 5.4 %shard_map.230.refs_2_ = f32[2,512,512]{2,1,0:T(8,128)} custom-call(bf16[512,512]{1,0:T(8,128)(2,1)} %refs_0_.4, bf16[512,512]{1,0:T(8,128)(2,1)} %refs_1_.5, bf16[512,512]{1,0:T(8,128)(2,1)} %refs_2_.7, bf16[512,512]{1,0:T(8,128)(2,1)} %get-tuple-element.103.refs_3_.refs_4_, bf16[512,512]{1,0:T(8,128)(2,1)} %get-tuple-element.104.refs_4_.refs_5_, ...), custom_call_target="tpu_custom_call" | custom-call | flops 4831838208 | bytes 20447232 | tf_op jit(solution)/shard_map/pallas_call | solution.py:118
  269.3 1.8 shard_map.241
  272.6 3.5 %collective-permute-done.18.refs_4_ = bf16[4,64,512]{2,1,0:T(8,128)(2,1)} collective-permute-done((bf16[4,64,512]{2,1,0:T(8,128)(2,1)S(1)}, bf16[4,64,512]{2,1,0:T(8,128)(2,1)}, u32[]{:S(2)}, u32[]{:S(2)}) %collective-permute-start.18) | collective-permute-done | bytes 262176 | tf_op jit(solution)/shard_map/ppermute | solution.py:36
  277.0 5.7 %shard_map.233 = (bf16[2,512,512]{2,1,0:T(8,128)(2,1)}, f32[2,8,512]{2,1,0:T(8,128)}) custom-call(bf16[2,512,512]{2,1,0:T(8,128)(2,1)} %refs_0_.5, f32[1,512]{1,0:T(1,128)} %bitcast.30, f32[2,512,512]{2,1,0:T(8,128)} %shard_map.230.refs_2_, bf16[8,8,16,512]{3,2,1,0:T(8,128)(2,1)} %copy-done.2, f32[2,16,512]{2,1,0:T(8,128)} %get-tuple-element.120.refs_4_, ...), custom_call_target="tpu_custom_call" | custom-call | bytes 19175424 | tf_op jit(solution)/shard_map/pallas_call | solution.py:118
  285.7 3.6 %all-to-all-start.7 = ((f32[32,8,512]{2,1,0:T(8,128)}), f32[32,8,512]{2,1,0:T(8,128)S(1)}, u32[]{:S(2)}, u32[]{:S(2)}) async-start(f32[32,8,512]{2,1,0:T(8,128)} %broadcast_in_dim.19), calls=%async_computation.7 | async-start | bytes 1048576 | tf_op jit(solution)/shard_map/all_to_all | solution.py:1086
  290.7 3.0 collective-permute-done.31
  295.4 1.9 collective-permute-start.34
  299.5 12.5 %collective-permute-done.36.refs_4_ = bf16[4,128,512]{2,1,0:T(8,128)(2,1)S(1)} collective-permute-done((bf16[4,128,512]{2,1,0:T(8,128)(2,1)S(1)}, bf16[4,128,512]{2,1,0:T(8,128)(2,1)S(1)}, u32[]{:S(2)}, u32[]{:S(2)}) %collective-permute-start.36) | collective-permute-done | bytes 524320 | tf_op jit(solution)/shard_map/ppermute | solution.py:36
  312.0 10.6 %collective-permute-done.35.refs_3_ = bf16[4,128,512]{2,1,0:T(8,128)(2,1)S(1)} collective-permute-done((bf16[4,128,512]{2,1,0:T(8,128)(2,1)S(1)}, bf16[4,128,512]{2,1,0:T(8,128)(2,1)S(1)}, u32[]{:S(2)}, u32[]{:S(2)}) %collective-permute-start.35) | collective-permute-done | bytes 524320 | tf_op jit(solution)/shard_map/ppermute | solution.py:36
  324.3 3.8 %shard_map.238 = (f32[512,512]{1,0:T(8,128)}, f32[512,512]{1,0:T(8,128)}, f32[512,512]{1,0:T(8,128)}, f32[512,512]{1,0:T(8,128)}) custom-call(s32[2]{0:T(128)} %pad_add_fusion.refs_0_, bf16[4,64,512]{2,1,0:T(8,128)(2,1)} %copy-done.7, bf16[4,64,512]{2,1,0:T(8,128)(2,1)} %collective-permute-done.16.refs_2_, ...), custom_call_target="tpu_custom_call" | custom-call | bytes 18874392 | tf_op jit(solution)/shard_map/pallas_call | solution.py:118
  328.1 5.0 %collective-permute-done.23 = bf16[512,512]{1,0:T(8,128)(2,1)S(1)} collective-permute-done((bf16[512,512]{1,0:T(8,128)(2,1)S(1)}, bf16[512,512]{1,0:T(8,128)(2,1)S(1)}, u32[]{:S(2)}, u32[]{:S(2)}) %collective-permute-start.23) | collective-permute-done | bytes 524320 | tf_op jit(solution)/shard_map/ppermute | solution.py:36
  336.8 6.1 %shard_map.242 = (f32[2048,512]{1,0:T(8,128)}, f32[512,2048]{1,0:T(8,128)}) custom-call(s32[2]{0:T(128)} %pad_add_fusion.refs_0_, bf16[4,128,512]{2,1,0:T(8,128)(2,1)} %copy-done.3, bf16[4,128,512]{2,1,0:T(8,128)(2,1)} %copy-done.11, bf16[4,128,512]{2,1,0:T(8,128)(2,1)} %copy-done.10, bf16[4,128,512]{2,1,0:T(8,128)(2,1)} %copy-done.9, ...), custom_call_target="tpu_custom_call" | custom-call | bytes 37748760 | tf_op jit(solution)/shard_map/pallas_call | solution.py:118
  (175 shorter events, 51.1 us)
Async XLA Ops:
  38.8 17.6 %all-to-all-start.2 = ((bf16[8,4,16,512]{3,2,1,0:T(8,128)(2,1)}), bf16[8,4,16,512]{3,2,1,0:T(8,128)(2,1)S(1)}, u32[]{:S(2)}, u32[]{:S(2)}) async-start(bf16[8,4,16,512]{3,2,1,0:T(8,128)(2,1)} %get-tuple-element.94), calls=%async_computation.2 | async-start | bytes 1048576 | tf_op jit(solution)/shard_map/all_to_all | solution.py:84
  56.4 18.1 %all-to-all-start.1 = ((bf16[8,4,16,512]{3,2,1,0:T(8,128)(2,1)}), bf16[8,4,16,512]{3,2,1,0:T(8,128)(2,1)S(1)}, u32[]{:S(2)}, u32[]{:S(2)}) async-start(bf16[8,4,16,512]{3,2,1,0:T(8,128)(2,1)} %shard_map.223), calls=%async_computation.1 | async-start | bytes 1048576 | tf_op jit(solution)/shard_map/all_to_all | solution.py:84
  74.5 17.4 %all-to-all-start.3 = ((bf16[8,4,16,512]{3,2,1,0:T(8,128)(2,1)}), bf16[8,4,16,512]{3,2,1,0:T(8,128)(2,1)S(1)}, u32[]{:S(2)}, u32[]{:S(2)}) async-start(bf16[8,4,16,512]{3,2,1,0:T(8,128)(2,1)} %shard_map.225), calls=%async_computation.3 | async-start | bytes 1048576 | tf_op jit(solution)/shard_map/all_to_all | solution.py:84
  139.4 17.7 %all-to-all-start.5 = ((bf16[8,4,16,512]{3,2,1,0:T(8,128)(2,1)}), bf16[8,4,16,512]{3,2,1,0:T(8,128)(2,1)S(1)}, u32[]{:S(2)}, u32[]{:S(2)}) async-start(bf16[8,4,16,512]{3,2,1,0:T(8,128)(2,1)} %get-tuple-element.113), calls=%async_computation.5 | async-start | bytes 1048576 | tf_op jit(solution)/shard_map/all_to_all | solution.py:84
  143.9 75.8 %collective-permute-start.24 = (bf16[16,128,512]{2,1,0:T(8,128)(2,1)}, bf16[16,128,512]{2,1,0:T(8,128)(2,1)S(1)}, u32[]{:S(2)}, u32[]{:S(2)}) collective-permute-start(bf16[16,128,512]{2,1,0:T(8,128)(2,1)} %get-tuple-element.149), channel_id=1, source_target_pairs={{0,8},{1,9},{2,10},{3,11},{4,12},{5,13},{6,14},{7,15},{8,0},{9,1},... | collective-permute-start | bytes 6291464 | tf_op jit(solution)/shard_map/ppermute | solution.py:36
  157.1 18.9 %all-to-all-start.4 = ((bf16[8,4,16,512]{3,2,1,0:T(8,128)(2,1)}), bf16[8,4,16,512]{3,2,1,0:T(8,128)(2,1)S(1)}, u32[]{:S(2)}, u32[]{:S(2)}) async-start(bf16[8,4,16,512]{3,2,1,0:T(8,128)(2,1)} %get-tuple-element.112), calls=%async_computation.4 | async-start | bytes 1048576 | tf_op jit(solution)/shard_map/all_to_all | solution.py:84
  168.4 17.6 %collective-permute-start.6 = (bf16[16,64,512]{2,1,0:T(8,128)(2,1)}, bf16[16,64,512]{2,1,0:T(8,128)(2,1)}, u32[]{:S(2)}, u32[]{:S(2)}) collective-permute-start(bf16[16,64,512]{2,1,0:T(8,128)(2,1)} %get-tuple-element.135), channel_id=1, source_target_pairs={{0,8},{1,9},{2,10},{3,11},{4,12},{5,13},{6,14},{7,15},{8,0},{9,1},... | collective-permute-start | bytes 3145736 | tf_op jit(solution)/shard_map/ppermute | solution.py:36
  180.2 95.9 %all-to-all-start.6 = ((bf16[8,8,16,512]{3,2,1,0:T(8,128)(2,1)}), bf16[8,8,16,512]{3,2,1,0:T(8,128)(2,1)S(1)}, u32[]{:S(2)}, u32[]{:S(2)}) async-start(bf16[8,8,16,512]{3,2,1,0:T(8,128)(2,1)} %get-tuple-element.114), calls=%async_computation.6 | async-start | bytes 2097152 | tf_op jit(solution)/shard_map/all_to_all | solution.py:84
  184.2 21.8 %collective-permute-start.2 = (bf16[2,128,128]{2,1,0:T(8,128)(2,1)S(1)}, bf16[2,128,128]{2,1,0:T(8,128)(2,1)S(1)}, u32[]{:S(2)}, u32[]{:S(2)}) collective-permute-start(bf16[2,128,128]{2,1,0:T(8,128)(2,1)S(1)} %copy-done.29), channel_id=1, source_target_pairs={{0,1},{1,0},{2,3},{3,2},{4,5},{5,4},{6,7},{7,6},{8,9},{9,8},{10,11... | collective-permute-start | bytes 196616 | tf_op jit(solution)/shard_map/ppermute | solution.py:29
  188.6 21.8 %collective-permute-start.7 = (bf16[4,64,512]{2,1,0:T(8,128)(2,1)}, bf16[4,64,512]{2,1,0:T(8,128)(2,1)S(1)}, u32[]{:S(2)}, u32[]{:S(2)}) collective-permute-start(bf16[4,64,512]{2,1,0:T(8,128)(2,1)} %get-tuple-element.137), channel_id=1, source_target_pairs={{0,1},{1,0},{2,3},{3,2},{4,5},{5,4},{6,7},{7,6},{8,9},{9,8},{10,11... | collective-permute-start | bytes 786440 | tf_op jit(solution)/shard_map/ppermute | solution.py:36
  188.8 21.6 %collective-permute-start.8 = (bf16[4,64,512]{2,1,0:T(8,128)(2,1)}, bf16[4,64,512]{2,1,0:T(8,128)(2,1)S(1)}, u32[]{:S(2)}, u32[]{:S(2)}) collective-permute-start(bf16[4,64,512]{2,1,0:T(8,128)(2,1)} %get-tuple-element.138), channel_id=1, source_target_pairs={{0,16},{1,17},{2,18},{3,19},{4,20},{5,21},{6,22},{7,23},{8,24},{9,... | collective-permute-start | bytes 786440 | tf_op jit(solution)/shard_map/ppermute | solution.py:36
  190.3 20.1 %collective-permute-start.9 = (bf16[4,64,512]{2,1,0:T(8,128)(2,1)}, bf16[4,64,512]{2,1,0:T(8,128)(2,1)S(1)}, u32[]{:S(2)}, u32[]{:S(2)}) collective-permute-start(bf16[4,64,512]{2,1,0:T(8,128)(2,1)} %get-tuple-element.139), channel_id=1, source_target_pairs={{0,17},{1,16},{2,19},{3,18},{4,21},{5,20},{6,23},{7,22},{8,25},{9,... | collective-permute-start | bytes 786440 | tf_op jit(solution)/shard_map/ppermute | solution.py:36
  206.0 19.5 %collective-permute-start.3 = (bf16[2,128,128]{2,1,0:T(8,128)(2,1)S(1)}, bf16[2,128,128]{2,1,0:T(8,128)(2,1)S(1)}, u32[]{:S(2)}, u32[]{:S(2)}) collective-permute-start(bf16[2,128,128]{2,1,0:T(8,128)(2,1)S(1)} %add_convert_fusion.3), channel_id=1, source_target_pairs={{0,2},{1,3},{2,0},{3,1},{4,6},{5,7},{6,4},{7,5},{8,10},{9,11},{10,... | collective-permute-start | bytes 196616 | tf_op jit(solution)/shard_map/ppermute | solution.py:29
  213.2 15.0 %collective-permute-start.10 = (bf16[1,64,512]{2,1,0:T(8,128)(2,1)}, bf16[1,64,512]{2,1,0:T(8,128)(2,1)S(1)}, u32[]{:S(2)}, u32[]{:S(2)}) collective-permute-start(bf16[1,64,512]{2,1,0:T(8,128)(2,1)} %get-tuple-element.141), channel_id=1, source_target_pairs={{0,4},{1,5},{2,6},{3,7},{4,0},{5,1},{6,2},{7,3},{8,12},{9,13},{10,... | collective-permute-start | bytes 196616 | tf_op jit(solution)/shard_map/ppermute | solution.py:36
  215.6 1.2 collective-permute-start
  216.7 8.3 %collective-permute-start.1 = (f32[8,128]{1,0:T(8,128)S(1)}, f32[8,128]{1,0:T(8,128)S(1)}, u32[]{:S(2)}, u32[]{:S(2)}) collective-permute-start(f32[8,128]{1,0:T(8,128)S(1)} %add.61), channel_id=1, source_target_pairs={{0,16},{8,24},{16,0},{24,8},{1,17},{9,25},{17,1},{25,9},{2,18},{10... | collective-permute-start | bytes 12296 | tf_op jit(solution)/shard_map/ppermute | solution.py:29
  218.2 10.7 %collective-permute-start.11 = (bf16[1,64,512]{2,1,0:T(8,128)(2,1)}, bf16[1,64,512]{2,1,0:T(8,128)(2,1)S(1)}, u32[]{:S(2)}, u32[]{:S(2)}) collective-permute-start(bf16[1,64,512]{2,1,0:T(8,128)(2,1)} %get-tuple-element.142), channel_id=1, source_target_pairs={{0,2},{1,3},{2,0},{3,1},{4,6},{5,7},{6,4},{7,5},{8,10},{9,11},{10,... | collective-permute-start | bytes 196616 | tf_op jit(solution)/shard_map/ppermute | solution.py:36
  224.7 19.4 %collective-permute-start.25 = (bf16[4,128,512]{2,1,0:T(8,128)(2,1)}, bf16[4,128,512]{2,1,0:T(8,128)(2,1)S(1)}, u32[]{:S(2)}, u32[]{:S(2)}) collective-permute-start(bf16[4,128,512]{2,1,0:T(8,128)(2,1)} %get-tuple-element.151), channel_id=1, source_target_pairs={{0,1},{1,0},{2,3},{3,2},{4,5},{5,4},{6,7},{7,6},{8,9},{9,8},{10,11... | collective-permute-start | bytes 1572872 | tf_op jit(solution)/shard_map/ppermute | solution.py:36
  225.0 19.2 %collective-permute-start.26 = (bf16[4,128,512]{2,1,0:T(8,128)(2,1)}, bf16[4,128,512]{2,1,0:T(8,128)(2,1)S(1)}, u32[]{:S(2)}, u32[]{:S(2)}) collective-permute-start(bf16[4,128,512]{2,1,0:T(8,128)(2,1)} %get-tuple-element.152), channel_id=1, source_target_pairs={{0,16},{1,17},{2,18},{3,19},{4,20},{5,21},{6,22},{7,23},{8,24},{9,... | collective-permute-start | bytes 1572872 | tf_op jit(solution)/shard_map/ppermute | solution.py:36
  225.6 25.2 %collective-permute-start.27 = (bf16[4,128,512]{2,1,0:T(8,128)(2,1)}, bf16[4,128,512]{2,1,0:T(8,128)(2,1)S(1)}, u32[]{:S(2)}, u32[]{:S(2)}) collective-permute-start(bf16[4,128,512]{2,1,0:T(8,128)(2,1)} %get-tuple-element.153), channel_id=1, source_target_pairs={{0,17},{1,16},{2,19},{3,18},{4,21},{5,20},{6,23},{7,22},{8,25},{9,... | collective-permute-start | bytes 1572872 | tf_op jit(solution)/shard_map/ppermute | solution.py:36
  228.2 6.2 %collective-permute-start.12 = (bf16[1,64,512]{2,1,0:T(8,128)(2,1)S(1)}, bf16[1,64,512]{2,1,0:T(8,128)(2,1)S(1)}, u32[]{:S(2)}, u32[]{:S(2)}) collective-permute-start(bf16[1,64,512]{2,1,0:T(8,128)(2,1)S(1)} %copy-done.34), channel_id=1, source_target_pairs={{0,6},{1,7},{2,4},{3,5},{4,2},{5,3},{6,0},{7,1},{8,14},{9,15},{10,... | collective-permute-start | bytes 196616 | tf_op jit(solution)/shard_map/ppermute | solution.py:36
  228.9 8.2 %collective-permute-start.4 = (bf16[2,128,128]{2,1,0:T(8,128)(2,1)S(1)}, bf16[2,128,128]{2,1,0:T(8,128)(2,1)S(1)}, u32[]{:S(2)}, u32[]{:S(2)}) collective-permute-start(bf16[2,128,128]{2,1,0:T(8,128)(2,1)S(1)} %add_convert_fusion.2), channel_id=1, source_target_pairs={{0,4},{1,5},{2,6},{3,7},{4,0},{5,1},{6,2},{7,3},{8,12},{9,13},{10,... | collective-permute-start | bytes 196616 | tf_op jit(solution)/shard_map/ppermute | solution.py:29
  236.7 17.9 %collective-permute-start.15 = (bf16[1,64,512]{2,1,0:T(8,128)(2,1)}, bf16[1,64,512]{2,1,0:T(8,128)(2,1)S(1)}, u32[]{:S(2)}, u32[]{:S(2)}) collective-permute-start(bf16[1,64,512]{2,1,0:T(8,128)(2,1)} %shard_map.237), channel_id=1, source_target_pairs={{0,6},{1,7},{2,4},{3,5},{4,2},{5,3},{6,0},{7,1},{8,14},{9,15},{10,... | collective-permute-start | bytes 196616 | tf_op jit(solution)/shard_map/ppermute | solution.py:36
  237.1 18.0 %collective-permute-start.14 = (bf16[1,64,512]{2,1,0:T(8,128)(2,1)}, bf16[1,64,512]{2,1,0:T(8,128)(2,1)S(1)}, u32[]{:S(2)}, u32[]{:S(2)}) collective-permute-start(bf16[1,64,512]{2,1,0:T(8,128)(2,1)} %shard_map.237), channel_id=1, source_target_pairs={{0,2},{1,3},{2,0},{3,1},{4,6},{5,7},{6,4},{7,5},{8,10},{9,11},{10,... | collective-permute-start | bytes 196616 | tf_op jit(solution)/shard_map/ppermute | solution.py:36
  244.1 27.0 %collective-permute-start.5 = (bf16[512,512]{1,0:T(8,128)(2,1)}, bf16[512,512]{1,0:T(8,128)(2,1)S(1)}, u32[]{:S(2)}, u32[]{:S(2)}) collective-permute-start(bf16[512,512]{1,0:T(8,128)(2,1)} %get-tuple-element.122), channel_id=1, source_target_pairs={{0,8},{1,9},{2,10},{3,11},{4,12},{5,13},{6,14},{7,15},{8,0},{9,1},... | collective-permute-start | bytes 1572872 | tf_op jit(solution)/shard_map/ppermute | solution.py:36
  244.2 20.4 %collective-permute-start.13 = (bf16[1,64,512]{2,1,0:T(8,128)(2,1)S(1)}, bf16[1,64,512]{2,1,0:T(8,128)(2,1)S(1)}, u32[]{:S(2)}, u32[]{:S(2)}) collective-permute-start(bf16[1,64,512]{2,1,0:T(8,128)(2,1)S(1)} %copy-done.23), channel_id=1, source_target_pairs={{0,4},{1,5},{2,6},{3,7},{4,0},{5,1},{6,2},{7,3},{8,12},{9,13},{10,... | collective-permute-start | bytes 196616 | tf_op jit(solution)/shard_map/ppermute | solution.py:36
  254.0 11.8 %collective-permute-start.28 = (bf16[1,128,512]{2,1,0:T(8,128)(2,1)}, bf16[1,128,512]{2,1,0:T(8,128)(2,1)S(1)}, u32[]{:S(2)}, u32[]{:S(2)}) collective-permute-start(bf16[1,128,512]{2,1,0:T(8,128)(2,1)} %get-tuple-element.155), channel_id=1, source_target_pairs={{0,4},{1,5},{2,6},{3,7},{4,0},{5,1},{6,2},{7,3},{8,12},{9,13},{10,... | collective-permute-start | bytes 393224 | tf_op jit(solution)/shard_map/ppermute | solution.py:36
  254.6 11.5 %collective-permute-start.29 = (bf16[1,128,512]{2,1,0:T(8,128)(2,1)}, bf16[1,128,512]{2,1,0:T(8,128)(2,1)S(1)}, u32[]{:S(2)}, u32[]{:S(2)}) collective-permute-start(bf16[1,128,512]{2,1,0:T(8,128)(2,1)} %get-tuple-element.156), channel_id=1, source_target_pairs={{0,2},{1,3},{2,0},{3,1},{4,6},{5,7},{6,4},{7,5},{8,10},{9,11},{10,... | collective-permute-start | bytes 393224 | tf_op jit(solution)/shard_map/ppermute | solution.py:36
  255.1 12.4 %collective-permute-start.30 = (bf16[1,128,512]{2,1,0:T(8,128)(2,1)}, bf16[1,128,512]{2,1,0:T(8,128)(2,1)S(1)}, u32[]{:S(2)}, u32[]{:S(2)}) collective-permute-start(bf16[1,128,512]{2,1,0:T(8,128)(2,1)} %get-tuple-element.157), channel_id=1, source_target_pairs={{0,6},{1,7},{2,4},{3,5},{4,2},{5,3},{6,0},{7,1},{8,14},{9,15},{10,... | collective-permute-start | bytes 393224 | tf_op jit(solution)/shard_map/ppermute | solution.py:36
  264.6 29.2 %collective-permute-start.19 = (bf16[4,64,512]{2,1,0:T(8,128)(2,1)S(1)}, bf16[4,64,512]{2,1,0:T(8,128)(2,1)}, u32[]{:S(2)}, u32[]{:S(2)}) collective-permute-start(bf16[4,64,512]{2,1,0:T(8,128)(2,1)S(1)} %pad_maximum_fusion.1.refs_1_), channel_id=1, source_target_pairs={{0,8},{1,9},{2,10},{3,11},{4,12},{5,13},{6,14},{7,15},{8,0},{9,1},... | collective-permute-start | bytes 786440 | tf_op jit(solution)/shard_map/ppermute | solution.py:36
  265.8 10.3 %collective-permute-start.18 = (bf16[4,64,512]{2,1,0:T(8,128)(2,1)S(1)}, bf16[4,64,512]{2,1,0:T(8,128)(2,1)}, u32[]{:S(2)}, u32[]{:S(2)}) collective-permute-start(bf16[4,64,512]{2,1,0:T(8,128)(2,1)S(1)} %pad_maximum_fusion.1.refs_1_), channel_id=1, source_target_pairs={{0,17},{1,16},{2,19},{3,18},{4,21},{5,20},{6,23},{7,22},{8,25},{9,... | collective-permute-start | bytes 786440 | tf_op jit(solution)/shard_map/ppermute | solution.py:36
  266.1 17.5 %collective-permute-start.17 = (bf16[4,64,512]{2,1,0:T(8,128)(2,1)S(1)}, bf16[4,64,512]{2,1,0:T(8,128)(2,1)}, u32[]{:S(2)}, u32[]{:S(2)}) collective-permute-start(bf16[4,64,512]{2,1,0:T(8,128)(2,1)S(1)} %pad_maximum_fusion.1.refs_1_), channel_id=1, source_target_pairs={{0,16},{1,17},{2,18},{3,19},{4,20},{5,21},{6,22},{7,23},{8,24},{9,... | collective-permute-start | bytes 786440 | tf_op jit(solution)/shard_map/ppermute | solution.py:36
  267.6 27.8 %collective-permute-start.16 = (bf16[4,64,512]{2,1,0:T(8,128)(2,1)S(1)}, bf16[4,64,512]{2,1,0:T(8,128)(2,1)}, u32[]{:S(2)}, u32[]{:S(2)}) collective-permute-start(bf16[4,64,512]{2,1,0:T(8,128)(2,1)S(1)} %pad_maximum_fusion.1.refs_1_), channel_id=1, source_target_pairs={{0,1},{1,0},{2,3},{3,2},{4,5},{5,4},{6,7},{7,6},{8,9},{9,8},{10,11... | collective-permute-start | bytes 786440 | tf_op jit(solution)/shard_map/ppermute | solution.py:36
  271.1 12.6 %collective-permute-start.33 = (bf16[1,128,512]{2,1,0:T(8,128)(2,1)}, bf16[1,128,512]{2,1,0:T(8,128)(2,1)S(1)}, u32[]{:S(2)}, u32[]{:S(2)}) collective-permute-start(bf16[1,128,512]{2,1,0:T(8,128)(2,1)} %shard_map.241), channel_id=1, source_target_pairs={{0,6},{1,7},{2,4},{3,5},{4,2},{5,3},{6,0},{7,1},{8,14},{9,15},{10,... | collective-permute-start | bytes 393224 | tf_op jit(solution)/shard_map/ppermute | solution.py:36
  276.1 21.3 %collective-permute-start.22 = (bf16[4,64,512]{2,1,0:T(8,128)(2,1)}, bf16[4,64,512]{2,1,0:T(8,128)(2,1)}, u32[]{:S(2)}, u32[]{:S(2)}) collective-permute-start(bf16[4,64,512]{2,1,0:T(8,128)(2,1)} %collective-permute-done.18.refs_4_), channel_id=1, source_target_pairs={{0,8},{1,9},{2,10},{3,11},{4,12},{5,13},{6,14},{7,15},{8,0},{9,1},... | collective-permute-start | bytes 786440 | tf_op jit(solution)/shard_map/ppermute | solution.py:36
  283.6 7.1 %collective-permute-start.32 = (bf16[1,128,512]{2,1,0:T(8,128)(2,1)S(1)}, bf16[1,128,512]{2,1,0:T(8,128)(2,1)S(1)}, u32[]{:S(2)}, u32[]{:S(2)}) collective-permute-start(bf16[1,128,512]{2,1,0:T(8,128)(2,1)S(1)} %copy-done.17), channel_id=1, source_target_pairs={{0,2},{1,3},{2,0},{3,1},{4,6},{5,7},{6,4},{7,5},{8,10},{9,11},{10,... | collective-permute-start | bytes 393224 | tf_op jit(solution)/shard_map/ppermute | solution.py:36
  283.7 10.0 %collective-permute-start.31 = (bf16[1,128,512]{2,1,0:T(8,128)(2,1)S(1)}, bf16[1,128,512]{2,1,0:T(8,128)(2,1)S(1)}, u32[]{:S(2)}, u32[]{:S(2)}) collective-permute-start(bf16[1,128,512]{2,1,0:T(8,128)(2,1)S(1)} %copy-done.17), channel_id=1, source_target_pairs={{0,4},{1,5},{2,6},{3,7},{4,0},{5,1},{6,2},{7,3},{8,12},{9,13},{10,... | collective-permute-start | bytes 393224 | tf_op jit(solution)/shard_map/ppermute | solution.py:36
  285.7 48.6 %all-to-all-start.7 = ((f32[32,8,512]{2,1,0:T(8,128)}), f32[32,8,512]{2,1,0:T(8,128)S(1)}, u32[]{:S(2)}, u32[]{:S(2)}) async-start(f32[32,8,512]{2,1,0:T(8,128)} %broadcast_in_dim.19), calls=%async_computation.7 | async-start | bytes 1048576 | tf_op jit(solution)/shard_map/all_to_all | solution.py:1086
  290.7 6.9 %collective-permute-start.21 = (bf16[4,64,512]{2,1,0:T(8,128)(2,1)}, bf16[4,64,512]{2,1,0:T(8,128)(2,1)S(1)}, u32[]{:S(2)}, u32[]{:S(2)}) collective-permute-start(bf16[4,64,512]{2,1,0:T(8,128)(2,1)} %collective-permute-done.17.refs_3_), channel_id=1, source_target_pairs={{0,8},{1,9},{2,10},{3,11},{4,12},{5,13},{6,14},{7,15},{8,0},{9,1},... | collective-permute-start | bytes 786440 | tf_op jit(solution)/shard_map/ppermute | solution.py:36
  293.8 18.3 %collective-permute-start.36 = (bf16[4,128,512]{2,1,0:T(8,128)(2,1)S(1)}, bf16[4,128,512]{2,1,0:T(8,128)(2,1)S(1)}, u32[]{:S(2)}, u32[]{:S(2)}) collective-permute-start(bf16[4,128,512]{2,1,0:T(8,128)(2,1)S(1)} %pad_maximum_fusion.refs_1_), channel_id=1, source_target_pairs={{0,17},{1,16},{2,19},{3,18},{4,21},{5,20},{6,23},{7,22},{8,25},{9,... | collective-permute-start | bytes 1572872 | tf_op jit(solution)/shard_map/ppermute | solution.py:36
  293.9 28.7 %collective-permute-start.35 = (bf16[4,128,512]{2,1,0:T(8,128)(2,1)S(1)}, bf16[4,128,512]{2,1,0:T(8,128)(2,1)S(1)}, u32[]{:S(2)}, u32[]{:S(2)}) collective-permute-start(bf16[4,128,512]{2,1,0:T(8,128)(2,1)S(1)} %pad_maximum_fusion.refs_1_), channel_id=1, source_target_pairs={{0,16},{1,17},{2,18},{3,19},{4,20},{5,21},{6,22},{7,23},{8,24},{9,... | collective-permute-start | bytes 1572872 | tf_op jit(solution)/shard_map/ppermute | solution.py:36
  295.4 27.3 %collective-permute-start.34 = (bf16[4,128,512]{2,1,0:T(8,128)(2,1)S(1)}, bf16[4,128,512]{2,1,0:T(8,128)(2,1)S(1)}, u32[]{:S(2)}, u32[]{:S(2)}) collective-permute-start(bf16[4,128,512]{2,1,0:T(8,128)(2,1)S(1)} %pad_maximum_fusion.refs_1_), channel_id=1, source_target_pairs={{0,1},{1,0},{2,3},{3,2},{4,5},{5,4},{6,7},{7,6},{8,9},{9,8},{10,11... | collective-permute-start | bytes 1572872 | tf_op jit(solution)/shard_map/ppermute | solution.py:36
  297.3 35.8 %collective-permute-start.23 = (bf16[512,512]{1,0:T(8,128)(2,1)S(1)}, bf16[512,512]{1,0:T(8,128)(2,1)S(1)}, u32[]{:S(2)}, u32[]{:S(2)}) collective-permute-start(bf16[512,512]{1,0:T(8,128)(2,1)S(1)} %copy-done.1), channel_id=1, source_target_pairs={{0,16},{1,17},{2,18},{3,19},{4,20},{5,21},{6,22},{7,23},{8,24},{9,... | collective-permute-start | bytes 1572872 | tf_op jit(solution)/shard_map/ppermute | solution.py:36
  297.6 1.7 collective-permute-start.20
  299.4 37.4 %collective-permute-start.37 = (bf16[4,128,512]{2,1,0:T(8,128)(2,1)S(1)}, bf16[4,128,512]{2,1,0:T(8,128)(2,1)}, u32[]{:S(2)}, u32[]{:S(2)}) collective-permute-start(bf16[4,128,512]{2,1,0:T(8,128)(2,1)S(1)} %pad_maximum_fusion.refs_1_), channel_id=1, source_target_pairs={{0,8},{1,9},{2,10},{3,11},{4,12},{5,13},{6,14},{7,15},{8,0},{9,1},... | collective-permute-start | bytes 1572872 | tf_op jit(solution)/shard_map/ppermute | solution.py:36
  312.0 24.8 %collective-permute-start.40 = (bf16[4,128,512]{2,1,0:T(8,128)(2,1)S(1)}, bf16[4,128,512]{2,1,0:T(8,128)(2,1)}, u32[]{:S(2)}, u32[]{:S(2)}) collective-permute-start(bf16[4,128,512]{2,1,0:T(8,128)(2,1)S(1)} %collective-permute-done.36.refs_4_), channel_id=1, source_target_pairs={{0,8},{1,9},{2,10},{3,11},{4,12},{5,13},{6,14},{7,15},{8,0},{9,1},... | collective-permute-start | bytes 1572872 | tf_op jit(solution)/shard_map/ppermute | solution.py:36
  322.6 14.2 %collective-permute-start.39 = (bf16[4,128,512]{2,1,0:T(8,128)(2,1)S(1)}, bf16[4,128,512]{2,1,0:T(8,128)(2,1)}, u32[]{:S(2)}, u32[]{:S(2)}) collective-permute-start(bf16[4,128,512]{2,1,0:T(8,128)(2,1)S(1)} %collective-permute-done.35.refs_3_), channel_id=1, source_target_pairs={{0,8},{1,9},{2,10},{3,11},{4,12},{5,13},{6,14},{7,15},{8,0},{9,1},... | collective-permute-start | bytes 1572872 | tf_op jit(solution)/shard_map/ppermute | solution.py:36
  322.6 14.2 %collective-permute-start.38 = (bf16[4,128,512]{2,1,0:T(8,128)(2,1)S(1)}, bf16[4,128,512]{2,1,0:T(8,128)(2,1)}, u32[]{:S(2)}, u32[]{:S(2)}) collective-permute-start(bf16[4,128,512]{2,1,0:T(8,128)(2,1)S(1)} %collective-permute-done.34.refs_2_), channel_id=1, source_target_pairs={{0,8},{1,9},{2,10},{3,11},{4,12},{5,13},{6,14},{7,15},{8,0},{9,1},... | collective-permute-start | bytes 1572872 | tf_op jit(solution)/shard_map/ppermute | solution.py:36
  (35 other events, 358.9 us)
where the time goes:
time: 345 us; the launch traced here: 344 us
  Pallas kernels  138 us (40%)
  waiting for transfers between devices  87.5 us (25%)
  starting transfers between devices  62.7 us (18%)
  blocking collectives  30.7 us (9%)
  local copies, waits for them, and re-layouts  12.8 us (4%)
  other arithmetic  8.19 us (2%)
  between operations  4.25 us (1%)
    pallas_call x21, Pallas kernels, call(): pl.pallas_call(lambda *refs: kernel(*refs[:count], *refs[count + skip:]),...  107 us
    ppermute x36, waiting for transfers between devices, send(): lax.ppermute(array, ('dp', 'seq'), [(i, i ^ mask) for i in range(count)])  48.5 us
    all_to_all x1, blocking collectives, exchange(): return lax.all_to_all(chunks, 'seq', 0, 0, tiled=True)  30.7 us
    ppermute x36, starting transfers between devices, send(): lax.ppermute(array, ('dp', 'seq'), [(i, i ^ mask) for i in range(count)])  30.4 us
    pallas_call x1, Pallas kernels, feed(): pl.pallas_call(lambda *refs: feed_kernel(len(att), *refs), grid_spec=pltp...  25.8 us
    all_to_all x6, waiting for transfers between devices, exchange(): return lax.all_to_all(chunks, 'seq', 0, 0, tiled=True)  23.9 us
    all_to_all x6, starting transfers between devices, exchange(): return lax.all_to_all(chunks, 'seq', 0, 0, tiled=True)  23.7 us
    ppermute x5, waiting for transfers between devices, swap(): lax.ppermute(array, axis, [(i, i ^ bit) for i in range(lax.axis_size(axis...  15.1 us
  transfers between devices with their start and end apart: 48, of which 18 were waited for; matrix products, arithmetic and copies ran while one was open for 3% of the time, Pallas kernels for 23%

commit v1 on v0

--- a/solution.py
+++ b/solution.py
@@ -29,16 +29,24 @@
     return lax.ppermute(array, axis, [(i, i ^ bit) for i in range(lax.axis_size(axis))])
 
 
-def send(array, dp_bits, seq_bits):
+def send(array, *to):
     seq = lax.axis_size("seq")
-    mask = dp_bits * seq + seq_bits
-    count = lax.axis_size("dp") * seq
-    return lax.ppermute(array, ("dp", "seq"), [(i, i ^ mask) for i in range(count)])
+    pairs = []
+    for i in range(lax.axis_size("dp") * seq):
+        dp_bits, seq_bits = to[-(i // seq % 2)]
+        pairs.append((i, i ^ (dp_bits * seq + seq_bits)))
+    return lax.ppermute(array, ("dp", "seq"), pairs)
 
 
 CORE = (1, 0)
-PLANE = ((0, 1), (2, 0), (2, 1))
+X, Y = (2, 0), (0, 1)
 LINE = ((0, 4), (0, 2), (0, 6))
+
+
+def spot(index, place, core):
+    at = (index ^ place) % 16
+    turned = at % 4 + at // 4 % 2 * 8 + at // 8 * 4
+    return jnp.where(core == 0, at, turned)
 
 
 def add_kernel(count, *refs):
@@ -49,35 +57,48 @@
         total = refs[0][part].astype(F32)
         for ref in refs[1:count]:
             total = total + ref[part].astype(F32)
-        out_ref[...] = total.astype(BF16)
-
-
-def add_split(arrays, pieces, after=()):
+        out_ref[...] = total.astype(out_ref.dtype)
+
+
+def add_split(arrays, pieces, dtype=BF16, **more):
     shape = arrays[0].shape
-    out = like((shape[0] // pieces,) + shape[1:], BF16)
+    out = like((shape[0] // pieces,) + shape[1:], dtype)
     kernel = lambda *refs: add_kernel(len(arrays), *refs)
-    return list(call(kernel, [out] * pieces, arrays, after=after))
-
-
-def sum_stages(keep, give):
-    got = send(give, *CORE)
-    own = add_split([keep, got], 4)
+    return list(call(kernel, [out] * pieces, arrays, **more))
+
+
+def join_kernel(*refs):
+    each = refs[0].shape[0]
+    for n, ref in enumerate(refs[:-1]):
+        refs[-1][n * each : (n + 1) * each] = ref[...]
+
+
+def join(arrays, **more):
+    shape = arrays[0].shape
+    out = like((len(arrays) * shape[0],) + shape[1:], BF16)
+    return list(call(join_kernel, [out], arrays, **more))
+
+
+def sum_stages(keep, give, more):
+    own = add_split([keep, send(give, CORE)], 2)
     yield own
-    got = [send(g, *to) for g, to in zip(own[1:], PLANE)]
-    own = add_split([own[0]] + got, 4)
+    own = add_split([own[0], send(own[1], X, Y)], 2)
     yield own
-    got = [send(g, *to) for g, to in zip(own[1:], LINE)]
-    own = add_split([own[0]] + got, 1)
+    own = add_split([own[0], send(own[1], Y, X)], 4, **more.get("second", {}))
+    yield own
+    got = [send(g, to) for g, to in zip(own[1:], LINE)]
+    own = add_split([own[0]] + got, 1, **more.get("line", {}))
     for bit in bits(lax.axis_size("seq"))[3:]:
-        own = add_split([own[0], send(own[0], 0, bit)], 1)
+        own = add_split([own[0], send(own[0], (0, bit))], 1) + own[1:]
     yield own
-    got = [send(own[0], *to) for to in LINE]
-    quarter = jnp.concatenate(own + got, axis=0)
-    yield [quarter]
-    got = [send(quarter, *to) for to in PLANE]
-    quarters = [quarter] + got
-    yield quarters
-    yield quarters + [send(q, *CORE) for q in quarters]
+    got = [send(own[0], to) for to in LINE]
+    quarter, *passed = join(own[:1] + got, **more.get("join", {}))
+    yield [quarter, *passed]
+    (half,) = join([quarter, send(quarter, Y, X)], **more.get("half", {}))
+    yield [half]
+    halves = [half, send(half, X, Y)]
+    yield halves
+    yield halves + [send(h, CORE) for h in halves]
 
 
 def exchange(chunks):
@@ -109,25 +130,41 @@
 
 
 def call(
-    kernel, outs, args, specs=None, scratch=(), flops=0, out_specs=None, grid=(1,), after=(), **more
+    kernel,
+    outs,
+    args,
+    specs=None,
+    scratch=(),
+    flops=0,
+    out_specs=None,
+    grid=(1,),
+    after=(),
+    passing=(),
 ):
     specs = specs or [whole(a) for a in args]
     moved = sum(math.prod(o.shape) * o.dtype.itemsize for o in outs)
     moved += sum(math.prod(a.shape) * a.dtype.itemsize for a in args)
-    count, skip = len(args), len(after)
+    count, made = len(args), len(outs)
+    extra = [*passing, *after]
+    skip, pas = len(extra), len(passing)
+    anywhere = pl.BlockSpec(memory_space=pl.ANY)
     return pl.pallas_call(
-        lambda *refs: kernel(*refs[:count], *refs[count + skip :]),
-        out_shape=outs,
+        lambda *refs: kernel(
+            *refs[:count],
+            *refs[count + skip : count + skip + made],
+            *refs[count + skip + made + pas :],
+        ),
+        out_shape=list(outs) + [like(p.shape, p.dtype) for p in passing],
         grid=grid,
-        in_specs=list(specs) + [pl.BlockSpec(memory_space=pl.ANY)] * skip,
-        out_specs=out_specs or [whole(o) for o in outs],
+        in_specs=list(specs) + [anywhere] * skip,
+        out_specs=list(out_specs or [whole(o) for o in outs]) + [anywhere] * pas,
         scratch_shapes=list(scratch),
+        input_output_aliases={count + k: made + k for k in range(pas)},
         compiler_params=pltpu.CompilerParams(vmem_limit_bytes=VMEM_BYTES),
         cost_estimate=pl.CostEstimate(
             flops=int(flops * COST), bytes_accessed=int(moved * COST), transcendentals=0
         ),
-        **more,
-    )(*args, *after)
+    )(*args, *extra)
 
 
 SCALAR = pl.BlockSpec(memory_space=pltpu.SMEM)
@@ -293,9 +330,12 @@
     proj_ref,
     steps_ref,
     plan_ref,
+    split_ref,
     d_summary_ref,
-    grad_ref,
+    keep_ref,
+    give_ref,
     buffer,
+    whole_grad,
 ):
     place = place_ref[0, 0]
     seqs = plan_ref.shape[0]
@@ -326,7 +366,12 @@
         d_summary_ref[s] = buffer[pl.ds(first, blocks), :]
         here = dot(summary, d_proj, 0, 0)
         grad_sort = here if grad_sort is None else grad_sort + here
-    grad_ref[...] = grad_sort.astype(grad_ref.dtype)
+    half = keep_ref.shape[0]
+    whole_grad[...] = grad_sort
+    keep_ref[...] = whole_grad[pl.ds(pl.multiple_of(split_ref[0] * half, half), half)].astype(BF16)
+    give_ref[...] = whole_grad[
+        pl.ds(pl.multiple_of((1 - split_ref[0]) * half, half), half)
+    ].astype(BF16)
 
 
 def spread_row(ref, t):
@@ -341,9 +386,10 @@
         mixed_ref[:, t] = mixed.reshape(parts, blocks, width)
 
 
-def mix(low, spread, index, width):
+def mix(low, spread, index, width, after=()):
     shape = chunk_shape(spread.shape[0], spread.shape[2], width)
-    return call(mix_kernel, [like(shape, BF16)], [low, spread], [nth(low, index), whole(spread)])[0]
+    specs = [nth(low, index), whole(spread)]
+    return call(mix_kernel, [like(shape, BF16)], [low, spread], specs, after=after)[0]
 
 
 def unmix_kernel(low_ref, *refs):
@@ -619,7 +665,7 @@
     for side, ref in ((core, keep_ref), (1 - core, give_ref)):
         for j in range(blocks):
             part = pl.ds(pl.multiple_of((side * blocks + j) * rows, rows), rows)
-            at = j ^ (place % blocks)
+            at = spot(j, place, side)
             for n in range(4):
                 ref[at, n * rows : (n + 1) * rows] = buffer[n, part].astype(BF16)
 
@@ -642,8 +688,10 @@
 def end_blocks(split_ref, refs):
     each = refs[0].shape[0]
     for n, ref in enumerate(refs):
+        core = split_ref[0] if n < 2 else 1 - split_ref[0]
         for r in range(each):
-            yield ref[r], (n * each + r) ^ split_ref[1]
+            index = core * 16 + spot(0, n % 2 * each + r, core)
+            yield ref[r], index ^ (split_ref[1] % 16)
 
 
 def late_end_kernel(split_ref, *refs):
@@ -655,13 +703,14 @@
             out_ref[part] = block[n * rows : (n + 1) * rows].astype(F32)
 
 
-def late_end(split, parts):
+def late_end(split, parts, after=()):
     width = parts[0].shape[2]
     return call(
         late_end_kernel,
         [like((width, width), F32)] * 4,
         [split, *parts],
         [SCALAR] + [whole(p) for p in parts],
+        after=after,
     )
 
 
@@ -759,7 +808,8 @@
         @pl.when(step // 2 * 2 == first)
         def _():
             for j in range(count):
-                at = ((step % 2) * count + j) ^ (split_ref[1] % blocks)
+                core = split_ref[0] if first else 1 - split_ref[0]
+                at = spot((step % 2) * count + j, split_ref[1], core)
                 for n in range(2):
                     ref[at, n * block : (n + 1) * block] = grads[n][j * block : (j + 1) * block]
 
@@ -901,6 +951,12 @@
     )
 
 
+def sort_end_kernel(split_ref, half_ref, other_ref, out_ref):
+    half = half_ref.shape[0]
+    for core, ref in ((split_ref[0], half_ref), (1 - split_ref[0], other_ref)):
+        out_ref[pl.ds(pl.multiple_of(core * half, half), half)] = ref[...].astype(F32)
+
+
 def plan_plain(sort_scale, summary_all, real, w_sort):
     def plan_of(logits):
         plan = jnp.where(real, logits, NEG)
@@ -953,6 +1009,11 @@
     place = place.astype(jnp.int32).reshape(1, 1)
     split = places()
 
+    segments = segment_ids.reshape(seqs, blocks, BLOCK)
+    allowed = (segments.transpose(0, 2, 1)[:, :, :, None] == segments[:, None]).astype(F32)
+    allowed = allowed.reshape(seqs, BLOCK, span)
+
+
     hidden, *rows = enter(inputs, gain_one, real_block, seq_size)
     spread = [exchange(r) for r in rows]
     q, k, v, qt, kt, vt = project(hidden, w_query, w_key, w_value)
@@ -983,13 +1044,9 @@
     for bit in bits(dp_size):
         total_blocks = total_blocks + swap(total_blocks, "dp", bit)
 
-    segments = segment_ids.reshape(seqs, blocks, BLOCK)
-    allowed = (segments.transpose(0, 2, 1)[:, :, :, None] == segments[:, None]).astype(F32)
-    allowed = allowed.reshape(seqs, BLOCK, span)
-
     att, kept = [], []
     for s in range(seqs):
-        part = mix(low, spread[s], s, width)
+        part = mix(low, spread[s], s, width, [allowed, split, gain_two, total_blocks] if s else ())
         here, *rest = attend(exchange(part), allowed, w_key, w_value, k, qt, vt, s)
         att.append(here)
         kept.append(rest)
@@ -1007,29 +1064,33 @@
     )
     d_resid = d_resid.reshape(inputs.shape)
     d_att = d_att.reshape(inputs.shape)
-    stages = sum_stages(keep, give)
-    next(stages)
+    more = {}
+    stages = sum_stages(keep, give, more)
+    summed = next(stages)
     grads, d_mixed = [], []
     chunks = chunk_shape(seq_size, blocks, width)
     for s in range(seqs):
-        sent, *here = attend_back(d_att, q, v, kt, kept[s][1:], w_key, w_value, chunks, s)
+        after = summed[:1] if s else ()
+        sent, *here = attend_back(d_att, q, v, kt, kept[s][1:], w_key, w_value, chunks, s, after)
         grads.append(here)
-        if s == 0:
-            next(stages)
         d_mixed.append(exchange(sent))
     parts = late(
         split, hidden, grad_output, [[kept[s][0], *grads[s]] for s in range(seqs)]
     )
+    plane = next(stages)
+    d_hidden = d_hidden_of(w_query, w_key, w_value, [g[:3] for g in grads])
+    late_more = {}
+    late_stages = sum_stages(*parts, late_more)
+    d_rows, d_prob = unmix(low, spread, d_mixed, plane[:1])
+    heard = sum_seq(d_prob)
+    more["line"] = dict(passing=[d_rows])
     next(stages)
-    d_hidden = d_hidden_of(w_query, w_key, w_value, [g[:3] for g in grads])
-    late_stages = sum_stages(*parts)
-    d_rows, d_prob = unmix(low, spread, d_mixed)
-    heard = sum_seq(d_prob)
+    _, d_rows = next(stages)
     d_rows = exchange(d_rows)
     *_, last = stages
     grad_out, grad_in = feed_end(split, last)
-    *_, last = late_stages
-    grad_query, grad_key, grad_value, grad_output = late_end(split, last)
+    next(late_stages)
+    late2 = next(late_stages)
 
     if small_plan:
         args = [
@@ -1042,16 +1103,16 @@
             steps,
             plan,
         ]
-        outs = [like((seqs, blocks, width), F32), like((width, width), BF16)]
-        d_summary, grad_sort = pl.pallas_call(
+        half = like((width // 2, width), BF16)
+        outs = [like((seqs, blocks, width), F32), half, half]
+        d_summary, sort_keep, sort_give = call(
             lambda *refs: plan_back_kernel(sort_scale, *refs),
-            out_shape=outs,
-            grid=(1,),
-            in_specs=[whole(total_blocks), SCALAR] + [whole(a) for a in args[2:]],
-            out_specs=[whole(o) for o in outs],
-            scratch_shapes=[pltpu.VMEM((count, width), F32)],
-            compiler_params=pltpu.CompilerParams(vmem_limit_bytes=VMEM_BYTES),
-        )(*args)
+            outs,
+            args + [split],
+            [whole(total_blocks), SCALAR] + [whole(a) for a in args[2:]] + [SCALAR],
+            [pltpu.VMEM((count, width), F32), pltpu.VMEM((width, width), F32)],
+            after=[late2[0], d_hidden],
+        )
     else:
         d_prob = heard.astype(F32)
         d_plan = prob * d_prob - (
@@ -1068,13 +1129,27 @@
             "sij,sid->sjd", d_logits, proj, preferred_element_type=F32
         ) + jnp.einsum("sie,de->sid", d_proj, w_sort, preferred_element_type=F32)
         d_summary = lax.dynamic_slice_in_dim(d_summary, first_block, blocks, 1)
-
-    grad_sort = grad_sort.astype(BF16)
-    grad_sort = add(grad_sort, send(grad_sort, *CORE))
+        sides = grad_sort.astype(BF16).reshape(2, width // 2, width)
+        sort_keep = lax.dynamic_index_in_dim(sides, split[0], 0, False)
+        sort_give = lax.dynamic_index_in_dim(sides, 1 - split[0], 0, False)
+
+    (sort_half,) = add_split([sort_keep, send(sort_give, CORE)], 1)
+    late_more["second"] = dict(after=[sort_half])
+    next(late_stages)
+    (sort_half,) = add_split([sort_half, send(sort_half, X)], 1)
+    late_more["line"] = dict(after=[sort_half])
+    sort_other = send(sort_half, CORE)
     input_grad, gains = leave(
-        inputs, gain_one, d_hidden, d_rows, d_summary, d_resid, (grad_sort,)
-    )
-    grad_sort = grad_sort.astype(F32) + send(grad_sort, 2, 0).astype(F32)
+        inputs, gain_one, d_hidden, d_rows, d_summary, d_resid, ()
+    )
+    *_, last = late_stages
+    grad_query, grad_key, grad_value, grad_output = late_end(split, last)
+    (grad_sort,) = call(
+        sort_end_kernel,
+        [like((width, width), F32)],
+        [split, sort_half, sort_other],
+        [SCALAR, whole(sort_half), whole(sort_other)],
+    )
     small = jnp.concatenate(
         [
             jnp.sum(gains[:, :1], axis=0),

time: 345 us -> 333 us (0.965)
  waiting for transfers between devices: 87.5 us -> 39.8 us
  Pallas kernels: 138 us -> 156 us
  starting transfers between devices: 62.7 us -> 72.2 us
  local copies, waits for them, and re-layouts: 12.8 us -> 22.2 us
    ppermute x36 -> x29, waiting for transfers between devices: 48.5 us -> 22.1 us  [send(): return lax.ppermute(array, ('dp', 'seq'), pairs)]
    pallas_call x22 -> x31, Pallas kernels: 112 us -> 130 us  [call(): pl.pallas_call(lambda *refs: kernel(*refs[:count], *refs[count + skip:cou...]
    all_to_all x6, waiting for transfers between devices: 23.9 us -> 10.3 us  [exchange(): return lax.all_to_all(chunks, 'seq', 0, 0, tiled=True)]
    unnamed x71 -> x79, local copies, waits for them, and re-layouts: 6.83 us -> 16.2 us
    ppermute x5, waiting for transfers between devices: 15.1 us -> 7.43 us  [swap(): lax.ppermute(array, axis, [(i, i ^ bit) for i in range(lax.axis_size(axis...]
    ppermute x5, starting transfers between devices: 4.97 us -> 8.69 us  [swap(): lax.ppermute(array, axis, [(i, i ^ bit) for i in range(lax.axis_size(axis...]
    ppermute x36 -> x29, starting transfers between devices: 30.4 us -> 33.2 us  [send(): return lax.ppermute(array, ('dp', 'seq'), pairs)]
  transfers between devices with their start and end apart: 48 -> 41, of which waited for: 18 -> 18; matrix products, arithmetic and copies ran while one was open for 3% -> 3% of each run, Pallas kernels for 23% -> 35%
where the time goes in v1:
time: 333 us; the launch traced here: 331 us
  Pallas kernels  156 us (47%)
  starting transfers between devices  72.2 us (22%)
  waiting for transfers between devices  39.8 us (12%)
  blocking collectives  30.7 us (9%)
  local copies, waits for them, and re-layouts  22.2 us (7%)
  other arithmetic  5.96 us (2%)
  between operations  4.09 us (1%)
    pallas_call x31, Pallas kernels, call(): pl.pallas_call(lambda *refs: kernel(*refs[:count], *refs[count + skip:cou...  130 us
    ppermute x29, starting transfers between devices, send(): return lax.ppermute(array, ('dp', 'seq'), pairs)  33.2 us
    all_to_all x1, blocking collectives, exchange(): return lax.all_to_all(chunks, 'seq', 0, 0, tiled=True)  30.7 us
    all_to_all x6, starting transfers between devices, exchange(): return lax.all_to_all(chunks, 'seq', 0, 0, tiled=True)  26.3 us
    pallas_call x1, Pallas kernels, feed(): pl.pallas_call(lambda *refs: feed_kernel(len(att), *refs), grid_spec=pltp...  26.2 us
    ppermute x29, waiting for transfers between devices, send(): return lax.ppermute(array, ('dp', 'seq'), pairs)  22.1 us
    unnamed x79, local copies, waits for them, and re-layouts  16.2 us
    all_to_all x6, waiting for transfers between devices, exchange(): return lax.all_to_all(chunks, 'seq', 0, 0, tiled=True)  10.3 us
  transfers between devices with their start and end apart: 41, of which 18 were waited for; matrix products, arithmetic and copies ran while one was open for 3% of the time, Pallas kernels for 35%

profile of v1, /device:TPU:0, one launch (start us, length us, event | category | flops | bytes accessed | tf_op | source)
XLA Modules:
  0.0 331.2 jit_solution(14616480504952199722)
XLA Ops:
  3.4 4.7 %shard_map.220 = (bf16[2,512,512]{2,1,0:T(8,128)(2,1)}, bf16[8,7,16,512]{3,2,1,0:T(8,128)(2,1)}, bf16[8,4,16,512]{3,2,1,0:T(8,128)(2,1)}) custom-call(bf16[2,512,512]{2,1,0:T(8,128)(2,1)} %refs_0_.5, f32[1,512]{1,0:T(1,128)} %bitcast.29, bf16[16,512]{1,0:T(8,128)(2,1)} %bitcast.26), custom_call_target="tpu_custom_call" | custom-call | bytes 10672128 | tf_op jit(solution)/shard_map/pallas_call | solution.py:151
  8.1 30.7 %all_to_all.40.refs_0_.refs_1_.refs_3_ = bf16[8,7,16,512]{3,2,1,0:T(8,128)(2,1)} all-to-all(bf16[8,7,16,512]{3,2,1,0:T(8,128)(2,1)} %get-tuple-element.89), channel_id=1, replica_groups=mesh['dp'=4,'seq'=8] {'seq'}, dimensions={0} | all-to-all | bytes 1835008 | tf_op jit(solution)/shard_map/all_to_all | solution.py:105
  38.8 3.5 %all-to-all-start.2 = ((bf16[8,4,16,512]{3,2,1,0:T(8,128)(2,1)}), bf16[8,4,16,512]{3,2,1,0:T(8,128)(2,1)S(1)}, u32[]{:S(2)}, u32[]{:S(2)}) async-start(bf16[8,4,16,512]{3,2,1,0:T(8,128)(2,1)} %get-tuple-element.97), calls=%async_computation.2 | async-start | bytes 1048576 | tf_op jit(solution)/shard_map/all_to_all | solution.py:105
  42.3 4.9 %shard_map.221 = (bf16[2,512,512]{2,1,0:T(8,128)(2,1)}, bf16[2,512,512]{2,1,0:T(8,128)(2,1)}, bf16[2,512,512]{2,1,0:T(8,128)(2,1)}, bf16[2,512,512]{2,1,0:T(8,12...) custom-call(bf16[2,512,512]{2,1,0:T(8,128)(2,1)} %get-tuple-element.90.refs_0_.refs_1_, ...), custom_call_target="tpu_custom_call" | custom-call | flops 4831838208 | bytes 26738688 | tf_op jit(solution)/shard_map/pallas_call | solution.py:151
  47.3 5.3 %shard_map.222 = (bf16[2,128,512]{2,1,0:T(8,128)(2,1)}, f32[16,2,128,128]{3,2,1,0:T(8,128)}, f32[2,128,128]{2,1,0:T(8,128)}, bf16[2,128,128]{2,1,0:T(8,128)(2,1)}, f32[8,128]{1,0:T(8,128)}, /*index=5*/f32[8,128]{1,0:T(8,128)}) custom-call(bf16[8,7,16,512]{3,2,1,0:T(8,128)(2,1)} %all_to_all.40.refs_0_.refs_1_.refs_3_, bf16[512,512]{1,0:T(8,128)(2,1)} %refs_4_.3, ...), custom_call_target="tpu_custom_call" | custom-call | bytes 12017664 | tf_op jit(solution)/shard_map/pallas_call | solution.py:151
  52.6 2.3 shard_map.223
  56.4 4.4 %all-to-all-start.1 = ((bf16[8,4,16,512]{3,2,1,0:T(8,128)(2,1)}), bf16[8,4,16,512]{3,2,1,0:T(8,128)(2,1)S(1)}, u32[]{:S(2)}, u32[]{:S(2)}) async-start(bf16[8,4,16,512]{3,2,1,0:T(8,128)(2,1)} %shard_map.223), calls=%async_computation.1 | async-start | bytes 1048576 | tf_op jit(solution)/shard_map/all_to_all | solution.py:105
  67.5 2.2 shard_map.225
  69.7 4.9 %all-to-all-done.1.refs_0_ = bf16[8,4,16,512]{3,2,1,0:T(8,128)(2,1)S(1)} async-done(((bf16[8,4,16,512]{3,2,1,0:T(8,128)(2,1)}), bf16[8,4,16,512]{3,2,1,0:T(8,128)(2,1)S(1)}, u32[]{:S(2)}, u32[]{:S(2)}) %all-to-all-start.1) | async-done | bytes 524320 | tf_op jit(solution)/shard_map/all_to_all | solution.py:105
  74.5 3.7 %all-to-all-start.3 = ((bf16[8,4,16,512]{3,2,1,0:T(8,128)(2,1)}), bf16[8,4,16,512]{3,2,1,0:T(8,128)(2,1)S(1)}, u32[]{:S(2)}, u32[]{:S(2)}) async-start(bf16[8,4,16,512]{3,2,1,0:T(8,128)(2,1)} %shard_map.225), calls=%async_computation.3 | async-start | bytes 1048576 | tf_op jit(solution)/shard_map/all_to_all | solution.py:105
  78.2 9.8 %shard_map.224 = (bf16[512,512]{1,0:T(8,128)(2,1)}, bf16[512,512]{1,0:T(8,128)(2,1)}, bf16[512,512]{1,0:T(8,128)(2,1)}, bf16[512,512]{1,0:T(8,128)(2,1)}, f32[16,64,256]{2,1,0:T(8,128)}) custom-call(bf16[8,4,16,512]{3,2,1,0:T(8,128)(2,1)} %copy-done.12, f32[2,32,512]{2,1,0:T(8,128)} %compare_convert_fusion.refs_1_.refs_2_, bf16[512,512]{1,0:T(8,128)(2,1)} %refs_1_.5, ...), custom_call_target="tpu_custom_call" | custom-call | flops 3221225472 | bytes 23986176 | tf_op jit(solution)/shard_map/pallas_call | solution.py:151
  88.0 3.9 %all-to-all-done.3.refs_0_ = bf16[8,4,16,512]{3,2,1,0:T(8,128)(2,1)S(1)} async-done(((bf16[8,4,16,512]{3,2,1,0:T(8,128)(2,1)}), bf16[8,4,16,512]{3,2,1,0:T(8,128)(2,1)S(1)}, u32[]{:S(2)}, u32[]{:S(2)}) %all-to-all-start.3) | async-done | bytes 524320 | tf_op jit(solution)/shard_map/all_to_all | solution.py:105
  92.7 9.8 %shard_map.226 = (bf16[512,512]{1,0:T(8,128)(2,1)}, bf16[512,512]{1,0:T(8,128)(2,1)}, bf16[512,512]{1,0:T(8,128)(2,1)}, bf16[512,512]{1,0:T(8,128)(2,1)}, f32[16,64,256]{2,1,0:T(8,128)}) custom-call(bf16[8,4,16,512]{3,2,1,0:T(8,128)(2,1)} %copy-done.14, f32[2,32,512]{2,1,0:T(8,128)} %compare_convert_fusion.refs_1_.refs_2_, bf16[512,512]{1,0:T(8,128)(2,1)} %refs_1_.5, ...), custom_call_target="tpu_custom_call" | custom-call | flops 3221225472 | bytes 23986176 | tf_op jit(solution)/shard_map/pallas_call | solution.py:151
  102.6 26.2 %shard_map.227 = (bf16[1024,512]{1,0:T(8,128)(2,1)}, bf16[16,128,512]{2,1,0:T(8,128)(2,1)}, bf16[16,128,512]{2,1,0:T(8,128)(2,1)}, bf16[512,512]{1,0:T(8,128)(2,...) custom-call(s32[2]{0:T(128)} %pad_add_fusion.refs_3_.refs_0_.refs_8_, ...), custom_call_target="tpu_custom_call" | custom-call | flops 38654705664 | bytes 75497472 | tf_op jit(solution)/shard_map/pallas_call | solution.py:857
  128.9 11.1 %shard_map.228 = (bf16[8,4,16,512]{3,2,1,0:T(8,128)(2,1)}, bf16[512,512]{1,0:T(8,128)(2,1)}, bf16[512,512]{1,0:T(8,128)(2,1)}, bf16[512,512]{1,0:T(8,128)(2,1)},...) custom-call(bf16[2,512,512]{2,1,0:T(8,128)(2,1)} %bitcast.38, ...), custom_call_target="tpu_custom_call" | custom-call | flops 4831838208 | bytes 31457280 | tf_op jit(solution)/shard_map/pallas_call | solution.py:151
  140.0 3.6 %all-to-all-start.4 = ((bf16[8,4,16,512]{3,2,1,0:T(8,128)(2,1)}), bf16[8,4,16,512]{3,2,1,0:T(8,128)(2,1)S(1)}, u32[]{:S(2)}, u32[]{:S(2)}) async-start(bf16[8,4,16,512]{3,2,1,0:T(8,128)(2,1)} %get-tuple-element.126), calls=%async_computation.4 | async-start | bytes 1048576 | tf_op jit(solution)/shard_map/all_to_all | solution.py:105
  144.9 3.8 %shard_map.229 = (bf16[8,128,512]{2,1,0:T(8,128)(2,1)}, bf16[8,128,512]{2,1,0:T(8,128)(2,1)}) custom-call(bf16[16,128,512]{2,1,0:T(8,128)(2,1)} %get-tuple-element.113.refs_0_, bf16[16,128,512]{2,1,0:T(8,128)(2,1)} %copy-done.5), custom_call_target="tpu_custom_call" | custom-call | bytes 18874368 | tf_op jit(solution)/shard_map/pallas_call | solution.py:151
  150.3 10.9 %shard_map.230 = (bf16[8,4,16,512]{3,2,1,0:T(8,128)(2,1)}, bf16[512,512]{1,0:T(8,128)(2,1)}, bf16[512,512]{1,0:T(8,128)(2,1)}, bf16[512,512]{1,0:T(8,128)(2,1)},...) custom-call(bf16[2,512,512]{2,1,0:T(8,128)(2,1)} %bitcast.39, ...), custom_call_target="tpu_custom_call" | custom-call | flops 4831838208 | bytes 31457280 | tf_op jit(solution)/shard_map/pallas_call | solution.py:151
  161.2 6.0 %all-to-all-start.5 = ((bf16[8,4,16,512]{3,2,1,0:T(8,128)(2,1)}), bf16[8,4,16,512]{3,2,1,0:T(8,128)(2,1)S(1)}, u32[]{:S(2)}, u32[]{:S(2)}) async-start(bf16[8,4,16,512]{3,2,1,0:T(8,128)(2,1)} %get-tuple-element.127), calls=%async_computation.5 | async-start | bytes 1048576 | tf_op jit(solution)/shard_map/all_to_all | solution.py:105
  167.2 7.7 %shard_map.236 = (bf16[16,64,512]{2,1,0:T(8,128)(2,1)}, bf16[16,64,512]{2,1,0:T(8,128)(2,1)}) custom-call(s32[2]{0:T(128)} %pad_add_fusion.refs_3_.refs_0_.refs_8_, bf16[2,512,512]{2,1,0:T(8,128)(2,1)} %get-tuple-element.90.refs_0_.refs_1_, bf16[512,512]{1,0:T(8,128)(2,1)} %get-tuple-element.134.refs_2_, bf16[512,512]{1,0:T(8,128)(2,1)} %get-tuple-element.135.refs_3_, ...), custom_call_target="tpu_custom_call" | custom-call | flops 8053063680 | bytes 29884440 | tf_op jit(solution)/shard_map/pallas_call | solution.py:151
  174.9 2.6 shard_map.232
  177.6 2.0 collective-permute-start.4
  179.6 7.4 %collective-permute-done.4.refs_1_ = bf16[4,128,512]{2,1,0:T(8,128)(2,1)S(1)} collective-permute-done((bf16[4,128,512]{2,1,0:T(8,128)(2,1)}, bf16[4,128,512]{2,1,0:T(8,128)(2,1)S(1)}, u32[]{:S(2)}, u32[]{:S(2)}) %collective-permute-start.4) | collective-permute-done | bytes 524320 | tf_op jit(solution)/shard_map/ppermute | solution.py:38
  187.8 2.0 shard_map.233
  189.8 2.9 collective-permute-start.5
  195.0 3.4 %shard_map.234 = (bf16[8,8,16,512]{3,2,1,0:T(8,128)(2,1)}, bf16[2,128,128]{2,1,0:T(8,128)(2,1)}) custom-call(bf16[2,128,128]{2,1,0:T(8,128)(2,1)} %get-tuple-element.92.refs_0_, bf16[8,7,16,512]{3,2,1,0:T(8,128)(2,1)} %all_to_all.40.refs_0_.refs_1_.refs_3_, bf16[8,4,16,512]{3,2,1,0:T(8,128)(2,1)} %copy-done, bf16[8,4,16,512]{3,2,1,0:T(8,128)(2,1)} %copy-done.6, ...), custom_call_target="tpu_custom_call" | custom-call | bytes 11010048 | tf_op jit(solution)/shard_map/pallas_call | solution.py:151
  205.6 2.4 collective-permute-start.29
  208.0 2.3 collective-permute-start.28
  210.3 5.1 %all-to-all-start.6 = ((bf16[8,8,16,512]{3,2,1,0:T(8,128)(2,1)}), bf16[8,8,16,512]{3,2,1,0:T(8,128)(2,1)S(1)}, u32[]{:S(2)}, u32[]{:S(2)}) async-start(bf16[8,8,16,512]{3,2,1,0:T(8,128)(2,1)} %get-tuple-element.129), calls=%async_computation.6 | async-start | bytes 2097152 | tf_op jit(solution)/shard_map/all_to_all | solution.py:105
  215.5 2.1 collective-permute-start.9
  218.5 2.6 shard_map.237
  225.1 4.4 %collective-permute-start.30 = (bf16[4,128,512]{2,1,0:T(8,128)(2,1)}, bf16[4,128,512]{2,1,0:T(8,128)(2,1)S(1)}, u32[]{:S(2)}, u32[]{:S(2)}) collective-permute-start(bf16[4,128,512]{2,1,0:T(8,128)(2,1)} %shard_map.249.refs_0_), channel_id=1, source_target_pairs={{0,1},{1,0},{2,3},{3,2},{4,5},{5,4},{6,7},{7,6},{8,24},{9,25},{10,... | collective-permute-start | bytes 1572872 | tf_op jit(solution)/shard_map/ppermute | solution.py:38
  229.5 5.3 %collective-permute-done.9 = bf16[2,128,128]{2,1,0:T(8,128)(2,1)S(1)} collective-permute-done((bf16[2,128,128]{2,1,0:T(8,128)(2,1)S(1)}, bf16[2,128,128]{2,1,0:T(8,128)(2,1)S(1)}, u32[]{:S(2)}, u32[]{:S(2)}) %collective-permute-start.9) | collective-permute-done | bytes 65568 | tf_op jit(solution)/shard_map/ppermute | solution.py:29
  234.8 3.1 collective-permute-start.10
  237.9 5.4 %shard_map.231.refs_10_.refs_2_ = f32[2,512,512]{2,1,0:T(8,128)} custom-call(bf16[512,512]{1,0:T(8,128)(2,1)} %refs_0_.4, bf16[512,512]{1,0:T(8,128)(2,1)} %refs_1_.5, bf16[512,512]{1,0:T(8,128)(2,1)} %refs_2_.7, bf16[512,512]{1,0:T(8,128)(2,1)} %get-tuple-element.107.refs_3_.refs_4_, bf16[512,512]{1,0:T(8,128)(2,1)} %get-tuple-element.108.refs_4_.refs_5_, ...), custom_call_target="tpu_custom_call" | custom-call | flops 4831838208 | bytes 20447232 | tf_op jit(solution)/shard_map/pallas_call | solution.py:151
  244.2 2.2 shard_map.250.refs_1_
  248.4 2.0 shard_map.238
  250.4 5.0 %shard_map.239 = (f32[2,16,512]{2,1,0:T(8,128)}, bf16[256,512]{1,0:T(8,128)(2,1)}, bf16[256,512]{1,0:T(8,128)(2,1)}) custom-call(f32[8,128]{1,0:T(8,128)} %add.56.refs_5_.refs_0_, s32[1,1]{1,0:T(1,128)} %bitcast.10.refs_1_, bf16[2,128,128]{2,1,0:T(8,128)(2,1)} %add_convert_fusion.refs_2_, bf16[8,7,16,512]{3,2,1,0:T(8,128)(2,1)} %all_to_all.40.refs_0_.refs_1_.refs_3_, ...), custom_call_target="tpu_custom_call" | custom-call | bytes 13774884 | tf_op jit(solution)/shard_map/pallas_call | solution.py:151
  264.5 2.5 collective-permute-start.16
  277.4 2.7 collective-permute-start.19
  280.1 2.6 collective-permute-done.21.refs_3_
  282.7 2.1 collective-permute-done.20.refs_2_
  291.9 2.4 collective-permute-done.22.refs_1_
  298.6 5.7 %shard_map.240 = (bf16[2,512,512]{2,1,0:T(8,128)(2,1)}, f32[2,8,512]{2,1,0:T(8,128)}) custom-call(bf16[2,512,512]{2,1,0:T(8,128)(2,1)} %refs_0_.5, f32[1,512]{1,0:T(1,128)} %bitcast.30, f32[2,512,512]{2,1,0:T(8,128)} %shard_map.231.refs_10_.refs_2_, bf16[8,8,16,512]{3,2,1,0:T(8,128)(2,1)} %copy-done.1, f32[2,16,512]{2,1,0:T(8,128)} %get-tuple-element.146.refs_4_, ...), custom_call_target="tpu_custom_call" | custom-call | bytes 19175424 | tf_op jit(solution)/shard_map/pallas_call | solution.py:151
  306.0 4.1 %all-to-all-start.7 = ((f32[32,8,512]{2,1,0:T(8,128)}), f32[32,8,512]{2,1,0:T(8,128)S(1)}, u32[]{:S(2)}, u32[]{:S(2)}) async-start(f32[32,8,512]{2,1,0:T(8,128)} %broadcast_in_dim.19), calls=%async_computation.7 | async-start | bytes 1048576 | tf_op jit(solution)/shard_map/all_to_all | solution.py:1161
  313.9 2.1 shard_map.248
  317.6 3.8 %shard_map.247 = (f32[512,512]{1,0:T(8,128)}, f32[512,512]{1,0:T(8,128)}, f32[512,512]{1,0:T(8,128)}, f32[512,512]{1,0:T(8,128)}) custom-call(s32[2]{0:T(128)} %pad_add_fusion.refs_3_.refs_0_.refs_8_, bf16[8,64,512]{2,1,0:T(8,128)(2,1)} %shard_map.246.refs_1_, bf16[8,64,512]{2,1,0:T(8,128)(2,1)} %copy-done.9, bf16[8,64,512]{2,1,0:T(8,128)(2,1)} %copy-done.10, ...), custom_call_target="tpu_custom_call" | custom-call | bytes 18874392 | tf_op jit(solution)/shard_map/pallas_call | solution.py:151
  321.4 6.2 %shard_map.251 = (f32[2048,512]{1,0:T(8,128)}, f32[512,2048]{1,0:T(8,128)}) custom-call(s32[2]{0:T(128)} %pad_add_fusion.refs_3_.refs_0_.refs_8_, bf16[8,128,512]{2,1,0:T(8,128)(2,1)} %shard_map.250.refs_1_, bf16[8,128,512]{2,1,0:T(8,128)(2,1)} %collective-permute-done.31.refs_2_, bf16[8,128,512]{2,1,0:T(8,128)(2,1)} %collective-permute-done.32.refs_3_, ...), custom_call_target="tpu_custom_call" | custom-call | bytes 37748760 | tf_op jit(solution)/shard_map/pallas_call | solution.py:151
  (174 shorter events, 70.9 us)
Async XLA Ops:
  38.8 17.6 %all-to-all-start.2 = ((bf16[8,4,16,512]{3,2,1,0:T(8,128)(2,1)}), bf16[8,4,16,512]{3,2,1,0:T(8,128)(2,1)S(1)}, u32[]{:S(2)}, u32[]{:S(2)}) async-start(bf16[8,4,16,512]{3,2,1,0:T(8,128)(2,1)} %get-tuple-element.97), calls=%async_computation.2 | async-start | bytes 1048576 | tf_op jit(solution)/shard_map/all_to_all | solution.py:105
  47.3 13.5 %copy-start.35 = (s32[2,512]{1,0:T(2,128)S(1)}, s32[2,512]{1,0:T(2,128)}, u32[]{:S(2)}) copy-start(s32[2,512]{1,0:T(2,128)} %param.14) | copy-start | bytes 12292
  52.6 12.8 %copy-start.37 = (bf16[512]{0:T(512)(128)(2,1)S(1)}, bf16[512]{0:T(512)(128)(2,1)}, u32[]{:S(2)}) copy-start(bf16[512]{0:T(512)(128)(2,1)} %param.22) | copy-start | bytes 3076
  56.4 18.1 %all-to-all-start.1 = ((bf16[8,4,16,512]{3,2,1,0:T(8,128)(2,1)}), bf16[8,4,16,512]{3,2,1,0:T(8,128)(2,1)S(1)}, u32[]{:S(2)}, u32[]{:S(2)}) async-start(bf16[8,4,16,512]{3,2,1,0:T(8,128)(2,1)} %shard_map.223), calls=%async_computation.1 | async-start | bytes 1048576 | tf_op jit(solution)/shard_map/all_to_all | solution.py:105
  62.1 1.2 collective-permute-start
  63.3 3.6 %collective-permute-start.1 = (f32[8,128]{1,0:T(8,128)S(1)}, f32[8,128]{1,0:T(8,128)S(1)}, u32[]{:S(2)}, u32[]{:S(2)}) collective-permute-start(f32[8,128]{1,0:T(8,128)S(1)} %add.55), channel_id=1, source_target_pairs={{0,16},{8,24},{16,0},{24,8},{1,17},{9,25},{17,1},{25,9},{2,18},{10... | collective-permute-start | bytes 12296 | tf_op jit(solution)/shard_map/ppermute | solution.py:29
  74.5 17.4 %all-to-all-start.3 = ((bf16[8,4,16,512]{3,2,1,0:T(8,128)(2,1)}), bf16[8,4,16,512]{3,2,1,0:T(8,128)(2,1)S(1)}, u32[]{:S(2)}, u32[]{:S(2)}) async-start(bf16[8,4,16,512]{3,2,1,0:T(8,128)(2,1)} %shard_map.225), calls=%async_computation.3 | async-start | bytes 1048576 | tf_op jit(solution)/shard_map/all_to_all | solution.py:105
  128.8 14.8 %collective-permute-start.2 = (bf16[16,128,512]{2,1,0:T(8,128)(2,1)}, bf16[16,128,512]{2,1,0:T(8,128)(2,1)S(1)}, u32[]{:S(2)}, u32[]{:S(2)}) collective-permute-start(bf16[16,128,512]{2,1,0:T(8,128)(2,1)} %get-tuple-element.114), channel_id=1, source_target_pairs={{0,8},{1,9},{2,10},{3,11},{4,12},{5,13},{6,14},{7,15},{8,0},{9,1},... | collective-permute-start | bytes 6291464 | tf_op jit(solution)/shard_map/ppermute | solution.py:38
  140.0 21.2 %all-to-all-start.4 = ((bf16[8,4,16,512]{3,2,1,0:T(8,128)(2,1)}), bf16[8,4,16,512]{3,2,1,0:T(8,128)(2,1)S(1)}, u32[]{:S(2)}, u32[]{:S(2)}) async-start(bf16[8,4,16,512]{3,2,1,0:T(8,128)(2,1)} %get-tuple-element.126), calls=%async_computation.4 | async-start | bytes 1048576 | tf_op jit(solution)/shard_map/all_to_all | solution.py:105
  148.8 26.2 %collective-permute-start.3 = (bf16[8,128,512]{2,1,0:T(8,128)(2,1)}, bf16[8,128,512]{2,1,0:T(8,128)(2,1)}, u32[]{:S(2)}, u32[]{:S(2)}) collective-permute-start(bf16[8,128,512]{2,1,0:T(8,128)(2,1)} %get-tuple-element.119), channel_id=1, source_target_pairs={{0,16},{1,17},{2,18},{3,19},{4,20},{5,21},{6,22},{7,23},{8,9},{9,8... | collective-permute-start | bytes 3145736 | tf_op jit(solution)/shard_map/ppermute | solution.py:38
  161.1 13.7 %copy-start.6 = (bf16[8,4,16,512]{3,2,1,0:T(8,128)(2,1)}, bf16[8,4,16,512]{3,2,1,0:T(8,128)(2,1)S(1)}, u32[]{:S(2)}) copy-start(bf16[8,4,16,512]{3,2,1,0:T(8,128)(2,1)S(1)} %all-to-all-done.4.refs_3_) | copy-start | bytes 1572868
  161.2 33.0 %all-to-all-start.5 = ((bf16[8,4,16,512]{3,2,1,0:T(8,128)(2,1)}), bf16[8,4,16,512]{3,2,1,0:T(8,128)(2,1)S(1)}, u32[]{:S(2)}, u32[]{:S(2)}) async-start(bf16[8,4,16,512]{3,2,1,0:T(8,128)(2,1)} %get-tuple-element.127), calls=%async_computation.5 | async-start | bytes 1048576 | tf_op jit(solution)/shard_map/all_to_all | solution.py:105
  174.9 42.7 %collective-permute-start.11 = (bf16[16,64,512]{2,1,0:T(8,128)(2,1)}, bf16[16,64,512]{2,1,0:T(8,128)(2,1)S(1)}, u32[]{:S(2)}, u32[]{:S(2)}) collective-permute-start(bf16[16,64,512]{2,1,0:T(8,128)(2,1)} %get-tuple-element.142), channel_id=1, source_target_pairs={{0,8},{1,9},{2,10},{3,11},{4,12},{5,13},{6,14},{7,15},{8,0},{9,1},... | collective-permute-start | bytes 3145736 | tf_op jit(solution)/shard_map/ppermute | solution.py:38
  177.6 9.4 %collective-permute-start.4 = (bf16[4,128,512]{2,1,0:T(8,128)(2,1)}, bf16[4,128,512]{2,1,0:T(8,128)(2,1)S(1)}, u32[]{:S(2)}, u32[]{:S(2)}) collective-permute-start(bf16[4,128,512]{2,1,0:T(8,128)(2,1)} %get-tuple-element.121), channel_id=1, source_target_pairs={{0,1},{1,0},{2,3},{3,2},{4,5},{5,4},{6,7},{7,6},{8,24},{9,25},{10,... | collective-permute-start | bytes 1572872 | tf_op jit(solution)/shard_map/ppermute | solution.py:38
  189.8 11.5 %collective-permute-start.5 = (bf16[1,128,512]{2,1,0:T(8,128)(2,1)}, bf16[1,128,512]{2,1,0:T(8,128)(2,1)S(1)}, u32[]{:S(2)}, u32[]{:S(2)}) collective-permute-start(bf16[1,128,512]{2,1,0:T(8,128)(2,1)} %get-tuple-element.123), channel_id=1, source_target_pairs={{0,4},{1,5},{2,6},{3,7},{4,0},{5,1},{6,2},{7,3},{8,12},{9,13},{10,... | collective-permute-start | bytes 393224 | tf_op jit(solution)/shard_map/ppermute | solution.py:38
  192.7 8.6 %collective-permute-start.6 = (bf16[1,128,512]{2,1,0:T(8,128)(2,1)}, bf16[1,128,512]{2,1,0:T(8,128)(2,1)S(1)}, u32[]{:S(2)}, u32[]{:S(2)}) collective-permute-start(bf16[1,128,512]{2,1,0:T(8,128)(2,1)} %get-tuple-element.124), channel_id=1, source_target_pairs={{0,2},{1,3},{2,0},{3,1},{4,6},{5,7},{6,4},{7,5},{8,10},{9,11},{10,... | collective-permute-start | bytes 393224 | tf_op jit(solution)/shard_map/ppermute | solution.py:38
  194.2 8.9 %collective-permute-start.7 = (bf16[1,128,512]{2,1,0:T(8,128)(2,1)}, bf16[1,128,512]{2,1,0:T(8,128)(2,1)S(1)}, u32[]{:S(2)}, u32[]{:S(2)}) collective-permute-start(bf16[1,128,512]{2,1,0:T(8,128)(2,1)} %get-tuple-element.125), channel_id=1, source_target_pairs={{0,6},{1,7},{2,4},{3,5},{4,2},{5,3},{6,0},{7,1},{8,14},{9,15},{10,... | collective-permute-start | bytes 393224 | tf_op jit(solution)/shard_map/ppermute | solution.py:38
  198.4 17.0 %copy-start.28 = (bf16[2,128,128]{2,1,0:T(8,128)(2,1)S(1)}, bf16[2,128,128]{2,1,0:T(8,128)(2,1)}, u32[]{:S(2)}) copy-start(bf16[2,128,128]{2,1,0:T(8,128)(2,1)} %get-tuple-element.130) | copy-start | bytes 196612
  198.4 17.0 %collective-permute-start.8 = (bf16[2,128,128]{2,1,0:T(8,128)(2,1)}, bf16[2,128,128]{2,1,0:T(8,128)(2,1)S(1)}, u32[]{:S(2)}, u32[]{:S(2)}) collective-permute-start(bf16[2,128,128]{2,1,0:T(8,128)(2,1)} %get-tuple-element.130), channel_id=1, source_target_pairs={{0,1},{1,0},{2,3},{3,2},{4,5},{5,4},{6,7},{7,6},{8,9},{9,8},{10,11... | collective-permute-start | bytes 196616 | tf_op jit(solution)/shard_map/ppermute | solution.py:29
  205.6 16.1 %collective-permute-start.29 = (bf16[1,128,512]{2,1,0:T(8,128)(2,1)}, bf16[1,128,512]{2,1,0:T(8,128)(2,1)S(1)}, u32[]{:S(2)}, u32[]{:S(2)}) collective-permute-start(bf16[1,128,512]{2,1,0:T(8,128)(2,1)} %get-tuple-element.163.refs_0_), channel_id=1, source_target_pairs={{0,6},{1,7},{2,4},{3,5},{4,2},{5,3},{6,0},{7,1},{8,14},{9,15},{10,... | collective-permute-start | bytes 393224 | tf_op jit(solution)/shard_map/ppermute | solution.py:38
  208.0 13.7 %collective-permute-start.28 = (bf16[1,128,512]{2,1,0:T(8,128)(2,1)}, bf16[1,128,512]{2,1,0:T(8,128)(2,1)S(1)}, u32[]{:S(2)}, u32[]{:S(2)}) collective-permute-start(bf16[1,128,512]{2,1,0:T(8,128)(2,1)} %get-tuple-element.163.refs_0_), channel_id=1, source_target_pairs={{0,2},{1,3},{2,0},{3,1},{4,6},{5,7},{6,4},{7,5},{8,10},{9,11},{10,... | collective-permute-start | bytes 393224 | tf_op jit(solution)/shard_map/ppermute | solution.py:38
  210.3 12.2 %collective-permute-start.27 = (bf16[1,128,512]{2,1,0:T(8,128)(2,1)}, bf16[1,128,512]{2,1,0:T(8,128)(2,1)S(1)}, u32[]{:S(2)}, u32[]{:S(2)}) collective-permute-start(bf16[1,128,512]{2,1,0:T(8,128)(2,1)} %get-tuple-element.163.refs_0_), channel_id=1, source_target_pairs={{0,4},{1,5},{2,6},{3,7},{4,0},{5,1},{6,2},{7,3},{8,12},{9,13},{10,... | collective-permute-start | bytes 393224 | tf_op jit(solution)/shard_map/ppermute | solution.py:38
  210.3 87.3 %all-to-all-start.6 = ((bf16[8,8,16,512]{3,2,1,0:T(8,128)(2,1)}), bf16[8,8,16,512]{3,2,1,0:T(8,128)(2,1)S(1)}, u32[]{:S(2)}, u32[]{:S(2)}) async-start(bf16[8,8,16,512]{3,2,1,0:T(8,128)(2,1)} %get-tuple-element.129), calls=%async_computation.6 | async-start | bytes 2097152 | tf_op jit(solution)/shard_map/all_to_all | solution.py:105
  215.5 19.3 %collective-permute-start.9 = (bf16[2,128,128]{2,1,0:T(8,128)(2,1)S(1)}, bf16[2,128,128]{2,1,0:T(8,128)(2,1)S(1)}, u32[]{:S(2)}, u32[]{:S(2)}) collective-permute-start(bf16[2,128,128]{2,1,0:T(8,128)(2,1)S(1)} %add_convert_fusion.2), channel_id=1, source_target_pairs={{0,2},{1,3},{2,0},{3,1},{4,6},{5,7},{6,4},{7,5},{8,10},{9,11},{10,... | collective-permute-start | bytes 196616 | tf_op jit(solution)/shard_map/ppermute | solution.py:29
  221.2 26.4 %collective-permute-start.12 = (bf16[8,64,512]{2,1,0:T(8,128)(2,1)}, bf16[8,64,512]{2,1,0:T(8,128)(2,1)S(1)}, u32[]{:S(2)}, u32[]{:S(2)}) collective-permute-start(bf16[8,64,512]{2,1,0:T(8,128)(2,1)} %get-tuple-element.144), channel_id=1, source_target_pairs={{0,16},{1,17},{2,18},{3,19},{4,20},{5,21},{6,22},{7,23},{8,9},{9,8... | collective-permute-start | bytes 1572872 | tf_op jit(solution)/shard_map/ppermute | solution.py:38
  225.1 18.3 %collective-permute-start.30 = (bf16[4,128,512]{2,1,0:T(8,128)(2,1)}, bf16[4,128,512]{2,1,0:T(8,128)(2,1)S(1)}, u32[]{:S(2)}, u32[]{:S(2)}) collective-permute-start(bf16[4,128,512]{2,1,0:T(8,128)(2,1)} %shard_map.249.refs_0_), channel_id=1, source_target_pairs={{0,1},{1,0},{2,3},{3,2},{4,5},{5,4},{6,7},{7,6},{8,24},{9,25},{10,... | collective-permute-start | bytes 1572872 | tf_op jit(solution)/shard_map/ppermute | solution.py:38
  234.8 12.1 %collective-permute-start.10 = (bf16[2,128,128]{2,1,0:T(8,128)(2,1)S(1)}, bf16[2,128,128]{2,1,0:T(8,128)(2,1)S(1)}, u32[]{:S(2)}, u32[]{:S(2)}) collective-permute-start(bf16[2,128,128]{2,1,0:T(8,128)(2,1)S(1)} %add_convert_fusion.1), channel_id=1, source_target_pairs={{0,4},{1,5},{2,6},{3,7},{4,0},{5,1},{6,2},{7,3},{8,12},{9,13},{10,... | collective-permute-start | bytes 196616 | tf_op jit(solution)/shard_map/ppermute | solution.py:29
  246.4 51.2 %collective-permute-start.31 = (bf16[8,128,512]{2,1,0:T(8,128)(2,1)}, bf16[8,128,512]{2,1,0:T(8,128)(2,1)}, u32[]{:S(2)}, u32[]{:S(2)}) collective-permute-start(bf16[8,128,512]{2,1,0:T(8,128)(2,1)} %shard_map.250.refs_1_), channel_id=1, source_target_pairs={{0,16},{1,17},{2,18},{3,19},{4,20},{5,21},{6,22},{7,23},{8,9},{9,8... | collective-permute-start | bytes 3145736 | tf_op jit(solution)/shard_map/ppermute | solution.py:38
  255.5 36.5 %copy-start.2 = (bf16[8,128,512]{2,1,0:T(8,128)(2,1)S(1)}, bf16[8,128,512]{2,1,0:T(8,128)(2,1)}, u32[]{:S(2)}) copy-start(bf16[8,128,512]{2,1,0:T(8,128)(2,1)} %shard_map.250.refs_1_) | copy-start | bytes 3145732
  255.5 1.7 collective-permute-start.14
  255.5 6.4 %collective-permute-start.13 = (bf16[4,64,512]{2,1,0:T(8,128)(2,1)S(1)}, bf16[4,64,512]{2,1,0:T(8,128)(2,1)S(1)}, u32[]{:S(2)}, u32[]{:S(2)}) collective-permute-start(bf16[4,64,512]{2,1,0:T(8,128)(2,1)S(1)} %copy-done.38), channel_id=1, source_target_pairs={{0,1},{1,0},{2,3},{3,2},{4,5},{5,4},{6,7},{7,6},{8,24},{9,25},{10,... | collective-permute-start | bytes 786440 | tf_op jit(solution)/shard_map/ppermute | solution.py:38
  259.7 10.1 %collective-permute-start.18 = (bf16[256,512]{1,0:T(8,128)(2,1)}, bf16[256,512]{1,0:T(8,128)(2,1)S(1)}, u32[]{:S(2)}, u32[]{:S(2)}) collective-permute-start(bf16[256,512]{1,0:T(8,128)(2,1)} %shard_map.241.refs_2_.refs_0_), channel_id=1, source_target_pairs={{0,16},{1,17},{2,18},{3,19},{4,20},{5,21},{6,22},{7,23},{8,24},{9,... | collective-permute-start | bytes 786440 | tf_op jit(solution)/shard_map/ppermute | solution.py:38
  264.3 7.9 %collective-permute-start.15 = (bf16[1,64,512]{2,1,0:T(8,128)(2,1)}, bf16[1,64,512]{2,1,0:T(8,128)(2,1)S(1)}, u32[]{:S(2)}, u32[]{:S(2)}) collective-permute-start(bf16[1,64,512]{2,1,0:T(8,128)(2,1)} %get-tuple-element.156), channel_id=1, source_target_pairs={{0,4},{1,5},{2,6},{3,7},{4,0},{5,1},{6,2},{7,3},{8,12},{9,13},{10,... | collective-permute-start | bytes 196616 | tf_op jit(solution)/shard_map/ppermute | solution.py:38
  264.5 7.8 %collective-permute-start.16 = (bf16[1,64,512]{2,1,0:T(8,128)(2,1)}, bf16[1,64,512]{2,1,0:T(8,128)(2,1)S(1)}, u32[]{:S(2)}, u32[]{:S(2)}) collective-permute-start(bf16[1,64,512]{2,1,0:T(8,128)(2,1)} %get-tuple-element.157), channel_id=1, source_target_pairs={{0,2},{1,3},{2,0},{3,1},{4,6},{5,7},{6,4},{7,5},{8,10},{9,11},{10,... | collective-permute-start | bytes 196616 | tf_op jit(solution)/shard_map/ppermute | solution.py:38
  267.0 6.5 %collective-permute-start.17 = (bf16[1,64,512]{2,1,0:T(8,128)(2,1)}, bf16[1,64,512]{2,1,0:T(8,128)(2,1)S(1)}, u32[]{:S(2)}, u32[]{:S(2)}) collective-permute-start(bf16[1,64,512]{2,1,0:T(8,128)(2,1)} %get-tuple-element.158), channel_id=1, source_target_pairs={{0,6},{1,7},{2,4},{3,5},{4,2},{5,3},{6,0},{7,1},{8,14},{9,15},{10,... | collective-permute-start | bytes 196616 | tf_op jit(solution)/shard_map/ppermute | solution.py:38
  275.7 7.0 %collective-permute-start.21 = (bf16[1,64,512]{2,1,0:T(8,128)(2,1)}, bf16[1,64,512]{2,1,0:T(8,128)(2,1)S(1)}, u32[]{:S(2)}, u32[]{:S(2)}) collective-permute-start(bf16[1,64,512]{2,1,0:T(8,128)(2,1)} %shard_map.244.refs_0_), channel_id=1, source_target_pairs={{0,6},{1,7},{2,4},{3,5},{4,2},{5,3},{6,0},{7,1},{8,14},{9,15},{10,... | collective-permute-start | bytes 196616 | tf_op jit(solution)/shard_map/ppermute | solution.py:38
  277.3 7.5 %collective-permute-start.20 = (bf16[1,64,512]{2,1,0:T(8,128)(2,1)}, bf16[1,64,512]{2,1,0:T(8,128)(2,1)S(1)}, u32[]{:S(2)}, u32[]{:S(2)}) collective-permute-start(bf16[1,64,512]{2,1,0:T(8,128)(2,1)} %shard_map.244.refs_0_), channel_id=1, source_target_pairs={{0,2},{1,3},{2,0},{3,1},{4,6},{5,7},{6,4},{7,5},{8,10},{9,11},{10,... | collective-permute-start | bytes 196616 | tf_op jit(solution)/shard_map/ppermute | solution.py:38
  277.4 7.5 %collective-permute-start.19 = (bf16[1,64,512]{2,1,0:T(8,128)(2,1)}, bf16[1,64,512]{2,1,0:T(8,128)(2,1)S(1)}, u32[]{:S(2)}, u32[]{:S(2)}) collective-permute-start(bf16[1,64,512]{2,1,0:T(8,128)(2,1)} %shard_map.244.refs_0_), channel_id=1, source_target_pairs={{0,4},{1,5},{2,6},{3,7},{4,0},{5,1},{6,2},{7,3},{8,12},{9,13},{10,... | collective-permute-start | bytes 196616 | tf_op jit(solution)/shard_map/ppermute | solution.py:38
  287.7 6.6 %collective-permute-start.22 = (bf16[4,64,512]{2,1,0:T(8,128)(2,1)}, bf16[4,64,512]{2,1,0:T(8,128)(2,1)S(1)}, u32[]{:S(2)}, u32[]{:S(2)}) collective-permute-start(bf16[4,64,512]{2,1,0:T(8,128)(2,1)} %shard_map.245.refs_0_), channel_id=1, source_target_pairs={{0,1},{1,0},{2,3},{3,2},{4,5},{5,4},{6,7},{7,6},{8,24},{9,25},{10,... | collective-permute-start | bytes 786440 | tf_op jit(solution)/shard_map/ppermute | solution.py:38
  291.9 29.5 %collective-permute-start.32 = (bf16[8,128,512]{2,1,0:T(8,128)(2,1)S(1)}, bf16[8,128,512]{2,1,0:T(8,128)(2,1)}, u32[]{:S(2)}, u32[]{:S(2)}) collective-permute-start(bf16[8,128,512]{2,1,0:T(8,128)(2,1)S(1)} %copy-done.2), channel_id=1, source_target_pairs={{0,8},{1,9},{2,10},{3,11},{4,12},{5,13},{6,14},{7,15},{8,0},{9,1},... | collective-permute-start | bytes 3145736 | tf_op jit(solution)/shard_map/ppermute | solution.py:38
  296.9 13.5 %collective-permute-start.23 = (bf16[8,64,512]{2,1,0:T(8,128)(2,1)}, bf16[8,64,512]{2,1,0:T(8,128)(2,1)S(1)}, u32[]{:S(2)}, u32[]{:S(2)}) collective-permute-start(bf16[8,64,512]{2,1,0:T(8,128)(2,1)} %shard_map.246.refs_1_), channel_id=1, source_target_pairs={{0,16},{1,17},{2,18},{3,19},{4,20},{5,21},{6,22},{7,23},{8,9},{9,8... | collective-permute-start | bytes 1572872 | tf_op jit(solution)/shard_map/ppermute | solution.py:38
  297.6 23.8 %collective-permute-start.33 = (bf16[8,128,512]{2,1,0:T(8,128)(2,1)}, bf16[8,128,512]{2,1,0:T(8,128)(2,1)}, u32[]{:S(2)}, u32[]{:S(2)}) collective-permute-start(bf16[8,128,512]{2,1,0:T(8,128)(2,1)} %collective-permute-done.31.refs_2_), channel_id=1, source_target_pairs={{0,8},{1,9},{2,10},{3,11},{4,12},{5,13},{6,14},{7,15},{8,0},{9,1},... | collective-permute-start | bytes 3145736 | tf_op jit(solution)/shard_map/ppermute | solution.py:38
  298.6 11.5 %copy-start.4 = (bf16[8,64,512]{2,1,0:T(8,128)(2,1)S(1)}, bf16[8,64,512]{2,1,0:T(8,128)(2,1)}, u32[]{:S(2)}) copy-start(bf16[8,64,512]{2,1,0:T(8,128)(2,1)} %shard_map.246.refs_1_) | copy-start | bytes 1572868
  298.6 12.1 %copy-start.3 = (bf16[256,512]{1,0:T(8,128)(2,1)S(1)}, bf16[256,512]{1,0:T(8,128)(2,1)}, u32[]{:S(2)}) copy-start(bf16[256,512]{1,0:T(8,128)(2,1)} %shard_map.243.refs_4_.refs_1_) | copy-start | bytes 786436
  306.0 21.6 %all-to-all-start.7 = ((f32[32,8,512]{2,1,0:T(8,128)}), f32[32,8,512]{2,1,0:T(8,128)S(1)}, u32[]{:S(2)}, u32[]{:S(2)}) async-start(f32[32,8,512]{2,1,0:T(8,128)} %broadcast_in_dim.19), calls=%async_computation.7 | async-start | bytes 1048576 | tf_op jit(solution)/shard_map/all_to_all | solution.py:1161
  310.1 5.9 %collective-permute-start.24 = (bf16[8,64,512]{2,1,0:T(8,128)(2,1)S(1)}, bf16[8,64,512]{2,1,0:T(8,128)(2,1)S(1)}, u32[]{:S(2)}, u32[]{:S(2)}) collective-permute-start(bf16[8,64,512]{2,1,0:T(8,128)(2,1)S(1)} %copy-done.4), channel_id=1, source_target_pairs={{0,8},{1,9},{2,10},{3,11},{4,12},{5,13},{6,14},{7,15},{8,0},{9,1},... | collective-permute-start | bytes 1572872 | tf_op jit(solution)/shard_map/ppermute | solution.py:38
  310.4 5.6 %collective-permute-start.25 = (bf16[8,64,512]{2,1,0:T(8,128)(2,1)S(1)}, bf16[8,64,512]{2,1,0:T(8,128)(2,1)S(1)}, u32[]{:S(2)}, u32[]{:S(2)}) collective-permute-start(bf16[8,64,512]{2,1,0:T(8,128)(2,1)S(1)} %collective-permute-done.23.refs_2_), channel_id=1, source_target_pairs={{0,8},{1,9},{2,10},{3,11},{4,12},{5,13},{6,14},{7,15},{8,0},{9,1},... | collective-permute-start | bytes 1572872 | tf_op jit(solution)/shard_map/ppermute | solution.py:38
  310.7 2.5 collective-permute-start.26
  (32 other events, 60.3 us)

commit v2 on v1

--- a/solution.py
+++ b/solution.py
@@ -250,7 +250,10 @@
     seqs, span, width = inputs.shape
     blocks = span // BLOCK
     p, r, n, w = chunk_shape(parts, blocks, width)
-    flags = jnp.repeat(real.astype(BF16).T, w // seqs, axis=1)
+    lane = jnp.arange(w)[None] * seqs // w
+    flags = jnp.zeros((blocks, w), BF16)
+    for s in range(seqs):
+        flags = jnp.where(lane == s, real[s].astype(BF16)[:, None], flags)
     more = seqs * (width // w) + 1
     return call(
         enter_kernel,
@@ -911,8 +914,20 @@
 
 
 def leave_kernel(
-    x_ref, gain_ref, d_hidden_ref, rows_ref, d_summary_ref, d_resid_ref, out_ref, total_ref, buffer
+    x_ref,
+    gain_ref,
+    d_hidden_ref,
+    rows_ref,
+    d_summary_ref,
+    d_resid_ref,
+    slope_ref,
+    entropy_ref,
+    out_ref,
+    small_ref,
+    buffer,
+    total,
 ):
+    step = pl.program_id(0)
     d_summary = d_summary_ref[0] * (1.0 / BLOCK)
     for t in range(BLOCK):
         strew(buffer, t, load_row(rows_ref, t).astype(F32) + d_summary)
@@ -920,18 +935,37 @@
     scale = lax.rsqrt(jnp.mean(x * x, axis=-1, keepdims=True) + EPS)
     n = x * scale
     up = d_hidden_ref[0] + lift(buffer)
-    total_ref[0] = jnp.broadcast_to(jnp.sum(up * n, axis=0, keepdims=True), total_ref.shape[1:])
+    here = jnp.sum(up * n, axis=0, keepdims=True)
+
+    @pl.when(step == 0)
+    def _():
+        total[...] = jnp.broadcast_to(here, total.shape)
+
+    @pl.when(step > 0)
+    def _():
+        total[...] = total[...] + here
+
     d_n = up * gain_ref[...]
     d_x = scale * (d_n - n * jnp.mean(d_n * n, axis=-1, keepdims=True))
     out_ref[0] = (d_x + d_resid_ref[0].astype(F32)).astype(BF16)
 
-
-def leave(inputs, gain, d_hidden, rows, d_summary, d_resid, after=()):
+    @pl.when(step == pl.num_programs(0) - 1)
+    def _():
+        row = lax.broadcasted_iota(jnp.int32, total.shape, 0)
+        entropy = entropy_ref[...]
+        entropy = jnp.concatenate([entropy] * (total.shape[1] // entropy.shape[1]), axis=1)
+        rest = jnp.where(row == 1, slope_ref[...], entropy)
+        all_rows = jnp.where(row == 0, total[...], rest)
+        for part in range(small_ref.shape[0]):
+            small_ref[part] = all_rows
+
+
+def leave(inputs, gain, d_hidden, rows, d_summary, d_resid, slope, entropy, parts):
     seqs, span, width = inputs.shape
     p, r, n, w = rows.shape
-    args = [inputs, gain, d_hidden, rows, d_summary, d_resid]
+    args = [inputs, gain, d_hidden, rows, d_summary, d_resid, slope, entropy]
     each = lambda a: pl.BlockSpec((1,) + a.shape[1:], lambda s: (s, 0, 0))
-    outs = [like(inputs.shape, BF16), like((seqs, 8, width), F32)]
+    outs = [like(inputs.shape, BF16), like((parts, 8, width), F32)]
     return call(
         leave_kernel,
         outs,
@@ -943,12 +977,21 @@
             pl.BlockSpec((p, r // seqs, n, w), lambda s: (0, s, 0, 0)),
             each(d_summary),
             each(d_resid),
+            whole(slope),
+            whole(entropy),
         ],
-        [row_buffer(span, width)],
+        [row_buffer(span, width), pltpu.VMEM((8, width), F32)],
         grid=(seqs,),
-        out_specs=[each(o) for o in outs],
-        after=after,
-    )
+        out_specs=[each(outs[0]), whole(outs[1])],
+    )
+
+
+def small_kernel(part, small_ref, count_ref, out_ref):
+    total = small_ref[0]
+    for k in range(1, small_ref.shape[0]):
+        total = total + small_ref[k]
+    row = lax.broadcasted_iota(jnp.int32, total.shape, 0)
+    out_ref[...] = jnp.where(row == 2, total * (-part / count_ref[:1, :1]), total)
 
 
 def sort_end_kernel(split_ref, half_ref, other_ref, out_ref):
@@ -1032,7 +1075,6 @@
             [spread[0], w_sort],
             after=(q,),
         )
-        entropy = entropy[0, 0]
     else:
         summary_all, reals = told_of(spread[0], seqs, width)
         real = reals[:, None, :] == 1
@@ -1041,6 +1083,7 @@
         low = prob.astype(BF16)
         entropy = jnp.sum(jnp.where(reals[:, :, None] == 1, prob * plan, 0.0))
         total_blocks = jnp.full((8, 128), jnp.sum(reals.astype(F32)))
+        entropy = jnp.full((8, 128), entropy)
     for bit in bits(dp_size):
         total_blocks = total_blocks + swap(total_blocks, "dp", bit)
 
@@ -1087,10 +1130,11 @@
     next(stages)
     _, d_rows = next(stages)
     d_rows = exchange(d_rows)
+    next(late_stages)
+    late2 = next(late_stages)
+    more["half"] = dict(after=[late2[0]])
     *_, last = stages
     grad_out, grad_in = feed_end(split, last)
-    next(late_stages)
-    late2 = next(late_stages)
 
     if small_plan:
         args = [
@@ -1139,9 +1183,18 @@
     (sort_half,) = add_split([sort_half, send(sort_half, X)], 1)
     late_more["line"] = dict(after=[sort_half])
     sort_other = send(sort_half, CORE)
-    input_grad, gains = leave(
-        inputs, gain_one, d_hidden, d_rows, d_summary, d_resid, ()
-    )
+    input_grad, small = leave(
+        inputs,
+        gain_one,
+        d_hidden,
+        d_rows,
+        d_summary,
+        d_resid,
+        slope,
+        entropy,
+        dp_size * seq_size,
+    )
+    small = lax.all_to_all(small, ("dp", "seq"), 0, 0, tiled=True)
     *_, last = late_stages
     grad_query, grad_key, grad_value, grad_output = late_end(split, last)
     (grad_sort,) = call(
@@ -1150,23 +1203,12 @@
         [split, sort_half, sort_other],
         [SCALAR, whole(sort_half), whole(sort_other)],
     )
-    small = jnp.concatenate(
-        [
-            jnp.sum(gains[:, :1], axis=0),
-            slope[:1],
-            jnp.full((1, width), entropy / seq_size),
-            jnp.zeros((5, width), F32),
-        ]
-    )
-    small = lax.all_to_all(
-        jnp.broadcast_to(small[None], (dp_size * seq_size,) + small.shape),
-        ("dp", "seq"),
-        0,
-        0,
-        tiled=True,
-    )
-    small = jnp.sum(small, axis=0)
-    penalty = -small[2, 0] / total_blocks[0, 0]
+    (small,) = call(
+        lambda *refs: small_kernel(1.0 / seq_size, *refs),
+        [like((8, width), F32)],
+        [small, total_blocks],
+    )
+    penalty = small[2, 0]
     return (
         output.reshape(inputs.shape),
         input_grad,

time: 333 us -> 331 us (level)
  waiting for transfers between devices: 39.8 us -> 47.2 us
  starting transfers between devices: 72.2 us -> 66.4 us
    ppermute x29, waiting for transfers between devices: 22.1 us -> 33.4 us  [send(): return lax.ppermute(array, ('dp', 'seq'), pairs)]
    ppermute x5, waiting for transfers between devices: 7.43 us -> 3.42 us  [swap(): lax.ppermute(array, axis, [(i, i ^ bit) for i in range(lax.axis_size(axis...]
    pallas_call x31 -> x32, Pallas kernels: 130 us -> 132 us  [call(): pl.pallas_call(lambda *refs: kernel(*refs[:count], *refs[count + skip:cou...]
    unnamed x79 -> x78, local copies, waits for them, and re-layouts: 16.2 us -> 16.4 us
  transfers between devices with their start and end apart: 41 -> 41, of which waited for: 18 -> 19; matrix products, arithmetic and copies ran while one was open for 3% -> 1% of each run, Pallas kernels for 35% -> 35%
where the time goes in v2:
time: 331 us; the launch traced here: 330 us
  Pallas kernels  158 us (48%)
  starting transfers between devices  66.4 us (20%)
  waiting for transfers between devices  47.2 us (14%)
  blocking collectives  30.7 us (9%)
  local copies, waits for them, and re-layouts  19.5 us (6%)
  other arithmetic  6.63 us (2%)
    pallas_call x32, Pallas kernels, call(): pl.pallas_call(lambda *refs: kernel(*refs[:count], *refs[count + skip:cou...  132 us
    ppermute x29, waiting for transfers between devices, send(): return lax.ppermute(array, ('dp', 'seq'), pairs)  33.4 us
    all_to_all x1, blocking collectives, exchange(): return lax.all_to_all(chunks, 'seq', 0, 0, tiled=True)  30.7 us
    ppermute x29, starting transfers between devices, send(): return lax.ppermute(array, ('dp', 'seq'), pairs)  30 us
    all_to_all x6, starting transfers between devices, exchange(): return lax.all_to_all(chunks, 'seq', 0, 0, tiled=True)  26.3 us
    pallas_call x1, Pallas kernels, feed(): pl.pallas_call(lambda *refs: feed_kernel(len(att), *refs), grid_spec=pltp...  26.2 us
    unnamed x78, local copies, waits for them, and re-layouts  16.4 us
    all_to_all x6, waiting for transfers between devices, exchange(): return lax.all_to_all(chunks, 'seq', 0, 0, tiled=True)  10.3 us
  transfers between devices with their start and end apart: 41, of which 19 were waited for; matrix products, arithmetic and copies ran while one was open for 1% of the time, Pallas kernels for 35%

profile of v2, /device:TPU:0, one launch (start us, length us, event | category | flops | bytes accessed | tf_op | source)
XLA Modules:
  0.0 329.6 jit_solution(17380734696771151235)
XLA Ops:
  3.3 4.7 %shard_map.220 = (bf16[2,512,512]{2,1,0:T(8,128)(2,1)}, bf16[8,7,16,512]{3,2,1,0:T(8,128)(2,1)}, bf16[8,4,16,512]{3,2,1,0:T(8,128)(2,1)}) custom-call(bf16[2,512,512]{2,1,0:T(8,128)(2,1)} %refs_0_.5, f32[1,512]{1,0:T(1,128)} %bitcast.23, bf16[16,512]{1,0:T(8,128)(2,1)} %select_select_fusion.refs_2_), custom_call_target="tpu_custom_call" | custom-call | bytes 10672128 | tf_op jit(solution)/shard_map/pallas_call | solution.py:151
  8.0 30.7 %all_to_all.40.refs_0_.refs_1_.refs_3_ = bf16[8,7,16,512]{3,2,1,0:T(8,128)(2,1)} all-to-all(bf16[8,7,16,512]{3,2,1,0:T(8,128)(2,1)} %get-tuple-element.89), channel_id=1, replica_groups=mesh['dp'=4,'seq'=8] {'seq'}, dimensions={0} | all-to-all | bytes 1835008 | tf_op jit(solution)/shard_map/all_to_all | solution.py:105
  38.7 3.5 %all-to-all-start.2 = ((bf16[8,4,16,512]{3,2,1,0:T(8,128)(2,1)}), bf16[8,4,16,512]{3,2,1,0:T(8,128)(2,1)S(1)}, u32[]{:S(2)}, u32[]{:S(2)}) async-start(bf16[8,4,16,512]{3,2,1,0:T(8,128)(2,1)} %get-tuple-element.97), calls=%async_computation.2 | async-start | bytes 1048576 | tf_op jit(solution)/shard_map/all_to_all | solution.py:105
  42.2 4.9 %shard_map.221 = (bf16[2,512,512]{2,1,0:T(8,128)(2,1)}, bf16[2,512,512]{2,1,0:T(8,128)(2,1)}, bf16[2,512,512]{2,1,0:T(8,128)(2,1)}, bf16[2,512,512]{2,1,0:T(8,12...) custom-call(bf16[2,512,512]{2,1,0:T(8,128)(2,1)} %get-tuple-element.90.refs_0_.refs_1_, ...), custom_call_target="tpu_custom_call" | custom-call | flops 4831838208 | bytes 26738688 | tf_op jit(solution)/shard_map/pallas_call | solution.py:151
  47.2 5.3 %shard_map.222 = (bf16[2,128,512]{2,1,0:T(8,128)(2,1)}, f32[16,2,128,128]{3,2,1,0:T(8,128)}, f32[2,128,128]{2,1,0:T(8,128)}, bf16[2,128,128]{2,1,0:T(8,128)(2,1)}, f32[8,128]{1,0:T(8,128)}, /*index=5*/f32[8,128]{1,0:T(8,128)}) custom-call(bf16[8,7,16,512]{3,2,1,0:T(8,128)(2,1)} %all_to_all.40.refs_0_.refs_1_.refs_3_, bf16[512,512]{1,0:T(8,128)(2,1)} %refs_4_.3, ...), custom_call_target="tpu_custom_call" | custom-call | bytes 12017664 | tf_op jit(solution)/shard_map/pallas_call | solution.py:151
  52.5 2.3 shard_map.223
  56.3 4.4 %all-to-all-start.1 = ((bf16[8,4,16,512]{3,2,1,0:T(8,128)(2,1)}), bf16[8,4,16,512]{3,2,1,0:T(8,128)(2,1)S(1)}, u32[]{:S(2)}, u32[]{:S(2)}) async-start(bf16[8,4,16,512]{3,2,1,0:T(8,128)(2,1)} %shard_map.223), calls=%async_computation.1 | async-start | bytes 1048576 | tf_op jit(solution)/shard_map/all_to_all | solution.py:105
  67.4 2.2 shard_map.225
  69.6 4.9 %all-to-all-done.1.refs_0_ = bf16[8,4,16,512]{3,2,1,0:T(8,128)(2,1)S(1)} async-done(((bf16[8,4,16,512]{3,2,1,0:T(8,128)(2,1)}), bf16[8,4,16,512]{3,2,1,0:T(8,128)(2,1)S(1)}, u32[]{:S(2)}, u32[]{:S(2)}) %all-to-all-start.1) | async-done | bytes 524320 | tf_op jit(solution)/shard_map/all_to_all | solution.py:105
  74.4 3.7 %all-to-all-start.3 = ((bf16[8,4,16,512]{3,2,1,0:T(8,128)(2,1)}), bf16[8,4,16,512]{3,2,1,0:T(8,128)(2,1)S(1)}, u32[]{:S(2)}, u32[]{:S(2)}) async-start(bf16[8,4,16,512]{3,2,1,0:T(8,128)(2,1)} %shard_map.225), calls=%async_computation.3 | async-start | bytes 1048576 | tf_op jit(solution)/shard_map/all_to_all | solution.py:105
  78.1 9.8 %shard_map.224 = (bf16[512,512]{1,0:T(8,128)(2,1)}, bf16[512,512]{1,0:T(8,128)(2,1)}, bf16[512,512]{1,0:T(8,128)(2,1)}, bf16[512,512]{1,0:T(8,128)(2,1)}, f32[16,64,256]{2,1,0:T(8,128)}) custom-call(bf16[8,4,16,512]{3,2,1,0:T(8,128)(2,1)} %copy-done.13, f32[2,32,512]{2,1,0:T(8,128)} %compare_convert_fusion.refs_1_.refs_2_, bf16[512,512]{1,0:T(8,128)(2,1)} %refs_1_.5, ...), custom_call_target="tpu_custom_call" | custom-call | flops 3221225472 | bytes 23986176 | tf_op jit(solution)/shard_map/pallas_call | solution.py:151
  87.9 4.0 %all-to-all-done.3.refs_0_ = bf16[8,4,16,512]{3,2,1,0:T(8,128)(2,1)S(1)} async-done(((bf16[8,4,16,512]{3,2,1,0:T(8,128)(2,1)}), bf16[8,4,16,512]{3,2,1,0:T(8,128)(2,1)S(1)}, u32[]{:S(2)}, u32[]{:S(2)}) %all-to-all-start.3) | async-done | bytes 524320 | tf_op jit(solution)/shard_map/all_to_all | solution.py:105
  92.6 9.8 %shard_map.226 = (bf16[512,512]{1,0:T(8,128)(2,1)}, bf16[512,512]{1,0:T(8,128)(2,1)}, bf16[512,512]{1,0:T(8,128)(2,1)}, bf16[512,512]{1,0:T(8,128)(2,1)}, f32[16,64,256]{2,1,0:T(8,128)}) custom-call(bf16[8,4,16,512]{3,2,1,0:T(8,128)(2,1)} %copy-done.15, f32[2,32,512]{2,1,0:T(8,128)} %compare_convert_fusion.refs_1_.refs_2_, bf16[512,512]{1,0:T(8,128)(2,1)} %refs_1_.5, ...), custom_call_target="tpu_custom_call" | custom-call | flops 3221225472 | bytes 23986176 | tf_op jit(solution)/shard_map/pallas_call | solution.py:151
  102.5 26.2 %shard_map.227 = (bf16[1024,512]{1,0:T(8,128)(2,1)}, bf16[16,128,512]{2,1,0:T(8,128)(2,1)}, bf16[16,128,512]{2,1,0:T(8,128)(2,1)}, bf16[512,512]{1,0:T(8,128)(2,...) custom-call(s32[2]{0:T(128)} %pad_add_fusion.refs_3_.refs_0_.refs_8_, ...), custom_call_target="tpu_custom_call" | custom-call | flops 38654705664 | bytes 75497472 | tf_op jit(solution)/shard_map/pallas_call | solution.py:860
  128.8 11.1 %shard_map.228 = (bf16[8,4,16,512]{3,2,1,0:T(8,128)(2,1)}, bf16[512,512]{1,0:T(8,128)(2,1)}, bf16[512,512]{1,0:T(8,128)(2,1)}, bf16[512,512]{1,0:T(8,128)(2,1)},...) custom-call(bf16[2,512,512]{2,1,0:T(8,128)(2,1)} %bitcast.31, ...), custom_call_target="tpu_custom_call" | custom-call | flops 4831838208 | bytes 31457280 | tf_op jit(solution)/shard_map/pallas_call | solution.py:151
  139.9 3.6 %all-to-all-start.4 = ((bf16[8,4,16,512]{3,2,1,0:T(8,128)(2,1)}), bf16[8,4,16,512]{3,2,1,0:T(8,128)(2,1)S(1)}, u32[]{:S(2)}, u32[]{:S(2)}) async-start(bf16[8,4,16,512]{3,2,1,0:T(8,128)(2,1)} %get-tuple-element.126), calls=%async_computation.4 | async-start | bytes 1048576 | tf_op jit(solution)/shard_map/all_to_all | solution.py:105
  144.8 3.8 %shard_map.229 = (bf16[8,128,512]{2,1,0:T(8,128)(2,1)}, bf16[8,128,512]{2,1,0:T(8,128)(2,1)}) custom-call(bf16[16,128,512]{2,1,0:T(8,128)(2,1)} %get-tuple-element.113.refs_0_, bf16[16,128,512]{2,1,0:T(8,128)(2,1)} %copy-done.5), custom_call_target="tpu_custom_call" | custom-call | bytes 18874368 | tf_op jit(solution)/shard_map/pallas_call | solution.py:151
  150.1 10.9 %shard_map.230 = (bf16[8,4,16,512]{3,2,1,0:T(8,128)(2,1)}, bf16[512,512]{1,0:T(8,128)(2,1)}, bf16[512,512]{1,0:T(8,128)(2,1)}, bf16[512,512]{1,0:T(8,128)(2,1)},...) custom-call(bf16[2,512,512]{2,1,0:T(8,128)(2,1)} %bitcast.32, ...), custom_call_target="tpu_custom_call" | custom-call | flops 4831838208 | bytes 31457280 | tf_op jit(solution)/shard_map/pallas_call | solution.py:151
  161.0 6.0 %all-to-all-start.5 = ((bf16[8,4,16,512]{3,2,1,0:T(8,128)(2,1)}), bf16[8,4,16,512]{3,2,1,0:T(8,128)(2,1)S(1)}, u32[]{:S(2)}, u32[]{:S(2)}) async-start(bf16[8,4,16,512]{3,2,1,0:T(8,128)(2,1)} %get-tuple-element.127), calls=%async_computation.5 | async-start | bytes 1048576 | tf_op jit(solution)/shard_map/all_to_all | solution.py:105
  167.0 7.7 %shard_map.236 = (bf16[16,64,512]{2,1,0:T(8,128)(2,1)}, bf16[16,64,512]{2,1,0:T(8,128)(2,1)}) custom-call(s32[2]{0:T(128)} %pad_add_fusion.refs_3_.refs_0_.refs_8_, bf16[2,512,512]{2,1,0:T(8,128)(2,1)} %get-tuple-element.90.refs_0_.refs_1_, bf16[512,512]{1,0:T(8,128)(2,1)} %get-tuple-element.134.refs_2_, bf16[512,512]{1,0:T(8,128)(2,1)} %get-tuple-element.135.refs_3_, ...), custom_call_target="tpu_custom_call" | custom-call | flops 8053063680 | bytes 29884440 | tf_op jit(solution)/shard_map/pallas_call | solution.py:151
  174.8 2.6 shard_map.232
  177.5 2.0 collective-permute-start.4
  179.5 7.4 %collective-permute-done.4.refs_1_ = bf16[4,128,512]{2,1,0:T(8,128)(2,1)S(1)} collective-permute-done((bf16[4,128,512]{2,1,0:T(8,128)(2,1)}, bf16[4,128,512]{2,1,0:T(8,128)(2,1)S(1)}, u32[]{:S(2)}, u32[]{:S(2)}) %collective-permute-start.4) | collective-permute-done | bytes 524320 | tf_op jit(solution)/shard_map/ppermute | solution.py:38
  187.7 2.0 shard_map.233
  189.7 2.9 collective-permute-start.5
  194.9 3.4 %shard_map.234 = (bf16[8,8,16,512]{3,2,1,0:T(8,128)(2,1)}, bf16[2,128,128]{2,1,0:T(8,128)(2,1)}) custom-call(bf16[2,128,128]{2,1,0:T(8,128)(2,1)} %get-tuple-element.92.refs_0_, bf16[8,7,16,512]{3,2,1,0:T(8,128)(2,1)} %all_to_all.40.refs_0_.refs_1_.refs_3_, bf16[8,4,16,512]{3,2,1,0:T(8,128)(2,1)} %copy-done, bf16[8,4,16,512]{3,2,1,0:T(8,128)(2,1)} %copy-done.7, ...), custom_call_target="tpu_custom_call" | custom-call | bytes 11010048 | tf_op jit(solution)/shard_map/pallas_call | solution.py:151
  198.3 2.0 collective-permute-start.8
  205.5 4.2 %collective-permute-start.27 = (bf16[1,128,512]{2,1,0:T(8,128)(2,1)}, bf16[1,128,512]{2,1,0:T(8,128)(2,1)S(1)}, u32[]{:S(2)}, u32[]{:S(2)}) collective-permute-start(bf16[1,128,512]{2,1,0:T(8,128)(2,1)} %get-tuple-element.163.refs_0_), channel_id=1, source_target_pairs={{0,4},{1,5},{2,6},{3,7},{4,0},{5,1},{6,2},{7,3},{8,12},{9,13},{10,... | collective-permute-start | bytes 393224 | tf_op jit(solution)/shard_map/ppermute | solution.py:38
  212.6 5.1 %all-to-all-start.6 = ((bf16[8,8,16,512]{3,2,1,0:T(8,128)(2,1)}), bf16[8,8,16,512]{3,2,1,0:T(8,128)(2,1)S(1)}, u32[]{:S(2)}, u32[]{:S(2)}) async-start(bf16[8,8,16,512]{3,2,1,0:T(8,128)(2,1)} %get-tuple-element.129), calls=%async_computation.6 | async-start | bytes 2097152 | tf_op jit(solution)/shard_map/all_to_all | solution.py:105
  218.7 2.6 shard_map.237
  223.2 1.9 shard_map.250.refs_0_
  225.1 2.0 collective-permute-start.30
  227.1 2.4 collective-permute-start.10
  229.6 5.4 %shard_map.231.refs_10_.refs_2_ = f32[2,512,512]{2,1,0:T(8,128)} custom-call(bf16[512,512]{1,0:T(8,128)(2,1)} %refs_0_.4, bf16[512,512]{1,0:T(8,128)(2,1)} %refs_1_.5, bf16[512,512]{1,0:T(8,128)(2,1)} %refs_2_.7, bf16[512,512]{1,0:T(8,128)(2,1)} %get-tuple-element.107.refs_3_.refs_4_, bf16[512,512]{1,0:T(8,128)(2,1)} %get-tuple-element.108.refs_4_.refs_5_, ...), custom_call_target="tpu_custom_call" | custom-call | flops 4831838208 | bytes 20447232 | tf_op jit(solution)/shard_map/pallas_call | solution.py:151
  235.8 2.1 shard_map.238
  237.9 4.6 %collective-permute-done.30.refs_1_ = bf16[4,128,512]{2,1,0:T(8,128)(2,1)S(1)} collective-permute-done((bf16[4,128,512]{2,1,0:T(8,128)(2,1)}, bf16[4,128,512]{2,1,0:T(8,128)(2,1)S(1)}, u32[]{:S(2)}, u32[]{:S(2)}) %collective-permute-start.30) | collective-permute-done | bytes 524320 | tf_op jit(solution)/shard_map/ppermute | solution.py:38
  243.3 2.2 shard_map.251.refs_1_
  248.1 5.0 %shard_map.239 = (f32[2,16,512]{2,1,0:T(8,128)}, bf16[256,512]{1,0:T(8,128)(2,1)}, bf16[256,512]{1,0:T(8,128)(2,1)}) custom-call(f32[8,128]{1,0:T(8,128)} %add.65.refs_5_.refs_0_.refs_1_, s32[1,1]{1,0:T(1,128)} %bitcast.11.refs_1_, bf16[2,128,128]{2,1,0:T(8,128)(2,1)} %add_convert_fusion.refs_2_, bf16[8,7,16,512]{3,2,1,0:T(8,128)(2,1)} %all_to_all.40.refs_0_.refs_1_.refs_3_, ...), custom_call_target="tpu_custom_call" | custom-call | bytes 13774884 | tf_op jit(solution)/shard_map/pallas_call | solution.py:151
  258.0 3.8 %collective-permute-done.13.refs_1_ = bf16[4,64,512]{2,1,0:T(8,128)(2,1)S(1)} collective-permute-done((bf16[4,64,512]{2,1,0:T(8,128)(2,1)S(1)}, bf16[4,64,512]{2,1,0:T(8,128)(2,1)S(1)}, u32[]{:S(2)}, u32[]{:S(2)}) %collective-permute-start.13) | collective-permute-done | bytes 262176 | tf_op jit(solution)/shard_map/ppermute | solution.py:38
  266.6 2.0 collective-permute-start.17
  279.6 3.7 %collective-permute-done.19.refs_1_ = bf16[1,64,512]{2,1,0:T(8,128)(2,1)S(1)} collective-permute-done((bf16[1,64,512]{2,1,0:T(8,128)(2,1)}, bf16[1,64,512]{2,1,0:T(8,128)(2,1)S(1)}, u32[]{:S(2)}, u32[]{:S(2)}) %collective-permute-start.19) | collective-permute-done | bytes 65568 | tf_op jit(solution)/shard_map/ppermute | solution.py:38
  287.2 5.9 %collective-permute-done.22.refs_1_ = bf16[4,64,512]{2,1,0:T(8,128)(2,1)S(1)} collective-permute-done((bf16[4,64,512]{2,1,0:T(8,128)(2,1)}, bf16[4,64,512]{2,1,0:T(8,128)(2,1)S(1)}, u32[]{:S(2)}, u32[]{:S(2)}) %collective-permute-start.22) | collective-permute-done | bytes 262176 | tf_op jit(solution)/shard_map/ppermute | solution.py:38
  297.5 6.1 %shard_map.240 = (bf16[2,512,512]{2,1,0:T(8,128)(2,1)}, f32[32,8,512]{2,1,0:T(8,128)}) custom-call(bf16[2,512,512]{2,1,0:T(8,128)(2,1)} %refs_0_.5, f32[1,512]{1,0:T(1,128)} %bitcast.24, f32[2,512,512]{2,1,0:T(8,128)} %shard_map.231.refs_10_.refs_2_, bf16[8,8,16,512]{3,2,1,0:T(8,128)(2,1)} %copy-done.2, f32[2,16,512]{2,1,0:T(8,128)} %get-tuple-element.146.refs_4_, ...), custom_call_target="tpu_custom_call" | custom-call | bytes 20711424 | tf_op jit(solution)/shard_map/pallas_call | solution.py:151
  303.6 3.5 %all-to-all-start.7 = ((f32[32,8,512]{2,1,0:T(8,128)}), f32[32,8,512]{2,1,0:T(8,128)S(1)}, u32[]{:S(2)}, u32[]{:S(2)}) async-start(f32[32,8,512]{2,1,0:T(8,128)} %get-tuple-element.151), calls=%async_computation.7 | async-start | bytes 1048576 | tf_op jit(solution)/shard_map/all_to_all | solution.py:1197
  307.9 2.3 collective-permute-done.26.refs_2_
  310.9 2.1 shard_map.249
  314.6 3.8 %shard_map.248 = (f32[512,512]{1,0:T(8,128)}, f32[512,512]{1,0:T(8,128)}, f32[512,512]{1,0:T(8,128)}, f32[512,512]{1,0:T(8,128)}) custom-call(s32[2]{0:T(128)} %pad_add_fusion.refs_3_.refs_0_.refs_8_, bf16[8,64,512]{2,1,0:T(8,128)(2,1)} %shard_map.247.refs_1_, bf16[8,64,512]{2,1,0:T(8,128)(2,1)} %copy-done.10, bf16[8,64,512]{2,1,0:T(8,128)(2,1)} %copy-done.11, ...), custom_call_target="tpu_custom_call" | custom-call | bytes 18874392 | tf_op jit(solution)/shard_map/pallas_call | solution.py:151
  318.4 6.2 %shard_map.252 = (f32[2048,512]{1,0:T(8,128)}, f32[512,2048]{1,0:T(8,128)}) custom-call(s32[2]{0:T(128)} %pad_add_fusion.refs_3_.refs_0_.refs_8_, bf16[8,128,512]{2,1,0:T(8,128)(2,1)} %shard_map.251.refs_1_, bf16[8,128,512]{2,1,0:T(8,128)(2,1)} %collective-permute-done.31.refs_2_, bf16[8,128,512]{2,1,0:T(8,128)(2,1)} %collective-permute-done.32.refs_3_, ...), custom_call_target="tpu_custom_call" | custom-call | bytes 37748760 | tf_op jit(solution)/shard_map/pallas_call | solution.py:151
  (165 shorter events, 69.9 us)
Async XLA Ops:
  38.7 17.6 %all-to-all-start.2 = ((bf16[8,4,16,512]{3,2,1,0:T(8,128)(2,1)}), bf16[8,4,16,512]{3,2,1,0:T(8,128)(2,1)S(1)}, u32[]{:S(2)}, u32[]{:S(2)}) async-start(bf16[8,4,16,512]{3,2,1,0:T(8,128)(2,1)} %get-tuple-element.97), calls=%async_computation.2 | async-start | bytes 1048576 | tf_op jit(solution)/shard_map/all_to_all | solution.py:105
  47.2 13.5 %copy-start.35 = (s32[2,512]{1,0:T(2,128)S(1)}, s32[2,512]{1,0:T(2,128)}, u32[]{:S(2)}) copy-start(s32[2,512]{1,0:T(2,128)} %param.14) | copy-start | bytes 12292
  52.5 12.8 %copy-start.37 = (bf16[512]{0:T(512)(128)(2,1)S(1)}, bf16[512]{0:T(512)(128)(2,1)}, u32[]{:S(2)}) copy-start(bf16[512]{0:T(512)(128)(2,1)} %param.22) | copy-start | bytes 3076
  56.3 11.1 %copy-start = (bf16[8,4,16,512]{3,2,1,0:T(8,128)(2,1)}, bf16[8,4,16,512]{3,2,1,0:T(8,128)(2,1)S(1)}, u32[]{:S(2)}) copy-start(bf16[8,4,16,512]{3,2,1,0:T(8,128)(2,1)S(1)} %all-to-all-done.2.refs_1_.refs_2_) | copy-start | bytes 1572868
  56.3 18.1 %all-to-all-start.1 = ((bf16[8,4,16,512]{3,2,1,0:T(8,128)(2,1)}), bf16[8,4,16,512]{3,2,1,0:T(8,128)(2,1)S(1)}, u32[]{:S(2)}, u32[]{:S(2)}) async-start(bf16[8,4,16,512]{3,2,1,0:T(8,128)(2,1)} %shard_map.223), calls=%async_computation.1 | async-start | bytes 1048576 | tf_op jit(solution)/shard_map/all_to_all | solution.py:105
  62.0 1.2 collective-permute-start
  63.2 3.6 %collective-permute-start.1 = (f32[8,128]{1,0:T(8,128)S(1)}, f32[8,128]{1,0:T(8,128)S(1)}, u32[]{:S(2)}, u32[]{:S(2)}) collective-permute-start(f32[8,128]{1,0:T(8,128)S(1)} %add.64), channel_id=1, source_target_pairs={{0,16},{8,24},{16,0},{24,8},{1,17},{9,25},{17,1},{25,9},{2,18},{10... | collective-permute-start | bytes 12296 | tf_op jit(solution)/shard_map/ppermute | solution.py:29
  74.4 17.4 %all-to-all-start.3 = ((bf16[8,4,16,512]{3,2,1,0:T(8,128)(2,1)}), bf16[8,4,16,512]{3,2,1,0:T(8,128)(2,1)S(1)}, u32[]{:S(2)}, u32[]{:S(2)}) async-start(bf16[8,4,16,512]{3,2,1,0:T(8,128)(2,1)} %shard_map.225), calls=%async_computation.3 | async-start | bytes 1048576 | tf_op jit(solution)/shard_map/all_to_all | solution.py:105
  128.7 14.8 %collective-permute-start.2 = (bf16[16,128,512]{2,1,0:T(8,128)(2,1)}, bf16[16,128,512]{2,1,0:T(8,128)(2,1)S(1)}, u32[]{:S(2)}, u32[]{:S(2)}) collective-permute-start(bf16[16,128,512]{2,1,0:T(8,128)(2,1)} %get-tuple-element.114), channel_id=1, source_target_pairs={{0,8},{1,9},{2,10},{3,11},{4,12},{5,13},{6,14},{7,15},{8,0},{9,1},... | collective-permute-start | bytes 6291464 | tf_op jit(solution)/shard_map/ppermute | solution.py:38
  139.9 21.2 %all-to-all-start.4 = ((bf16[8,4,16,512]{3,2,1,0:T(8,128)(2,1)}), bf16[8,4,16,512]{3,2,1,0:T(8,128)(2,1)S(1)}, u32[]{:S(2)}, u32[]{:S(2)}) async-start(bf16[8,4,16,512]{3,2,1,0:T(8,128)(2,1)} %get-tuple-element.126), calls=%async_computation.4 | async-start | bytes 1048576 | tf_op jit(solution)/shard_map/all_to_all | solution.py:105
  148.7 26.2 %collective-permute-start.3 = (bf16[8,128,512]{2,1,0:T(8,128)(2,1)}, bf16[8,128,512]{2,1,0:T(8,128)(2,1)}, u32[]{:S(2)}, u32[]{:S(2)}) collective-permute-start(bf16[8,128,512]{2,1,0:T(8,128)(2,1)} %get-tuple-element.119), channel_id=1, source_target_pairs={{0,16},{1,17},{2,18},{3,19},{4,20},{5,21},{6,22},{7,23},{8,9},{9,8... | collective-permute-start | bytes 3145736 | tf_op jit(solution)/shard_map/ppermute | solution.py:38
  161.0 13.7 %copy-start.7 = (bf16[8,4,16,512]{3,2,1,0:T(8,128)(2,1)}, bf16[8,4,16,512]{3,2,1,0:T(8,128)(2,1)S(1)}, u32[]{:S(2)}) copy-start(bf16[8,4,16,512]{3,2,1,0:T(8,128)(2,1)S(1)} %all-to-all-done.4.refs_3_) | copy-start | bytes 1572868
  161.0 33.0 %all-to-all-start.5 = ((bf16[8,4,16,512]{3,2,1,0:T(8,128)(2,1)}), bf16[8,4,16,512]{3,2,1,0:T(8,128)(2,1)S(1)}, u32[]{:S(2)}, u32[]{:S(2)}) async-start(bf16[8,4,16,512]{3,2,1,0:T(8,128)(2,1)} %get-tuple-element.127), calls=%async_computation.5 | async-start | bytes 1048576 | tf_op jit(solution)/shard_map/all_to_all | solution.py:105
  174.7 42.9 %collective-permute-start.11 = (bf16[16,64,512]{2,1,0:T(8,128)(2,1)}, bf16[16,64,512]{2,1,0:T(8,128)(2,1)S(1)}, u32[]{:S(2)}, u32[]{:S(2)}) collective-permute-start(bf16[16,64,512]{2,1,0:T(8,128)(2,1)} %get-tuple-element.142), channel_id=1, source_target_pairs={{0,8},{1,9},{2,10},{3,11},{4,12},{5,13},{6,14},{7,15},{8,0},{9,1},... | collective-permute-start | bytes 3145736 | tf_op jit(solution)/shard_map/ppermute | solution.py:38
  177.5 9.4 %collective-permute-start.4 = (bf16[4,128,512]{2,1,0:T(8,128)(2,1)}, bf16[4,128,512]{2,1,0:T(8,128)(2,1)S(1)}, u32[]{:S(2)}, u32[]{:S(2)}) collective-permute-start(bf16[4,128,512]{2,1,0:T(8,128)(2,1)} %get-tuple-element.121), channel_id=1, source_target_pairs={{0,1},{1,0},{2,3},{3,2},{4,5},{5,4},{6,7},{7,6},{8,24},{9,25},{10,... | collective-permute-start | bytes 1572872 | tf_op jit(solution)/shard_map/ppermute | solution.py:38
  189.7 11.5 %collective-permute-start.5 = (bf16[1,128,512]{2,1,0:T(8,128)(2,1)}, bf16[1,128,512]{2,1,0:T(8,128)(2,1)S(1)}, u32[]{:S(2)}, u32[]{:S(2)}) collective-permute-start(bf16[1,128,512]{2,1,0:T(8,128)(2,1)} %get-tuple-element.123), channel_id=1, source_target_pairs={{0,4},{1,5},{2,6},{3,7},{4,0},{5,1},{6,2},{7,3},{8,12},{9,13},{10,... | collective-permute-start | bytes 393224 | tf_op jit(solution)/shard_map/ppermute | solution.py:38
  192.6 8.6 %collective-permute-start.6 = (bf16[1,128,512]{2,1,0:T(8,128)(2,1)}, bf16[1,128,512]{2,1,0:T(8,128)(2,1)S(1)}, u32[]{:S(2)}, u32[]{:S(2)}) collective-permute-start(bf16[1,128,512]{2,1,0:T(8,128)(2,1)} %get-tuple-element.124), channel_id=1, source_target_pairs={{0,2},{1,3},{2,0},{3,1},{4,6},{5,7},{6,4},{7,5},{8,10},{9,11},{10,... | collective-permute-start | bytes 393224 | tf_op jit(solution)/shard_map/ppermute | solution.py:38
  194.1 8.9 %collective-permute-start.7 = (bf16[1,128,512]{2,1,0:T(8,128)(2,1)}, bf16[1,128,512]{2,1,0:T(8,128)(2,1)S(1)}, u32[]{:S(2)}, u32[]{:S(2)}) collective-permute-start(bf16[1,128,512]{2,1,0:T(8,128)(2,1)} %get-tuple-element.125), channel_id=1, source_target_pairs={{0,6},{1,7},{2,4},{3,5},{4,2},{5,3},{6,0},{7,1},{8,14},{9,15},{10,... | collective-permute-start | bytes 393224 | tf_op jit(solution)/shard_map/ppermute | solution.py:38
  198.3 12.8 %collective-permute-start.8 = (bf16[2,128,128]{2,1,0:T(8,128)(2,1)}, bf16[2,128,128]{2,1,0:T(8,128)(2,1)S(1)}, u32[]{:S(2)}, u32[]{:S(2)}) collective-permute-start(bf16[2,128,128]{2,1,0:T(8,128)(2,1)} %get-tuple-element.130), channel_id=1, source_target_pairs={{0,1},{1,0},{2,3},{3,2},{4,5},{5,4},{6,7},{7,6},{8,9},{9,8},{10,11... | collective-permute-start | bytes 196616 | tf_op jit(solution)/shard_map/ppermute | solution.py:29
  205.5 16.4 %collective-permute-start.27 = (bf16[1,128,512]{2,1,0:T(8,128)(2,1)}, bf16[1,128,512]{2,1,0:T(8,128)(2,1)S(1)}, u32[]{:S(2)}, u32[]{:S(2)}) collective-permute-start(bf16[1,128,512]{2,1,0:T(8,128)(2,1)} %get-tuple-element.163.refs_0_), channel_id=1, source_target_pairs={{0,4},{1,5},{2,6},{3,7},{4,0},{5,1},{6,2},{7,3},{8,12},{9,13},{10,... | collective-permute-start | bytes 393224 | tf_op jit(solution)/shard_map/ppermute | solution.py:38
  209.6 12.2 %collective-permute-start.28 = (bf16[1,128,512]{2,1,0:T(8,128)(2,1)}, bf16[1,128,512]{2,1,0:T(8,128)(2,1)S(1)}, u32[]{:S(2)}, u32[]{:S(2)}) collective-permute-start(bf16[1,128,512]{2,1,0:T(8,128)(2,1)} %get-tuple-element.163.refs_0_), channel_id=1, source_target_pairs={{0,2},{1,3},{2,0},{3,1},{4,6},{5,7},{6,4},{7,5},{8,10},{9,11},{10,... | collective-permute-start | bytes 393224 | tf_op jit(solution)/shard_map/ppermute | solution.py:38
  209.6 12.2 %collective-permute-start.29 = (bf16[1,128,512]{2,1,0:T(8,128)(2,1)}, bf16[1,128,512]{2,1,0:T(8,128)(2,1)S(1)}, u32[]{:S(2)}, u32[]{:S(2)}) collective-permute-start(bf16[1,128,512]{2,1,0:T(8,128)(2,1)} %get-tuple-element.163.refs_0_), channel_id=1, source_target_pairs={{0,6},{1,7},{2,4},{3,5},{4,2},{5,3},{6,0},{7,1},{8,14},{9,15},{10,... | collective-permute-start | bytes 393224 | tf_op jit(solution)/shard_map/ppermute | solution.py:38
  212.0 15.2 %collective-permute-start.9 = (bf16[2,128,128]{2,1,0:T(8,128)(2,1)S(1)}, bf16[2,128,128]{2,1,0:T(8,128)(2,1)S(1)}, u32[]{:S(2)}, u32[]{:S(2)}) collective-permute-start(bf16[2,128,128]{2,1,0:T(8,128)(2,1)S(1)} %add_convert_fusion.2), channel_id=1, source_target_pairs={{0,2},{1,3},{2,0},{3,1},{4,6},{5,7},{6,4},{7,5},{8,10},{9,11},{10,... | collective-permute-start | bytes 196616 | tf_op jit(solution)/shard_map/ppermute | solution.py:29
  212.6 84.0 %all-to-all-start.6 = ((bf16[8,8,16,512]{3,2,1,0:T(8,128)(2,1)}), bf16[8,8,16,512]{3,2,1,0:T(8,128)(2,1)S(1)}, u32[]{:S(2)}, u32[]{:S(2)}) async-start(bf16[8,8,16,512]{3,2,1,0:T(8,128)(2,1)} %get-tuple-element.129), calls=%async_computation.6 | async-start | bytes 2097152 | tf_op jit(solution)/shard_map/all_to_all | solution.py:105
  221.3 13.7 %collective-permute-start.12 = (bf16[8,64,512]{2,1,0:T(8,128)(2,1)}, bf16[8,64,512]{2,1,0:T(8,128)(2,1)S(1)}, u32[]{:S(2)}, u32[]{:S(2)}) collective-permute-start(bf16[8,64,512]{2,1,0:T(8,128)(2,1)} %get-tuple-element.144), channel_id=1, source_target_pairs={{0,16},{1,17},{2,18},{3,19},{4,20},{5,21},{6,22},{7,23},{8,9},{9,8... | collective-permute-start | bytes 1572872 | tf_op jit(solution)/shard_map/ppermute | solution.py:38
  225.1 17.4 %collective-permute-start.30 = (bf16[4,128,512]{2,1,0:T(8,128)(2,1)}, bf16[4,128,512]{2,1,0:T(8,128)(2,1)S(1)}, u32[]{:S(2)}, u32[]{:S(2)}) collective-permute-start(bf16[4,128,512]{2,1,0:T(8,128)(2,1)} %shard_map.250.refs_0_), channel_id=1, source_target_pairs={{0,1},{1,0},{2,3},{3,2},{4,5},{5,4},{6,7},{7,6},{8,24},{9,25},{10,... | collective-permute-start | bytes 1572872 | tf_op jit(solution)/shard_map/ppermute | solution.py:38
  227.1 20.3 %collective-permute-start.10 = (bf16[2,128,128]{2,1,0:T(8,128)(2,1)S(1)}, bf16[2,128,128]{2,1,0:T(8,128)(2,1)S(1)}, u32[]{:S(2)}, u32[]{:S(2)}) collective-permute-start(bf16[2,128,128]{2,1,0:T(8,128)(2,1)S(1)} %add_convert_fusion.1), channel_id=1, source_target_pairs={{0,4},{1,5},{2,6},{3,7},{4,0},{5,1},{6,2},{7,3},{8,12},{9,13},{10,... | collective-permute-start | bytes 196616 | tf_op jit(solution)/shard_map/ppermute | solution.py:29
  245.6 50.5 %collective-permute-start.31 = (bf16[8,128,512]{2,1,0:T(8,128)(2,1)}, bf16[8,128,512]{2,1,0:T(8,128)(2,1)}, u32[]{:S(2)}, u32[]{:S(2)}) collective-permute-start(bf16[8,128,512]{2,1,0:T(8,128)(2,1)} %shard_map.251.refs_1_), channel_id=1, source_target_pairs={{0,16},{1,17},{2,18},{3,19},{4,20},{5,21},{6,22},{7,23},{8,9},{9,8... | collective-permute-start | bytes 3145736 | tf_op jit(solution)/shard_map/ppermute | solution.py:38
  253.1 1.7 collective-permute-start.14
  253.1 8.6 %collective-permute-start.13 = (bf16[4,64,512]{2,1,0:T(8,128)(2,1)S(1)}, bf16[4,64,512]{2,1,0:T(8,128)(2,1)S(1)}, u32[]{:S(2)}, u32[]{:S(2)}) collective-permute-start(bf16[4,64,512]{2,1,0:T(8,128)(2,1)S(1)} %copy-done.38), channel_id=1, source_target_pairs={{0,1},{1,0},{2,3},{3,2},{4,5},{5,4},{6,7},{7,6},{8,24},{9,25},{10,... | collective-permute-start | bytes 786440 | tf_op jit(solution)/shard_map/ppermute | solution.py:38
  255.6 40.5 %copy-start.1 = (bf16[8,128,512]{2,1,0:T(8,128)(2,1)S(1)}, bf16[8,128,512]{2,1,0:T(8,128)(2,1)}, u32[]{:S(2)}) copy-start(bf16[8,128,512]{2,1,0:T(8,128)(2,1)} %shard_map.251.refs_1_) | copy-start | bytes 3145732
  257.4 11.5 %collective-permute-start.18 = (bf16[256,512]{1,0:T(8,128)(2,1)}, bf16[256,512]{1,0:T(8,128)(2,1)S(1)}, u32[]{:S(2)}, u32[]{:S(2)}) collective-permute-start(bf16[256,512]{1,0:T(8,128)(2,1)} %shard_map.242.refs_2_.refs_0_), channel_id=1, source_target_pairs={{0,16},{1,17},{2,18},{3,19},{4,20},{5,21},{6,22},{7,23},{8,24},{9,... | collective-permute-start | bytes 786440 | tf_op jit(solution)/shard_map/ppermute | solution.py:38
  264.2 7.6 %collective-permute-start.15 = (bf16[1,64,512]{2,1,0:T(8,128)(2,1)}, bf16[1,64,512]{2,1,0:T(8,128)(2,1)S(1)}, u32[]{:S(2)}, u32[]{:S(2)}) collective-permute-start(bf16[1,64,512]{2,1,0:T(8,128)(2,1)} %get-tuple-element.156), channel_id=1, source_target_pairs={{0,4},{1,5},{2,6},{3,7},{4,0},{5,1},{6,2},{7,3},{8,12},{9,13},{10,... | collective-permute-start | bytes 196616 | tf_op jit(solution)/shard_map/ppermute | solution.py:38
  265.5 6.3 %collective-permute-start.16 = (bf16[1,64,512]{2,1,0:T(8,128)(2,1)}, bf16[1,64,512]{2,1,0:T(8,128)(2,1)S(1)}, u32[]{:S(2)}, u32[]{:S(2)}) collective-permute-start(bf16[1,64,512]{2,1,0:T(8,128)(2,1)} %get-tuple-element.157), channel_id=1, source_target_pairs={{0,2},{1,3},{2,0},{3,1},{4,6},{5,7},{6,4},{7,5},{8,10},{9,11},{10,... | collective-permute-start | bytes 196616 | tf_op jit(solution)/shard_map/ppermute | solution.py:38
  266.6 6.4 %collective-permute-start.17 = (bf16[1,64,512]{2,1,0:T(8,128)(2,1)}, bf16[1,64,512]{2,1,0:T(8,128)(2,1)S(1)}, u32[]{:S(2)}, u32[]{:S(2)}) collective-permute-start(bf16[1,64,512]{2,1,0:T(8,128)(2,1)} %get-tuple-element.158), channel_id=1, source_target_pairs={{0,6},{1,7},{2,4},{3,5},{4,2},{5,3},{6,0},{7,1},{8,14},{9,15},{10,... | collective-permute-start | bytes 196616 | tf_op jit(solution)/shard_map/ppermute | solution.py:38
  275.2 8.1 %collective-permute-start.19 = (bf16[1,64,512]{2,1,0:T(8,128)(2,1)}, bf16[1,64,512]{2,1,0:T(8,128)(2,1)S(1)}, u32[]{:S(2)}, u32[]{:S(2)}) collective-permute-start(bf16[1,64,512]{2,1,0:T(8,128)(2,1)} %shard_map.245.refs_0_), channel_id=1, source_target_pairs={{0,4},{1,5},{2,6},{3,7},{4,0},{5,1},{6,2},{7,3},{8,12},{9,13},{10,... | collective-permute-start | bytes 196616 | tf_op jit(solution)/shard_map/ppermute | solution.py:38
  276.4 6.9 %collective-permute-start.20 = (bf16[1,64,512]{2,1,0:T(8,128)(2,1)}, bf16[1,64,512]{2,1,0:T(8,128)(2,1)S(1)}, u32[]{:S(2)}, u32[]{:S(2)}) collective-permute-start(bf16[1,64,512]{2,1,0:T(8,128)(2,1)} %shard_map.245.refs_0_), channel_id=1, source_target_pairs={{0,2},{1,3},{2,0},{3,1},{4,6},{5,7},{6,4},{7,5},{8,10},{9,11},{10,... | collective-permute-start | bytes 196616 | tf_op jit(solution)/shard_map/ppermute | solution.py:38
  277.8 6.4 %collective-permute-start.21 = (bf16[1,64,512]{2,1,0:T(8,128)(2,1)}, bf16[1,64,512]{2,1,0:T(8,128)(2,1)S(1)}, u32[]{:S(2)}, u32[]{:S(2)}) collective-permute-start(bf16[1,64,512]{2,1,0:T(8,128)(2,1)} %shard_map.245.refs_0_), channel_id=1, source_target_pairs={{0,6},{1,7},{2,4},{3,5},{4,2},{5,3},{6,0},{7,1},{8,14},{9,15},{10,... | collective-permute-start | bytes 196616 | tf_op jit(solution)/shard_map/ppermute | solution.py:38
  286.4 6.6 %collective-permute-start.22 = (bf16[4,64,512]{2,1,0:T(8,128)(2,1)}, bf16[4,64,512]{2,1,0:T(8,128)(2,1)S(1)}, u32[]{:S(2)}, u32[]{:S(2)}) collective-permute-start(bf16[4,64,512]{2,1,0:T(8,128)(2,1)} %shard_map.246.refs_0_), channel_id=1, source_target_pairs={{0,1},{1,0},{2,3},{3,2},{4,5},{5,4},{6,7},{7,6},{8,24},{9,25},{10,... | collective-permute-start | bytes 786440 | tf_op jit(solution)/shard_map/ppermute | solution.py:38
  295.6 11.8 %collective-permute-start.23 = (bf16[8,64,512]{2,1,0:T(8,128)(2,1)}, bf16[8,64,512]{2,1,0:T(8,128)(2,1)S(1)}, u32[]{:S(2)}, u32[]{:S(2)}) collective-permute-start(bf16[8,64,512]{2,1,0:T(8,128)(2,1)} %shard_map.247.refs_1_), channel_id=1, source_target_pairs={{0,16},{1,17},{2,18},{3,19},{4,20},{5,21},{6,22},{7,23},{8,9},{9,8... | collective-permute-start | bytes 1572872 | tf_op jit(solution)/shard_map/ppermute | solution.py:38
  296.0 22.4 %collective-permute-start.32 = (bf16[8,128,512]{2,1,0:T(8,128)(2,1)S(1)}, bf16[8,128,512]{2,1,0:T(8,128)(2,1)}, u32[]{:S(2)}, u32[]{:S(2)}) collective-permute-start(bf16[8,128,512]{2,1,0:T(8,128)(2,1)S(1)} %copy-done.1), channel_id=1, source_target_pairs={{0,8},{1,9},{2,10},{3,11},{4,12},{5,13},{6,14},{7,15},{8,0},{9,1},... | collective-permute-start | bytes 3145736 | tf_op jit(solution)/shard_map/ppermute | solution.py:38
  296.0 22.3 %collective-permute-start.33 = (bf16[8,128,512]{2,1,0:T(8,128)(2,1)}, bf16[8,128,512]{2,1,0:T(8,128)(2,1)}, u32[]{:S(2)}, u32[]{:S(2)}) collective-permute-start(bf16[8,128,512]{2,1,0:T(8,128)(2,1)} %collective-permute-done.31.refs_2_), channel_id=1, source_target_pairs={{0,8},{1,9},{2,10},{3,11},{4,12},{5,13},{6,14},{7,15},{8,0},{9,1},... | collective-permute-start | bytes 3145736 | tf_op jit(solution)/shard_map/ppermute | solution.py:38
  297.5 9.6 %copy-start.4 = (bf16[8,64,512]{2,1,0:T(8,128)(2,1)S(1)}, bf16[8,64,512]{2,1,0:T(8,128)(2,1)}, u32[]{:S(2)}) copy-start(bf16[8,64,512]{2,1,0:T(8,128)(2,1)} %shard_map.247.refs_1_) | copy-start | bytes 1572868
  297.5 10.1 %copy-start.3 = (bf16[256,512]{1,0:T(8,128)(2,1)S(1)}, bf16[256,512]{1,0:T(8,128)(2,1)}, u32[]{:S(2)}) copy-start(bf16[256,512]{1,0:T(8,128)(2,1)} %shard_map.244.refs_4_.refs_1_) | copy-start | bytes 786436
  303.6 21.0 %all-to-all-start.7 = ((f32[32,8,512]{2,1,0:T(8,128)}), f32[32,8,512]{2,1,0:T(8,128)S(1)}, u32[]{:S(2)}, u32[]{:S(2)}) async-start(f32[32,8,512]{2,1,0:T(8,128)} %get-tuple-element.151), calls=%async_computation.7 | async-start | bytes 1048576 | tf_op jit(solution)/shard_map/all_to_all | solution.py:1197
  307.1 5.9 %collective-permute-start.24 = (bf16[8,64,512]{2,1,0:T(8,128)(2,1)S(1)}, bf16[8,64,512]{2,1,0:T(8,128)(2,1)S(1)}, u32[]{:S(2)}, u32[]{:S(2)}) collective-permute-start(bf16[8,64,512]{2,1,0:T(8,128)(2,1)S(1)} %copy-done.4), channel_id=1, source_target_pairs={{0,8},{1,9},{2,10},{3,11},{4,12},{5,13},{6,14},{7,15},{8,0},{9,1},... | collective-permute-start | bytes 1572872 | tf_op jit(solution)/shard_map/ppermute | solution.py:38
  307.4 5.6 %collective-permute-start.25 = (bf16[8,64,512]{2,1,0:T(8,128)(2,1)S(1)}, bf16[8,64,512]{2,1,0:T(8,128)(2,1)S(1)}, u32[]{:S(2)}, u32[]{:S(2)}) collective-permute-start(bf16[8,64,512]{2,1,0:T(8,128)(2,1)S(1)} %collective-permute-done.23.refs_2_), channel_id=1, source_target_pairs={{0,8},{1,9},{2,10},{3,11},{4,12},{5,13},{6,14},{7,15},{8,0},{9,1},... | collective-permute-start | bytes 1572872 | tf_op jit(solution)/shard_map/ppermute | solution.py:38
  307.7 2.5 collective-permute-start.26
  (32 other events, 48.6 us)

commit v3 on v2

--- a/solution.py
+++ b/solution.py
@@ -64,7 +64,7 @@
     shape = arrays[0].shape
     out = like((shape[0] // pieces,) + shape[1:], dtype)
     kernel = lambda *refs: add_kernel(len(arrays), *refs)
-    return list(call(kernel, [out] * pieces, arrays, **more))
+    return list(call(kernel, [out] * pieces, arrays, HELD, out_specs=HELD, **more))
 
 
 def join_kernel(*refs):
@@ -76,7 +76,7 @@
 def join(arrays, **more):
     shape = arrays[0].shape
     out = like((len(arrays) * shape[0],) + shape[1:], BF16)
-    return list(call(join_kernel, [out], arrays, **more))
+    return list(call(join_kernel, [out], arrays, HELD, out_specs=HELD, **more))
 
 
 def sum_stages(keep, give, more):
@@ -141,6 +141,10 @@
     after=(),
     passing=(),
 ):
+    vmem = VMEM_BYTES
+    if specs is HELD:
+        specs, out_specs = [IN_VMEM] * len(args), [IN_VMEM] * len(outs)
+        vmem = 16 * 2**20
     specs = specs or [whole(a) for a in args]
     moved = sum(math.prod(o.shape) * o.dtype.itemsize for o in outs)
     moved += sum(math.prod(a.shape) * a.dtype.itemsize for a in args)
@@ -160,13 +164,15 @@
         out_specs=list(out_specs or [whole(o) for o in outs]) + [anywhere] * pas,
         scratch_shapes=list(scratch),
         input_output_aliases={count + k: made + k for k in range(pas)},
-        compiler_params=pltpu.CompilerParams(vmem_limit_bytes=VMEM_BYTES),
+        compiler_params=pltpu.CompilerParams(vmem_limit_bytes=vmem),
         cost_estimate=pl.CostEstimate(
             flops=int(flops * COST), bytes_accessed=int(moved * COST), transcendentals=0
         ),
     )(*args, *extra)
 
 
+HELD = object()
+IN_VMEM = pl.BlockSpec(memory_space=pltpu.VMEM)
 SCALAR = pl.BlockSpec(memory_space=pltpu.SMEM)
 
 

time: 331 us -> 313 us (0.946)
  Pallas kernels: 158 us -> 134 us
  waiting for transfers between devices: 47.2 us -> 60 us
  local copies, waits for them, and re-layouts: 19.5 us -> 12.2 us
    pallas_call x32, Pallas kernels: 132 us -> 108 us  [call(): pl.pallas_call(lambda *refs: kernel(*refs[:count], *refs[count + skip:cou...]
    ppermute x29, waiting for transfers between devices: 33.4 us -> 42.8 us  [send(): return lax.ppermute(array, ('dp', 'seq'), pairs)]
    unnamed x78 -> x50, local copies, waits for them, and re-layouts: 16.4 us -> 9.03 us
    ppermute x5, waiting for transfers between devices: 3.42 us -> 6.86 us  [swap(): lax.ppermute(array, axis, [(i, i ^ bit) for i in range(lax.axis_size(axis...]
  transfers between devices with their start and end apart: 41 -> 41, of which waited for: 19 -> 21; matrix products, arithmetic and copies ran while one was open for 1% -> 1% of each run, Pallas kernels for 35% -> 29%
where the time goes in v3:
time: 313 us; the launch traced here: 311 us
  Pallas kernels  134 us (43%)
  starting transfers between devices  66.8 us (21%)
  waiting for transfers between devices  60 us (19%)
  blocking collectives  30.7 us (10%)
  local copies, waits for them, and re-layouts  12.2 us (4%)
  other arithmetic  6.67 us (2%)
    pallas_call x32, Pallas kernels, call(): pl.pallas_call(lambda *refs: kernel(*refs[:count], *refs[count + skip:cou...  108 us
    ppermute x29, waiting for transfers between devices, send(): return lax.ppermute(array, ('dp', 'seq'), pairs)  42.8 us
    ppermute x29, starting transfers between devices, send(): return lax.ppermute(array, ('dp', 'seq'), pairs)  30.9 us
    all_to_all x1, blocking collectives, exchange(): return lax.all_to_all(chunks, 'seq', 0, 0, tiled=True)  30.7 us
    all_to_all x6, starting transfers between devices, exchange(): return lax.all_to_all(chunks, 'seq', 0, 0, tiled=True)  26.3 us
    pallas_call x1, Pallas kernels, feed(): pl.pallas_call(lambda *refs: feed_kernel(len(att), *refs), grid_spec=pltp...  26.2 us
    all_to_all x6, waiting for transfers between devices, exchange(): return lax.all_to_all(chunks, 'seq', 0, 0, tiled=True)  10.4 us
    unnamed x50, local copies, waits for them, and re-layouts  9.03 us
  transfers between devices with their start and end apart: 41, of which 21 were waited for; matrix products, arithmetic and copies ran while one was open for 1% of the time, Pallas kernels for 29%

profile of v3, /device:TPU:0, one launch (start us, length us, event | category | flops | bytes accessed | tf_op | source)
XLA Modules:
  0.0 311.4 jit_solution(11252323676655402194)
XLA Ops:
  3.3 4.7 %shard_map.220 = (bf16[2,512,512]{2,1,0:T(8,128)(2,1)}, bf16[8,7,16,512]{3,2,1,0:T(8,128)(2,1)}, bf16[8,4,16,512]{3,2,1,0:T(8,128)(2,1)}) custom-call(bf16[2,512,512]{2,1,0:T(8,128)(2,1)} %refs_0_.5, f32[1,512]{1,0:T(1,128)} %bitcast.23, bf16[16,512]{1,0:T(8,128)(2,1)} %select_select_fusion.refs_2_), custom_call_target="tpu_custom_call" | custom-call | bytes 10672128 | tf_op jit(solution)/shard_map/pallas_call | solution.py:155
  8.0 30.7 %all_to_all.40.refs_0_.refs_1_.refs_3_ = bf16[8,7,16,512]{3,2,1,0:T(8,128)(2,1)} all-to-all(bf16[8,7,16,512]{3,2,1,0:T(8,128)(2,1)} %get-tuple-element.89), channel_id=1, replica_groups=mesh['dp'=4,'seq'=8] {'seq'}, dimensions={0} | all-to-all | bytes 1835008 | tf_op jit(solution)/shard_map/all_to_all | solution.py:105
  38.7 3.5 %all-to-all-start.2 = ((bf16[8,4,16,512]{3,2,1,0:T(8,128)(2,1)}), bf16[8,4,16,512]{3,2,1,0:T(8,128)(2,1)S(1)}, u32[]{:S(2)}, u32[]{:S(2)}) async-start(bf16[8,4,16,512]{3,2,1,0:T(8,128)(2,1)} %get-tuple-element.97), calls=%async_computation.2 | async-start | bytes 1048576 | tf_op jit(solution)/shard_map/all_to_all | solution.py:105
  42.2 4.9 %shard_map.221 = (bf16[2,512,512]{2,1,0:T(8,128)(2,1)}, bf16[2,512,512]{2,1,0:T(8,128)(2,1)}, bf16[2,512,512]{2,1,0:T(8,128)(2,1)}, bf16[2,512,512]{2,1,0:T(8,12...) custom-call(bf16[2,512,512]{2,1,0:T(8,128)(2,1)} %get-tuple-element.90.refs_0_.refs_1_, ...), custom_call_target="tpu_custom_call" | custom-call | flops 4831838208 | bytes 26738688 | tf_op jit(solution)/shard_map/pallas_call | solution.py:155
  47.2 5.3 %shard_map.222 = (bf16[2,128,512]{2,1,0:T(8,128)(2,1)}, f32[16,2,128,128]{3,2,1,0:T(8,128)}, f32[2,128,128]{2,1,0:T(8,128)}, bf16[2,128,128]{2,1,0:T(8,128)(2,1)}, f32[8,128]{1,0:T(8,128)}, /*index=5*/f32[8,128]{1,0:T(8,128)}) custom-call(bf16[8,7,16,512]{3,2,1,0:T(8,128)(2,1)} %all_to_all.40.refs_0_.refs_1_.refs_3_, bf16[512,512]{1,0:T(8,128)(2,1)} %refs_4_.3, ...), custom_call_target="tpu_custom_call" | custom-call | bytes 12017664 | tf_op jit(solution)/shard_map/pallas_call | solution.py:155
  52.5 2.3 shard_map.223
  56.3 4.4 %all-to-all-start.1 = ((bf16[8,4,16,512]{3,2,1,0:T(8,128)(2,1)}), bf16[8,4,16,512]{3,2,1,0:T(8,128)(2,1)S(1)}, u32[]{:S(2)}, u32[]{:S(2)}) async-start(bf16[8,4,16,512]{3,2,1,0:T(8,128)(2,1)} %shard_map.223), calls=%async_computation.1 | async-start | bytes 1048576 | tf_op jit(solution)/shard_map/all_to_all | solution.py:105
  67.4 2.2 shard_map.225
  69.5 4.9 %all-to-all-done.1.refs_0_ = bf16[8,4,16,512]{3,2,1,0:T(8,128)(2,1)S(1)} async-done(((bf16[8,4,16,512]{3,2,1,0:T(8,128)(2,1)}), bf16[8,4,16,512]{3,2,1,0:T(8,128)(2,1)S(1)}, u32[]{:S(2)}, u32[]{:S(2)}) %all-to-all-start.1) | async-done | bytes 524320 | tf_op jit(solution)/shard_map/all_to_all | solution.py:105
  74.4 3.7 %all-to-all-start.3 = ((bf16[8,4,16,512]{3,2,1,0:T(8,128)(2,1)}), bf16[8,4,16,512]{3,2,1,0:T(8,128)(2,1)S(1)}, u32[]{:S(2)}, u32[]{:S(2)}) async-start(bf16[8,4,16,512]{3,2,1,0:T(8,128)(2,1)} %shard_map.225), calls=%async_computation.3 | async-start | bytes 1048576 | tf_op jit(solution)/shard_map/all_to_all | solution.py:105
  78.1 9.8 %shard_map.224 = (bf16[512,512]{1,0:T(8,128)(2,1)}, bf16[512,512]{1,0:T(8,128)(2,1)}, bf16[512,512]{1,0:T(8,128)(2,1)}, bf16[512,512]{1,0:T(8,128)(2,1)}, f32[16,64,256]{2,1,0:T(8,128)}) custom-call(bf16[8,4,16,512]{3,2,1,0:T(8,128)(2,1)} %copy-done.19, f32[2,32,512]{2,1,0:T(8,128)} %compare_convert_fusion.refs_1_.refs_2_, bf16[512,512]{1,0:T(8,128)(2,1)} %refs_1_.5, ...), custom_call_target="tpu_custom_call" | custom-call | flops 3221225472 | bytes 23986176 | tf_op jit(solution)/shard_map/pallas_call | solution.py:155
  87.9 4.0 %all-to-all-done.3.refs_0_ = bf16[8,4,16,512]{3,2,1,0:T(8,128)(2,1)S(1)} async-done(((bf16[8,4,16,512]{3,2,1,0:T(8,128)(2,1)}), bf16[8,4,16,512]{3,2,1,0:T(8,128)(2,1)S(1)}, u32[]{:S(2)}, u32[]{:S(2)}) %all-to-all-start.3) | async-done | bytes 524320 | tf_op jit(solution)/shard_map/all_to_all | solution.py:105
  92.6 9.8 %shard_map.226 = (bf16[512,512]{1,0:T(8,128)(2,1)}, bf16[512,512]{1,0:T(8,128)(2,1)}, bf16[512,512]{1,0:T(8,128)(2,1)}, bf16[512,512]{1,0:T(8,128)(2,1)}, f32[16,64,256]{2,1,0:T(8,128)}) custom-call(bf16[8,4,16,512]{3,2,1,0:T(8,128)(2,1)} %copy-done.20, f32[2,32,512]{2,1,0:T(8,128)} %compare_convert_fusion.refs_1_.refs_2_, bf16[512,512]{1,0:T(8,128)(2,1)} %refs_1_.5, ...), custom_call_target="tpu_custom_call" | custom-call | flops 3221225472 | bytes 23986176 | tf_op jit(solution)/shard_map/pallas_call | solution.py:155
  102.4 26.2 %shard_map.227 = (bf16[1024,512]{1,0:T(8,128)(2,1)}, bf16[16,128,512]{2,1,0:T(8,128)(2,1)}, bf16[16,128,512]{2,1,0:T(8,128)(2,1)}, bf16[512,512]{1,0:T(8,128)(2,...) custom-call(s32[2]{0:T(128)} %pad_add_fusion.refs_3_.refs_0_.refs_8_, ...), custom_call_target="tpu_custom_call" | custom-call | flops 38654705664 | bytes 75497472 | tf_op jit(solution)/shard_map/pallas_call | solution.py:866
  128.7 11.3 %shard_map.228 = (bf16[8,4,16,512]{3,2,1,0:T(8,128)(2,1)}, bf16[512,512]{1,0:T(8,128)(2,1)}, bf16[512,512]{1,0:T(8,128)(2,1)}, bf16[512,512]{1,0:T(8,128)(2,1)},...) custom-call(bf16[2,512,512]{2,1,0:T(8,128)(2,1)} %bitcast.31, ...), custom_call_target="tpu_custom_call" | custom-call | flops 4831838208 | bytes 31457280 | tf_op jit(solution)/shard_map/pallas_call | solution.py:155
  140.0 3.6 %all-to-all-start.4 = ((bf16[8,4,16,512]{3,2,1,0:T(8,128)(2,1)}), bf16[8,4,16,512]{3,2,1,0:T(8,128)(2,1)S(1)}, u32[]{:S(2)}, u32[]{:S(2)}) async-start(bf16[8,4,16,512]{3,2,1,0:T(8,128)(2,1)} %get-tuple-element.126), calls=%async_computation.4 | async-start | bytes 1048576 | tf_op jit(solution)/shard_map/all_to_all | solution.py:105
  143.6 2.8 shard_map.229
  148.9 10.9 %shard_map.230 = (bf16[8,4,16,512]{3,2,1,0:T(8,128)(2,1)}, bf16[512,512]{1,0:T(8,128)(2,1)}, bf16[512,512]{1,0:T(8,128)(2,1)}, bf16[512,512]{1,0:T(8,128)(2,1)},...) custom-call(bf16[2,512,512]{2,1,0:T(8,128)(2,1)} %bitcast.32, ...), custom_call_target="tpu_custom_call" | custom-call | flops 4831838208 | bytes 31457280 | tf_op jit(solution)/shard_map/pallas_call | solution.py:155
  159.8 6.0 %all-to-all-start.5 = ((bf16[8,4,16,512]{3,2,1,0:T(8,128)(2,1)}), bf16[8,4,16,512]{3,2,1,0:T(8,128)(2,1)}, u32[]{:S(2)}, u32[]{:S(2)}) async-start(bf16[8,4,16,512]{3,2,1,0:T(8,128)(2,1)} %get-tuple-element.127), calls=%async_computation.5 | async-start | bytes 1048576 | tf_op jit(solution)/shard_map/all_to_all | solution.py:105
  165.8 7.8 %shard_map.236 = (bf16[16,64,512]{2,1,0:T(8,128)(2,1)}, bf16[16,64,512]{2,1,0:T(8,128)(2,1)}) custom-call(s32[2]{0:T(128)} %pad_add_fusion.refs_3_.refs_0_.refs_8_, bf16[2,512,512]{2,1,0:T(8,128)(2,1)} %get-tuple-element.90.refs_0_.refs_1_, bf16[512,512]{1,0:T(8,128)(2,1)} %get-tuple-element.134.refs_2_, bf16[512,512]{1,0:T(8,128)(2,1)} %get-tuple-element.135.refs_3_, ...), custom_call_target="tpu_custom_call" | custom-call | flops 8053063680 | bytes 29884440 | tf_op jit(solution)/shard_map/pallas_call | solution.py:155
  175.2 2.1 collective-permute-start.4
  177.3 7.2 %collective-permute-done.4.refs_1_ = bf16[4,128,512]{2,1,0:T(8,128)(2,1)S(1)} collective-permute-done((bf16[4,128,512]{2,1,0:T(8,128)(2,1)S(1)}, bf16[4,128,512]{2,1,0:T(8,128)(2,1)S(1)}, u32[]{:S(2)}, u32[]{:S(2)}) %collective-permute-start.4) | collective-permute-done | bytes 524320 | tf_op jit(solution)/shard_map/ppermute | solution.py:38
  184.6 3.0 collective-permute-start.5
  189.1 3.5 %shard_map.234 = (bf16[8,8,16,512]{3,2,1,0:T(8,128)(2,1)}, bf16[2,128,128]{2,1,0:T(8,128)(2,1)}) custom-call(bf16[2,128,128]{2,1,0:T(8,128)(2,1)} %get-tuple-element.92.refs_0_, bf16[8,7,16,512]{3,2,1,0:T(8,128)(2,1)} %all_to_all.40.refs_0_.refs_1_.refs_3_, bf16[8,4,16,512]{3,2,1,0:T(8,128)(2,1)} %copy-done.13, bf16[8,4,16,512]{3,2,1,0:T(8,128)(2,1)} %copy-done.15, ...), custom_call_target="tpu_custom_call" | custom-call | bytes 11010048 | tf_op jit(solution)/shard_map/pallas_call | solution.py:155
  192.6 2.0 collective-permute-start.8
  195.9 1.8 collective-permute-done.7.refs_3_
  200.0 4.2 %collective-permute-start.27 = (bf16[1,128,512]{2,1,0:T(8,128)(2,1)S(1)}, bf16[1,128,512]{2,1,0:T(8,128)(2,1)S(1)}, u32[]{:S(2)}, u32[]{:S(2)}) collective-permute-start(bf16[1,128,512]{2,1,0:T(8,128)(2,1)S(1)} %get-tuple-element.163.refs_0_), channel_id=1, source_target_pairs={{0,4},{1,5},{2,6},{3,7},{4,0},{5,1},{6,2},{7,3},{8,12},{9,13},{10,... | collective-permute-start | bytes 393224 | tf_op jit(solution)/shard_map/ppermute | solution.py:38
  207.1 5.1 %all-to-all-start.6 = ((bf16[8,8,16,512]{3,2,1,0:T(8,128)(2,1)}), bf16[8,8,16,512]{3,2,1,0:T(8,128)(2,1)}, u32[]{:S(2)}, u32[]{:S(2)}) async-start(bf16[8,8,16,512]{3,2,1,0:T(8,128)(2,1)} %copy-done.2), calls=%async_computation.6 | async-start | bytes 2097152 | tf_op jit(solution)/shard_map/all_to_all | solution.py:105
  213.1 2.5 collective-permute-done.28.refs_2_
  217.2 2.1 collective-permute-start.10
  219.3 5.4 %shard_map.231.refs_10_.refs_2_ = f32[2,512,512]{2,1,0:T(8,128)} custom-call(bf16[512,512]{1,0:T(8,128)(2,1)} %refs_0_.4, bf16[512,512]{1,0:T(8,128)(2,1)} %refs_1_.5, bf16[512,512]{1,0:T(8,128)(2,1)} %refs_2_.7, bf16[512,512]{1,0:T(8,128)(2,1)} %get-tuple-element.107.refs_3_.refs_4_, bf16[512,512]{1,0:T(8,128)(2,1)} %get-tuple-element.108.refs_4_.refs_5_, ...), custom_call_target="tpu_custom_call" | custom-call | flops 4831838208 | bytes 20447232 | tf_op jit(solution)/shard_map/pallas_call | solution.py:155
  224.7 2.1 collective-permute-done.12.refs_1_
  226.9 9.2 %collective-permute-done.30.refs_1_ = bf16[4,128,512]{2,1,0:T(8,128)(2,1)S(1)} collective-permute-done((bf16[4,128,512]{2,1,0:T(8,128)(2,1)S(1)}, bf16[4,128,512]{2,1,0:T(8,128)(2,1)S(1)}, u32[]{:S(2)}, u32[]{:S(2)}) %collective-permute-start.30) | collective-permute-done | bytes 524320 | tf_op jit(solution)/shard_map/ppermute | solution.py:38
  236.8 4.8 %collective-permute-done.10 = bf16[2,128,128]{2,1,0:T(8,128)(2,1)S(1)} collective-permute-done((bf16[2,128,128]{2,1,0:T(8,128)(2,1)S(1)}, bf16[2,128,128]{2,1,0:T(8,128)(2,1)S(1)}, u32[]{:S(2)}, u32[]{:S(2)}) %collective-permute-start.10) | collective-permute-done | bytes 65568 | tf_op jit(solution)/shard_map/ppermute | solution.py:29
  242.3 5.0 %shard_map.239 = (f32[2,16,512]{2,1,0:T(8,128)}, bf16[256,512]{1,0:T(8,128)(2,1)}, bf16[256,512]{1,0:T(8,128)(2,1)}) custom-call(f32[8,128]{1,0:T(8,128)} %add.65.refs_5_.refs_0_.refs_1_, s32[1,1]{1,0:T(1,128)} %bitcast.11.refs_1_, bf16[2,128,128]{2,1,0:T(8,128)(2,1)} %add_convert_fusion.refs_2_, bf16[8,7,16,512]{3,2,1,0:T(8,128)(2,1)} %all_to_all.40.refs_0_.refs_1_.refs_3_, ...), custom_call_target="tpu_custom_call" | custom-call | bytes 13774884 | tf_op jit(solution)/shard_map/pallas_call | solution.py:155
  250.6 3.0 collective-permute-done.13.refs_1_
  254.8 1.8 collective-permute-start.16
  256.5 2.6 collective-permute-start.17
  261.0 2.0 collective-permute-done.17.refs_3_
  267.5 3.2 %collective-permute-done.19.refs_1_ = bf16[1,64,512]{2,1,0:T(8,128)(2,1)S(1)} collective-permute-done((bf16[1,64,512]{2,1,0:T(8,128)(2,1)S(1)}, bf16[1,64,512]{2,1,0:T(8,128)(2,1)S(1)}, u32[]{:S(2)}, u32[]{:S(2)}) %collective-permute-start.19) | collective-permute-done | bytes 65568 | tf_op jit(solution)/shard_map/ppermute | solution.py:38
  273.5 5.0 %collective-permute-done.22.refs_1_ = bf16[4,64,512]{2,1,0:T(8,128)(2,1)S(1)} collective-permute-done((bf16[4,64,512]{2,1,0:T(8,128)(2,1)S(1)}, bf16[4,64,512]{2,1,0:T(8,128)(2,1)S(1)}, u32[]{:S(2)}, u32[]{:S(2)}) %collective-permute-start.22) | collective-permute-done | bytes 262176 | tf_op jit(solution)/shard_map/ppermute | solution.py:38
  279.7 6.0 %shard_map.240 = (bf16[2,512,512]{2,1,0:T(8,128)(2,1)}, f32[32,8,512]{2,1,0:T(8,128)}) custom-call(bf16[2,512,512]{2,1,0:T(8,128)(2,1)} %refs_0_.5, f32[1,512]{1,0:T(1,128)} %bitcast.24, f32[2,512,512]{2,1,0:T(8,128)} %shard_map.231.refs_10_.refs_2_, bf16[8,8,16,512]{3,2,1,0:T(8,128)(2,1)} %all-to-all-done.6.refs_3_, ...), custom_call_target="tpu_custom_call" | custom-call | bytes 20711424 | tf_op jit(solution)/shard_map/pallas_call | solution.py:155
  285.7 3.5 %all-to-all-start.7 = ((f32[32,8,512]{2,1,0:T(8,128)}), f32[32,8,512]{2,1,0:T(8,128)S(1)}, u32[]{:S(2)}, u32[]{:S(2)}) async-start(f32[32,8,512]{2,1,0:T(8,128)} %get-tuple-element.151), calls=%async_computation.7 | async-start | bytes 1048576 | tf_op jit(solution)/shard_map/all_to_all | solution.py:1203
  290.1 1.9 collective-permute-done.26.refs_2_
  292.7 2.1 shard_map.249
  296.4 3.8 %shard_map.248 = (f32[512,512]{1,0:T(8,128)}, f32[512,512]{1,0:T(8,128)}, f32[512,512]{1,0:T(8,128)}, f32[512,512]{1,0:T(8,128)}) custom-call(s32[2]{0:T(128)} %pad_add_fusion.refs_3_.refs_0_.refs_8_, bf16[8,64,512]{2,1,0:T(8,128)(2,1)} %copy-done.6, bf16[8,64,512]{2,1,0:T(8,128)(2,1)} %collective-permute-done.23.refs_2_, bf16[8,64,512]{2,1,0:T(8,128)(2,1)} %copy-done.17, ...), custom_call_target="tpu_custom_call" | custom-call | bytes 18874392 | tf_op jit(solution)/shard_map/pallas_call | solution.py:155
  300.2 6.2 %shard_map.252 = (f32[2048,512]{1,0:T(8,128)}, f32[512,2048]{1,0:T(8,128)}) custom-call(s32[2]{0:T(128)} %pad_add_fusion.refs_3_.refs_0_.refs_8_, bf16[8,128,512]{2,1,0:T(8,128)(2,1)} %copy-done, bf16[8,128,512]{2,1,0:T(8,128)(2,1)} %copy-done.16, bf16[8,128,512]{2,1,0:T(8,128)(2,1)} %collective-permute-done.32.refs_3_, ...), custom_call_target="tpu_custom_call" | custom-call | bytes 37748760 | tf_op jit(solution)/shard_map/pallas_call | solution.py:155
  307.1 1.7 shard_map.241
  (137 shorter events, 49.1 us)
Async XLA Ops:
  38.7 17.6 %all-to-all-start.2 = ((bf16[8,4,16,512]{3,2,1,0:T(8,128)(2,1)}), bf16[8,4,16,512]{3,2,1,0:T(8,128)(2,1)S(1)}, u32[]{:S(2)}, u32[]{:S(2)}) async-start(bf16[8,4,16,512]{3,2,1,0:T(8,128)(2,1)} %get-tuple-element.97), calls=%async_computation.2 | async-start | bytes 1048576 | tf_op jit(solution)/shard_map/all_to_all | solution.py:105
  56.3 18.1 %all-to-all-start.1 = ((bf16[8,4,16,512]{3,2,1,0:T(8,128)(2,1)}), bf16[8,4,16,512]{3,2,1,0:T(8,128)(2,1)S(1)}, u32[]{:S(2)}, u32[]{:S(2)}) async-start(bf16[8,4,16,512]{3,2,1,0:T(8,128)(2,1)} %shard_map.223), calls=%async_computation.1 | async-start | bytes 1048576 | tf_op jit(solution)/shard_map/all_to_all | solution.py:105
  62.0 1.2 collective-permute-start
  63.2 3.6 %collective-permute-start.1 = (f32[8,128]{1,0:T(8,128)S(1)}, f32[8,128]{1,0:T(8,128)S(1)}, u32[]{:S(2)}, u32[]{:S(2)}) collective-permute-start(f32[8,128]{1,0:T(8,128)S(1)} %add.64), channel_id=1, source_target_pairs={{0,16},{8,24},{16,0},{24,8},{1,17},{9,25},{17,1},{25,9},{2,18},{10... | collective-permute-start | bytes 12296 | tf_op jit(solution)/shard_map/ppermute | solution.py:29
  74.4 17.4 %all-to-all-start.3 = ((bf16[8,4,16,512]{3,2,1,0:T(8,128)(2,1)}), bf16[8,4,16,512]{3,2,1,0:T(8,128)(2,1)S(1)}, u32[]{:S(2)}, u32[]{:S(2)}) async-start(bf16[8,4,16,512]{3,2,1,0:T(8,128)(2,1)} %shard_map.225), calls=%async_computation.3 | async-start | bytes 1048576 | tf_op jit(solution)/shard_map/all_to_all | solution.py:105
  128.6 15.0 %collective-permute-start.2 = (bf16[16,128,512]{2,1,0:T(8,128)(2,1)}, bf16[16,128,512]{2,1,0:T(8,128)(2,1)}, u32[]{:S(2)}, u32[]{:S(2)}) collective-permute-start(bf16[16,128,512]{2,1,0:T(8,128)(2,1)} %get-tuple-element.114), channel_id=1, source_target_pairs={{0,8},{1,9},{2,10},{3,11},{4,12},{5,13},{6,14},{7,15},{8,0},{9,1},... | collective-permute-start | bytes 6291464 | tf_op jit(solution)/shard_map/ppermute | solution.py:38
  128.7 14.9 %copy-start.7 = (bf16[16,128,512]{2,1,0:T(8,128)(2,1)S(1)}, bf16[16,128,512]{2,1,0:T(8,128)(2,1)}, u32[]{:S(2)}) copy-start(bf16[16,128,512]{2,1,0:T(8,128)(2,1)} %get-tuple-element.113.refs_0_) | copy-start | bytes 6291460
  140.0 19.8 %all-to-all-start.4 = ((bf16[8,4,16,512]{3,2,1,0:T(8,128)(2,1)}), bf16[8,4,16,512]{3,2,1,0:T(8,128)(2,1)S(1)}, u32[]{:S(2)}, u32[]{:S(2)}) async-start(bf16[8,4,16,512]{3,2,1,0:T(8,128)(2,1)} %get-tuple-element.126), calls=%async_computation.4 | async-start | bytes 1048576 | tf_op jit(solution)/shard_map/all_to_all | solution.py:105
  147.4 26.3 %collective-permute-start.3 = (bf16[8,128,512]{2,1,0:T(8,128)(2,1)}, bf16[8,128,512]{2,1,0:T(8,128)(2,1)}, u32[]{:S(2)}, u32[]{:S(2)}) collective-permute-start(bf16[8,128,512]{2,1,0:T(8,128)(2,1)} %get-tuple-element.119), channel_id=1, source_target_pairs={{0,16},{1,17},{2,18},{3,19},{4,20},{5,21},{6,22},{7,23},{8,9},{9,8... | collective-permute-start | bytes 3145736 | tf_op jit(solution)/shard_map/ppermute | solution.py:38
  159.8 13.8 %copy-start.15 = (bf16[8,4,16,512]{3,2,1,0:T(8,128)(2,1)}, bf16[8,4,16,512]{3,2,1,0:T(8,128)(2,1)S(1)}, u32[]{:S(2)}) copy-start(bf16[8,4,16,512]{3,2,1,0:T(8,128)(2,1)S(1)} %all-to-all-done.4.refs_3_) | copy-start | bytes 1572868
  159.8 29.3 %all-to-all-start.5 = ((bf16[8,4,16,512]{3,2,1,0:T(8,128)(2,1)}), bf16[8,4,16,512]{3,2,1,0:T(8,128)(2,1)}, u32[]{:S(2)}, u32[]{:S(2)}) async-start(bf16[8,4,16,512]{3,2,1,0:T(8,128)(2,1)} %get-tuple-element.127), calls=%async_computation.5 | async-start | bytes 1048576 | tf_op jit(solution)/shard_map/all_to_all | solution.py:105
  173.6 38.6 %collective-permute-start.11 = (bf16[16,64,512]{2,1,0:T(8,128)(2,1)}, bf16[16,64,512]{2,1,0:T(8,128)(2,1)S(1)}, u32[]{:S(2)}, u32[]{:S(2)}) collective-permute-start(bf16[16,64,512]{2,1,0:T(8,128)(2,1)} %get-tuple-element.142), channel_id=1, source_target_pairs={{0,8},{1,9},{2,10},{3,11},{4,12},{5,13},{6,14},{7,15},{8,0},{9,1},... | collective-permute-start | bytes 3145736 | tf_op jit(solution)/shard_map/ppermute | solution.py:38
  175.2 13.9 %copy-start.8 = (bf16[4,128,512]{2,1,0:T(8,128)(2,1)}, bf16[4,128,512]{2,1,0:T(8,128)(2,1)S(1)}, u32[]{:S(2)}) copy-start(bf16[4,128,512]{2,1,0:T(8,128)(2,1)S(1)} %get-tuple-element.120.refs_0_.refs_5_) | copy-start | bytes 1572868
  175.2 9.2 %collective-permute-start.4 = (bf16[4,128,512]{2,1,0:T(8,128)(2,1)S(1)}, bf16[4,128,512]{2,1,0:T(8,128)(2,1)S(1)}, u32[]{:S(2)}, u32[]{:S(2)}) collective-permute-start(bf16[4,128,512]{2,1,0:T(8,128)(2,1)S(1)} %get-tuple-element.121), channel_id=1, source_target_pairs={{0,1},{1,0},{2,3},{3,2},{4,5},{5,4},{6,7},{7,6},{8,24},{9,25},{10,... | collective-permute-start | bytes 1572872 | tf_op jit(solution)/shard_map/ppermute | solution.py:38
  184.6 11.3 %collective-permute-start.5 = (bf16[1,128,512]{2,1,0:T(8,128)(2,1)S(1)}, bf16[1,128,512]{2,1,0:T(8,128)(2,1)S(1)}, u32[]{:S(2)}, u32[]{:S(2)}) collective-permute-start(bf16[1,128,512]{2,1,0:T(8,128)(2,1)S(1)} %get-tuple-element.123), channel_id=1, source_target_pairs={{0,4},{1,5},{2,6},{3,7},{4,0},{5,1},{6,2},{7,3},{8,12},{9,13},{10,... | collective-permute-start | bytes 393224 | tf_op jit(solution)/shard_map/ppermute | solution.py:38
  187.5 8.4 %collective-permute-start.6 = (bf16[1,128,512]{2,1,0:T(8,128)(2,1)S(1)}, bf16[1,128,512]{2,1,0:T(8,128)(2,1)S(1)}, u32[]{:S(2)}, u32[]{:S(2)}) collective-permute-start(bf16[1,128,512]{2,1,0:T(8,128)(2,1)S(1)} %get-tuple-element.124), channel_id=1, source_target_pairs={{0,2},{1,3},{2,0},{3,1},{4,6},{5,7},{6,4},{7,5},{8,10},{9,11},{10,... | collective-permute-start | bytes 393224 | tf_op jit(solution)/shard_map/ppermute | solution.py:38
  189.0 8.7 %collective-permute-start.7 = (bf16[1,128,512]{2,1,0:T(8,128)(2,1)S(1)}, bf16[1,128,512]{2,1,0:T(8,128)(2,1)S(1)}, u32[]{:S(2)}, u32[]{:S(2)}) collective-permute-start(bf16[1,128,512]{2,1,0:T(8,128)(2,1)S(1)} %get-tuple-element.125), channel_id=1, source_target_pairs={{0,6},{1,7},{2,4},{3,5},{4,2},{5,3},{6,0},{7,1},{8,14},{9,15},{10,... | collective-permute-start | bytes 393224 | tf_op jit(solution)/shard_map/ppermute | solution.py:38
  189.1 23.1 %copy-start.9 = (bf16[16,64,512]{2,1,0:T(8,128)(2,1)S(1)}, bf16[16,64,512]{2,1,0:T(8,128)(2,1)}, u32[]{:S(2)}) copy-start(bf16[16,64,512]{2,1,0:T(8,128)(2,1)} %get-tuple-element.141.refs_0_) | copy-start | bytes 3145732
  192.6 13.1 %collective-permute-start.8 = (bf16[2,128,128]{2,1,0:T(8,128)(2,1)}, bf16[2,128,128]{2,1,0:T(8,128)(2,1)S(1)}, u32[]{:S(2)}, u32[]{:S(2)}) collective-permute-start(bf16[2,128,128]{2,1,0:T(8,128)(2,1)} %get-tuple-element.130), channel_id=1, source_target_pairs={{0,1},{1,0},{2,3},{3,2},{4,5},{5,4},{6,7},{7,6},{8,9},{9,8},{10,11... | collective-permute-start | bytes 196616 | tf_op jit(solution)/shard_map/ppermute | solution.py:29
  200.0 13.1 %collective-permute-start.27 = (bf16[1,128,512]{2,1,0:T(8,128)(2,1)S(1)}, bf16[1,128,512]{2,1,0:T(8,128)(2,1)S(1)}, u32[]{:S(2)}, u32[]{:S(2)}) collective-permute-start(bf16[1,128,512]{2,1,0:T(8,128)(2,1)S(1)} %get-tuple-element.163.refs_0_), channel_id=1, source_target_pairs={{0,4},{1,5},{2,6},{3,7},{4,0},{5,1},{6,2},{7,3},{8,12},{9,13},{10,... | collective-permute-start | bytes 393224 | tf_op jit(solution)/shard_map/ppermute | solution.py:38
  204.2 11.5 %collective-permute-start.28 = (bf16[1,128,512]{2,1,0:T(8,128)(2,1)S(1)}, bf16[1,128,512]{2,1,0:T(8,128)(2,1)S(1)}, u32[]{:S(2)}, u32[]{:S(2)}) collective-permute-start(bf16[1,128,512]{2,1,0:T(8,128)(2,1)S(1)} %get-tuple-element.163.refs_0_), channel_id=1, source_target_pairs={{0,2},{1,3},{2,0},{3,1},{4,6},{5,7},{6,4},{7,5},{8,10},{9,11},{10,... | collective-permute-start | bytes 393224 | tf_op jit(solution)/shard_map/ppermute | solution.py:38
  204.2 11.5 %collective-permute-start.29 = (bf16[1,128,512]{2,1,0:T(8,128)(2,1)S(1)}, bf16[1,128,512]{2,1,0:T(8,128)(2,1)S(1)}, u32[]{:S(2)}, u32[]{:S(2)}) collective-permute-start(bf16[1,128,512]{2,1,0:T(8,128)(2,1)S(1)} %get-tuple-element.163.refs_0_), channel_id=1, source_target_pairs={{0,6},{1,7},{2,4},{3,5},{4,2},{5,3},{6,0},{7,1},{8,14},{9,15},{10,... | collective-permute-start | bytes 393224 | tf_op jit(solution)/shard_map/ppermute | solution.py:38
  206.5 10.7 %collective-permute-start.9 = (bf16[2,128,128]{2,1,0:T(8,128)(2,1)S(1)}, bf16[2,128,128]{2,1,0:T(8,128)(2,1)S(1)}, u32[]{:S(2)}, u32[]{:S(2)}) collective-permute-start(bf16[2,128,128]{2,1,0:T(8,128)(2,1)S(1)} %add_convert_fusion.2), channel_id=1, source_target_pairs={{0,2},{1,3},{2,0},{3,1},{4,6},{5,7},{6,4},{7,5},{8,10},{9,11},{10,... | collective-permute-start | bytes 196616 | tf_op jit(solution)/shard_map/ppermute | solution.py:29
  207.1 72.6 %all-to-all-start.6 = ((bf16[8,8,16,512]{3,2,1,0:T(8,128)(2,1)}), bf16[8,8,16,512]{3,2,1,0:T(8,128)(2,1)}, u32[]{:S(2)}, u32[]{:S(2)}) async-start(bf16[8,8,16,512]{3,2,1,0:T(8,128)(2,1)} %copy-done.2), calls=%async_computation.6 | async-start | bytes 2097152 | tf_op jit(solution)/shard_map/all_to_all | solution.py:105
  212.5 14.3 %collective-permute-start.12 = (bf16[8,64,512]{2,1,0:T(8,128)(2,1)S(1)}, bf16[8,64,512]{2,1,0:T(8,128)(2,1)S(1)}, u32[]{:S(2)}, u32[]{:S(2)}) collective-permute-start(bf16[8,64,512]{2,1,0:T(8,128)(2,1)S(1)} %get-tuple-element.144), channel_id=1, source_target_pairs={{0,16},{1,17},{2,18},{3,19},{4,20},{5,21},{6,22},{7,23},{8,9},{9,8... | collective-permute-start | bytes 1572872 | tf_op jit(solution)/shard_map/ppermute | solution.py:38
  215.7 20.4 %collective-permute-start.30 = (bf16[4,128,512]{2,1,0:T(8,128)(2,1)S(1)}, bf16[4,128,512]{2,1,0:T(8,128)(2,1)S(1)}, u32[]{:S(2)}, u32[]{:S(2)}) collective-permute-start(bf16[4,128,512]{2,1,0:T(8,128)(2,1)S(1)} %shard_map.250.refs_0_), channel_id=1, source_target_pairs={{0,1},{1,0},{2,3},{3,2},{4,5},{5,4},{6,7},{7,6},{8,24},{9,25},{10,... | collective-permute-start | bytes 1572872 | tf_op jit(solution)/shard_map/ppermute | solution.py:38
  217.2 24.4 %collective-permute-start.10 = (bf16[2,128,128]{2,1,0:T(8,128)(2,1)S(1)}, bf16[2,128,128]{2,1,0:T(8,128)(2,1)S(1)}, u32[]{:S(2)}, u32[]{:S(2)}) collective-permute-start(bf16[2,128,128]{2,1,0:T(8,128)(2,1)S(1)} %add_convert_fusion.1), channel_id=1, source_target_pairs={{0,4},{1,5},{2,6},{3,7},{4,0},{5,1},{6,2},{7,3},{8,12},{9,13},{10,... | collective-permute-start | bytes 196616 | tf_op jit(solution)/shard_map/ppermute | solution.py:29
  226.9 15.4 %copy-start.3 = (bf16[4,64,512]{2,1,0:T(8,128)(2,1)}, bf16[4,64,512]{2,1,0:T(8,128)(2,1)S(1)}, u32[]{:S(2)}) copy-start(bf16[4,64,512]{2,1,0:T(8,128)(2,1)S(1)} %get-tuple-element.145.refs_9_.refs_0_.refs_2_) | copy-start | bytes 786436
  236.2 43.0 %copy-start = (bf16[8,128,512]{2,1,0:T(8,128)(2,1)}, bf16[8,128,512]{2,1,0:T(8,128)(2,1)S(1)}, u32[]{:S(2)}) copy-start(bf16[8,128,512]{2,1,0:T(8,128)(2,1)S(1)} %shard_map.251.refs_1_) | copy-start | bytes 3145732
  236.2 43.0 %collective-permute-start.31 = (bf16[8,128,512]{2,1,0:T(8,128)(2,1)S(1)}, bf16[8,128,512]{2,1,0:T(8,128)(2,1)S(1)}, u32[]{:S(2)}, u32[]{:S(2)}) collective-permute-start(bf16[8,128,512]{2,1,0:T(8,128)(2,1)S(1)} %shard_map.251.refs_1_), channel_id=1, source_target_pairs={{0,16},{1,17},{2,18},{3,19},{4,20},{5,21},{6,22},{7,23},{8,9},{9,8... | collective-permute-start | bytes 3145736 | tf_op jit(solution)/shard_map/ppermute | solution.py:38
  247.3 1.7 collective-permute-start.14
  247.3 6.4 %collective-permute-start.13 = (bf16[4,64,512]{2,1,0:T(8,128)(2,1)S(1)}, bf16[4,64,512]{2,1,0:T(8,128)(2,1)S(1)}, u32[]{:S(2)}, u32[]{:S(2)}) collective-permute-start(bf16[4,64,512]{2,1,0:T(8,128)(2,1)S(1)} %get-tuple-element.152), channel_id=1, source_target_pairs={{0,1},{1,0},{2,3},{3,2},{4,5},{5,4},{6,7},{7,6},{8,24},{9,25},{10,... | collective-permute-start | bytes 786440 | tf_op jit(solution)/shard_map/ppermute | solution.py:38
  250.0 9.3 %collective-permute-start.18 = (bf16[256,512]{1,0:T(8,128)(2,1)S(1)}, bf16[256,512]{1,0:T(8,128)(2,1)S(1)}, u32[]{:S(2)}, u32[]{:S(2)}) collective-permute-start(bf16[256,512]{1,0:T(8,128)(2,1)S(1)} %shard_map.242.refs_2_.refs_0_), channel_id=1, source_target_pairs={{0,16},{1,17},{2,18},{3,19},{4,20},{5,21},{6,22},{7,23},{8,24},{9,... | collective-permute-start | bytes 786440 | tf_op jit(solution)/shard_map/ppermute | solution.py:38
  254.6 6.4 %collective-permute-start.15 = (bf16[1,64,512]{2,1,0:T(8,128)(2,1)S(1)}, bf16[1,64,512]{2,1,0:T(8,128)(2,1)S(1)}, u32[]{:S(2)}, u32[]{:S(2)}) collective-permute-start(bf16[1,64,512]{2,1,0:T(8,128)(2,1)S(1)} %get-tuple-element.156), channel_id=1, source_target_pairs={{0,4},{1,5},{2,6},{3,7},{4,0},{5,1},{6,2},{7,3},{8,12},{9,13},{10,... | collective-permute-start | bytes 196616 | tf_op jit(solution)/shard_map/ppermute | solution.py:38
  254.8 6.3 %collective-permute-start.16 = (bf16[1,64,512]{2,1,0:T(8,128)(2,1)S(1)}, bf16[1,64,512]{2,1,0:T(8,128)(2,1)S(1)}, u32[]{:S(2)}, u32[]{:S(2)}) collective-permute-start(bf16[1,64,512]{2,1,0:T(8,128)(2,1)S(1)} %get-tuple-element.157), channel_id=1, source_target_pairs={{0,2},{1,3},{2,0},{3,1},{4,6},{5,7},{6,4},{7,5},{8,10},{9,11},{10,... | collective-permute-start | bytes 196616 | tf_op jit(solution)/shard_map/ppermute | solution.py:38
  256.5 6.5 %collective-permute-start.17 = (bf16[1,64,512]{2,1,0:T(8,128)(2,1)S(1)}, bf16[1,64,512]{2,1,0:T(8,128)(2,1)S(1)}, u32[]{:S(2)}, u32[]{:S(2)}) collective-permute-start(bf16[1,64,512]{2,1,0:T(8,128)(2,1)S(1)} %get-tuple-element.158), channel_id=1, source_target_pairs={{0,6},{1,7},{2,4},{3,5},{4,2},{5,3},{6,0},{7,1},{8,14},{9,15},{10,... | collective-permute-start | bytes 196616 | tf_op jit(solution)/shard_map/ppermute | solution.py:38
  259.4 30.4 %copy-start.5 = (bf16[256,512]{1,0:T(8,128)(2,1)}, bf16[256,512]{1,0:T(8,128)(2,1)S(1)}, u32[]{:S(2)}) copy-start(bf16[256,512]{1,0:T(8,128)(2,1)S(1)} %shard_map.244.refs_4_.refs_1_) | copy-start | bytes 786436
  263.1 7.6 %collective-permute-start.19 = (bf16[1,64,512]{2,1,0:T(8,128)(2,1)S(1)}, bf16[1,64,512]{2,1,0:T(8,128)(2,1)S(1)}, u32[]{:S(2)}, u32[]{:S(2)}) collective-permute-start(bf16[1,64,512]{2,1,0:T(8,128)(2,1)S(1)} %shard_map.245.refs_0_), channel_id=1, source_target_pairs={{0,4},{1,5},{2,6},{3,7},{4,0},{5,1},{6,2},{7,3},{8,12},{9,13},{10,... | collective-permute-start | bytes 196616 | tf_op jit(solution)/shard_map/ppermute | solution.py:38
  264.6 6.1 %collective-permute-start.20 = (bf16[1,64,512]{2,1,0:T(8,128)(2,1)S(1)}, bf16[1,64,512]{2,1,0:T(8,128)(2,1)S(1)}, u32[]{:S(2)}, u32[]{:S(2)}) collective-permute-start(bf16[1,64,512]{2,1,0:T(8,128)(2,1)S(1)} %shard_map.245.refs_0_), channel_id=1, source_target_pairs={{0,2},{1,3},{2,0},{3,1},{4,6},{5,7},{6,4},{7,5},{8,10},{9,11},{10,... | collective-permute-start | bytes 196616 | tf_op jit(solution)/shard_map/ppermute | solution.py:38
  265.9 6.2 %collective-permute-start.21 = (bf16[1,64,512]{2,1,0:T(8,128)(2,1)S(1)}, bf16[1,64,512]{2,1,0:T(8,128)(2,1)S(1)}, u32[]{:S(2)}, u32[]{:S(2)}) collective-permute-start(bf16[1,64,512]{2,1,0:T(8,128)(2,1)S(1)} %shard_map.245.refs_0_), channel_id=1, source_target_pairs={{0,6},{1,7},{2,4},{3,5},{4,2},{5,3},{6,0},{7,1},{8,14},{9,15},{10,... | collective-permute-start | bytes 196616 | tf_op jit(solution)/shard_map/ppermute | solution.py:38
  272.1 6.4 %collective-permute-start.22 = (bf16[4,64,512]{2,1,0:T(8,128)(2,1)S(1)}, bf16[4,64,512]{2,1,0:T(8,128)(2,1)S(1)}, u32[]{:S(2)}, u32[]{:S(2)}) collective-permute-start(bf16[4,64,512]{2,1,0:T(8,128)(2,1)S(1)} %shard_map.246.refs_0_), channel_id=1, source_target_pairs={{0,1},{1,0},{2,3},{3,2},{4,5},{5,4},{6,7},{7,6},{8,24},{9,25},{10,... | collective-permute-start | bytes 786440 | tf_op jit(solution)/shard_map/ppermute | solution.py:38
  278.6 11.0 %collective-permute-start.23 = (bf16[8,64,512]{2,1,0:T(8,128)(2,1)S(1)}, bf16[8,64,512]{2,1,0:T(8,128)(2,1)}, u32[]{:S(2)}, u32[]{:S(2)}) collective-permute-start(bf16[8,64,512]{2,1,0:T(8,128)(2,1)S(1)} %shard_map.247.refs_1_), channel_id=1, source_target_pairs={{0,16},{1,17},{2,18},{3,19},{4,20},{5,21},{6,22},{7,23},{8,9},{9,8... | collective-permute-start | bytes 1572872 | tf_op jit(solution)/shard_map/ppermute | solution.py:38
  279.2 21.0 %collective-permute-start.32 = (bf16[8,128,512]{2,1,0:T(8,128)(2,1)S(1)}, bf16[8,128,512]{2,1,0:T(8,128)(2,1)}, u32[]{:S(2)}, u32[]{:S(2)}) collective-permute-start(bf16[8,128,512]{2,1,0:T(8,128)(2,1)S(1)} %shard_map.251.refs_1_), channel_id=1, source_target_pairs={{0,8},{1,9},{2,10},{3,11},{4,12},{5,13},{6,14},{7,15},{8,0},{9,1},... | collective-permute-start | bytes 3145736 | tf_op jit(solution)/shard_map/ppermute | solution.py:38
  279.2 21.0 %collective-permute-start.33 = (bf16[8,128,512]{2,1,0:T(8,128)(2,1)S(1)}, bf16[8,128,512]{2,1,0:T(8,128)(2,1)}, u32[]{:S(2)}, u32[]{:S(2)}) collective-permute-start(bf16[8,128,512]{2,1,0:T(8,128)(2,1)S(1)} %collective-permute-done.31.refs_2_), channel_id=1, source_target_pairs={{0,8},{1,9},{2,10},{3,11},{4,12},{5,13},{6,14},{7,15},{8,0},{9,1},... | collective-permute-start | bytes 3145736 | tf_op jit(solution)/shard_map/ppermute | solution.py:38
  285.7 20.6 %all-to-all-start.7 = ((f32[32,8,512]{2,1,0:T(8,128)}), f32[32,8,512]{2,1,0:T(8,128)S(1)}, u32[]{:S(2)}, u32[]{:S(2)}) async-start(f32[32,8,512]{2,1,0:T(8,128)} %get-tuple-element.151), calls=%async_computation.7 | async-start | bytes 1048576 | tf_op jit(solution)/shard_map/all_to_all | solution.py:1203
  289.2 5.5 %collective-permute-start.24 = (bf16[8,64,512]{2,1,0:T(8,128)(2,1)S(1)}, bf16[8,64,512]{2,1,0:T(8,128)(2,1)S(1)}, u32[]{:S(2)}, u32[]{:S(2)}) collective-permute-start(bf16[8,64,512]{2,1,0:T(8,128)(2,1)S(1)} %shard_map.247.refs_1_), channel_id=1, source_target_pairs={{0,8},{1,9},{2,10},{3,11},{4,12},{5,13},{6,14},{7,15},{8,0},{9,1},... | collective-permute-start | bytes 1572872 | tf_op jit(solution)/shard_map/ppermute | solution.py:38
  289.6 5.2 %collective-permute-start.25 = (bf16[8,64,512]{2,1,0:T(8,128)(2,1)}, bf16[8,64,512]{2,1,0:T(8,128)(2,1)S(1)}, u32[]{:S(2)}, u32[]{:S(2)}) collective-permute-start(bf16[8,64,512]{2,1,0:T(8,128)(2,1)} %collective-permute-done.23.refs_2_), channel_id=1, source_target_pairs={{0,8},{1,9},{2,10},{3,11},{4,12},{5,13},{6,14},{7,15},{8,0},{9,1},... | collective-permute-start | bytes 1572872 | tf_op jit(solution)/shard_map/ppermute | solution.py:38
  289.8 2.1 collective-permute-start.26
  (18 other events, 84.7 us)
